TPU v7x, 256 devices: a whole 4x4x8 slice. The times are simulated.
256 devices in a mesh: ctx: 16 (over z_hi, y, core), head: 16 (over z_lo, x).
Axes of the slice: x: 4, y: 4, z: 8 (z_hi: 2, z_lo: 4; z = z_hi * 4 + z_lo), core: 2. Of those that a mesh axis runs over, the one named last changes fastest.
Arguments:
- queries: bfloat16 [32768, 2048], P(('ctx', 'head')), may hold values from -10 to 10
- keys: bfloat16 [32768, 2048], P(('ctx', 'head')), may hold values from -10 to 10
- values: bfloat16 [32768, 2048], P(('ctx', 'head')), may hold values from -6 to 6
- out_grad: bfloat16 [32768, 2048], P(('ctx', 'head')), may hold values from -6 to 6
- key_lists: int32 [256, 4], replicated, may hold values from 0 to 255, as said below
Outputs:
- attended: bfloat16 [32768, 2048], P(('ctx', 'head'))
- query_grad: bfloat16 [32768, 2048], P(('ctx', 'head'))
- key_grad: bfloat16 [32768, 2048], P(('ctx', 'head'))
- value_grad: bfloat16 [32768, 2048], P(('ctx', 'head'))
Inputs may be any that keep to these rules, and one draw needn't show every extreme that they name: `key_lists`: row n lists block n in slot 0 and block (n - 1) mod 256 in slot 1; slots 2 and 3 name blocks of slabs other than n's own slab of 16 blocks. Over the 32 entries in slots 2 and 3 of one slab's rows, each other slab is named floor or ceil of 2 * 16 / 15 times, some slab exactly 3 times.
All inputs are finite; a program needn't handle non-finite values.
Results may differ from a plain program's by a relative error of at most 0.029.
Values may be sent and summed in bfloat16 or wider, within the bound.
No kernel may reach another device: no remote copies, remote signals or barrier semaphores. Data moves between devices by JAX's collectives and lax.ppermute only.
A program may use at most 128 MiB of HBM per device.

v0:
```python
import functools

import jax
import jax.numpy as jnp
from jax import lax
from jax.experimental import pallas as pl
from jax.experimental.pallas import tpu as pltpu
from jax.sharding import PartitionSpec as P

HEAD_DIM = 128
BLOCK = 128
ANY = pl.BlockSpec(memory_space=pl.ANY)
VMEM = pl.BlockSpec(memory_space=pltpu.VMEM)
SMEM = pl.BlockSpec(memory_space=pltpu.SMEM)
FULL = 60 * 1024 * 1024


def call(kernel, out_shape, ins, outs, name, flops, nbytes, scratch=(), limit=52 * 1024 * 1024):
    return pl.pallas_call(
        kernel,
        out_shape=out_shape,
        in_specs=list(ins),
        out_specs=outs,
        scratch_shapes=list(scratch),
        compiler_params=pltpu.CompilerParams(vmem_limit_bytes=limit),
        cost_estimate=pl.CostEstimate(flops=flops, bytes_accessed=nbytes, transcendentals=0),
        name=name,
    )


def start_all(copies):
    for copy in copies:
        copy.start()


def wait_all(copies):
    for copy in copies:
        copy.wait()


def dot(a, b, dims):
    return lax.dot_general(a, b, (dims, ((), ())), preferred_element_type=jnp.float32)


def split_kernel(heads, count, *refs):
    arrays, out = refs[:count], refs[count]
    held, packed, sems, out_sems = refs[count + 1 :]
    reads = [pltpu.make_async_copy(arrays[w], held.at[w], sems.at[w]) for w in range(count)]
    writes = [
        pltpu.make_async_copy(packed.at[head], out.at[head], out_sems.at[head]) for head in range(heads)
    ]
    start_all(reads)
    wait_all(reads)
    for head in range(heads):
        for w in range(count):
            packed[head, w] = held[w, :, pl.ds(head * HEAD_DIM, HEAD_DIM)]
        writes[head].start()
    wait_all(writes)


def split_heads(*arrays):
    rows, features = arrays[0].shape
    heads, count = features // HEAD_DIM, len(arrays)
    dtype = arrays[0].dtype
    packed = (heads, count, rows, HEAD_DIM)
    return call(
        functools.partial(split_kernel, heads, count),
        pltpu.HBM(packed, dtype),
        [ANY] * count,
        ANY,
        "split_heads",
        0,
        4 * count * arrays[0].size,
        [
            pltpu.VMEM((count, rows, features), dtype),
            pltpu.VMEM(packed, dtype),
            pltpu.SemaphoreType.DMA((count,)),
            pltpu.SemaphoreType.DMA((heads,)),
        ],
        FULL,
    )(*arrays)


def join_kernel(heads, count, in_ref, *refs):
    outs = refs[:count]
    held, sems = refs[count:]
    writes = [pltpu.make_async_copy(held.at[w], outs[w], sems.at[w]) for w in range(count)]
    for w in range(count):
        for head in range(heads):
            held[w, :, pl.ds(head * HEAD_DIM, HEAD_DIM)] = in_ref[head, w]
        writes[w].start()
    wait_all(writes)


def join_heads(packed):
    heads, count, rows, depth = packed.shape
    features, dtype = heads * depth, packed.dtype
    return call(
        functools.partial(join_kernel, heads, count),
        (pltpu.HBM((rows, features), dtype),) * count,
        [VMEM],
        (ANY,) * count,
        "join_heads",
        0,
        4 * packed.size,
        [pltpu.VMEM((count, rows, features), dtype), pltpu.SemaphoreType.DMA((count,))],
    )(packed)


def pick_third_kernel(blocks, lanes, third_ref, kv_ref, *refs):
    thirds, edge_ref = refs[:lanes], refs[lanes]
    edge_ref[...] = kv_ref[blocks - 1]
    for step in range(lanes):
        for side in range(2):
            index = third_ref[2 * step + side]

            @pl.when(index >= 0)
            def _():
                thirds[step][side] = kv_ref[index]


def pick_third(index, kv):
    lanes = index.shape[0] // 2
    outs = call(
        functools.partial(pick_third_kernel, kv.shape[0], lanes),
        (jax.ShapeDtypeStruct((2,) + kv.shape[1:], kv.dtype),) * lanes
        + (jax.ShapeDtypeStruct(kv.shape[1:], kv.dtype),),
        [SMEM, VMEM],
        (VMEM,) * (lanes + 1),
        "pick_third",
        0,
        8 * kv[0].size,
    )(index, kv)
    return outs[:lanes], outs[lanes]


def pack_kernel(rows, limit, index_ref, in_ref, out, sems):
    copies = [
        pltpu.make_async_copy(in_ref.at[jnp.minimum(index_ref[i], limit)], out.at[i], sems.at[i])
        for i in range(rows)
    ]
    start_all(copies)
    wait_all(copies)


def pack(index, array):
    rows = index.shape[0]
    return call(
        functools.partial(pack_kernel, rows, array.shape[0] - 1),
        pltpu.HBM((rows,) + array.shape[1:], array.dtype),
        [SMEM, VMEM],
        ANY,
        "pack",
        0,
        4 * rows * array[0].size,
        [pltpu.SemaphoreType.DMA((rows,))],
    )(index, array)


def pick_cross_kernel(lanes, step_ref, *refs):
    ins, out_ref = refs[:lanes], refs[lanes]
    for j in range(2):
        for step in range(lanes):

            @pl.when(step_ref[j] == step)
            def _():
                out_ref[j] = ins[step][1]


def pick_cross(steps, thirds):
    lanes = len(thirds)
    return call(
        functools.partial(pick_cross_kernel, lanes),
        jax.ShapeDtypeStruct(thirds[0].shape, thirds[0].dtype),
        [SMEM] + [VMEM] * lanes,
        VMEM,
        "pick_cross",
        0,
        4 * thirds[0].size,
    )(steps, *thirds)


def pick_back_kernel(lanes, near_ref, cross_ref, own, crossed, *outs):
    for j in range(2):
        for step in range(lanes):

            @pl.when(near_ref[j] == step)
            def _():
                outs[step][0] = own[j]

            @pl.when(cross_ref[j] == step)
            def _():
                outs[step][1] = crossed[j]


def pick_back(near_steps, cross_steps, own, crossed, lanes):
    return call(
        functools.partial(pick_back_kernel, lanes),
        (jax.ShapeDtypeStruct(own.shape, own.dtype),) * lanes,
        [SMEM, SMEM, VMEM, VMEM],
        (VMEM,) * lanes,
        "pick_back",
        0,
        8 * own.size,
    )(near_steps, cross_steps, own, crossed)


def attention(q, g, k, v):
    scale = HEAD_DIM ** (-0.5)
    s = dot(k, q, ((1,), (1,))) * scale
    dp = dot(v, g, ((1,), (1,)))
    w = jnp.exp(s - jnp.max(s, axis=0, keepdims=True))
    p = w * (1.0 / jnp.sum(w, axis=0, keepdims=True))
    p_low = p.astype(jnp.bfloat16)
    delta = jnp.sum(p_low.astype(jnp.float32) * dp, axis=0, keepdims=True)
    return p_low, (p * (dp - delta) * scale).astype(jnp.bfloat16)


def collect_kernel(lanes, slots, request_ref, third_ref, near_ref, kv_ref, qg_ref, edge_ref, cross_ref, main_ref, *refs):
    thirds = refs[:lanes]
    far_ref, grad_ref = refs[lanes:]
    for slot in range(slots):
        far_ref[request_ref[slot]] = main_ref[slot]
    for j in range(2):
        for step in range(1, lanes):

            @pl.when(near_ref[j] == step)
            def _():
                far_ref[third_ref[j]] = thirds[step][0]

        @pl.when(near_ref[j] < 0)
        def _():
            far_ref[third_ref[j]] = cross_ref[j]

    for j in range(2):
        r = third_ref[j]
        n = r // 2
        other = n * 4 + 1 - r
        listed = []
        for which in range(2):
            before = jnp.where(n == 0, edge_ref[which], kv_ref[jnp.maximum(n - 1, 0), which])
            listed.append(
                jnp.concatenate(
                    [far_ref[r, which], kv_ref[n, which], before, far_ref[other, which]], axis=0
                )
            )
        q, g = qg_ref[n, 0], qg_ref[n, 1]
        p_low, ds = attention(q, g, *listed)
        grad_ref[j, 0] = dot(ds[:BLOCK], q, ((1,), (0,))).astype(grad_ref.dtype)
        grad_ref[j, 1] = dot(p_low[:BLOCK], g, ((1,), (0,))).astype(grad_ref.dtype)


def collect(request, third, near, kv, qg, edge, cross, main, thirds):
    lanes, slots = len(thirds), main.shape[0]
    return call(
        functools.partial(collect_kernel, lanes, slots),
        (
            jax.ShapeDtypeStruct((slots + 1,) + kv.shape[1:], kv.dtype),
            jax.ShapeDtypeStruct(cross.shape, cross.dtype),
        ),
        [SMEM] * 3 + [VMEM] * (5 + lanes),
        (VMEM, VMEM),
        "collect",
        5 * 2 * 2 * 4 * BLOCK * BLOCK * HEAD_DIM,
        4 * main.size,
    )(request, third, near, kv, qg, edge, cross, main, *thirds)


def attend_kernel(blocks, kv_ref, qg_ref, edge_ref, far_ref, out, sum_ref, edge_out, far_out, out_ref, sems):
    bf16 = jnp.bfloat16

    def finished(n):
        return pltpu.make_async_copy(out_ref.at[n], out.at[n], sems.at[n])

    def one(n, first):
        q, g = qg_ref[n, 0], qg_ref[n, 1]
        r2, r3 = 2 * n, 2 * n + 1
        listed = []
        for which in range(2):
            before = edge_ref[which] if first else kv_ref[n - 1, which]
            listed.append(
                jnp.concatenate([kv_ref[n, which], before, far_ref[r2, which], far_ref[r3, which]], axis=0)
            )
        k, v = listed
        p_low, ds = attention(q, g, k, v)
        out_ref[n, 0] = dot(p_low, v, ((0,), (0,))).astype(bf16)
        out_ref[n, 1] = dot(ds, k, ((0,), (0,))).astype(bf16)
        finished(n).start()
        dk = dot(ds, q, ((1,), (0,)))
        dv = dot(p_low, g, ((1,), (0,)))
        for which, d in enumerate((dk, dv)):
            sum_ref[n, which] = d[:BLOCK]
            if first:
                edge_out[which] = d[BLOCK : 2 * BLOCK].astype(bf16)
            else:
                sum_ref[n - 1, which] += d[BLOCK : 2 * BLOCK]
            far_out[r2, which] = d[2 * BLOCK : 3 * BLOCK].astype(bf16)
            far_out[r3, which] = d[3 * BLOCK :].astype(bf16)

    one(0, True)
    lax.fori_loop(1, blocks, lambda n, _: one(n, False), None, unroll=3)
    wait_all([finished(n) for n in range(blocks)])


def attend(kv, qg, edge, far):
    blocks = kv.shape[0]
    bf16 = kv.dtype
    return call(
        functools.partial(attend_kernel, blocks),
        (
            pltpu.HBM(qg.shape, bf16),
            jax.ShapeDtypeStruct(kv.shape, jnp.float32),
            jax.ShapeDtypeStruct(edge.shape, bf16),
            jax.ShapeDtypeStruct((2 * blocks,) + kv.shape[1:], bf16),
        ),
        [VMEM] * 4,
        (ANY, VMEM, VMEM, VMEM),
        "attend",
        5 * 2 * blocks * 4 * BLOCK * BLOCK * HEAD_DIM,
        2 * (6 * kv.size + 2 * far.size),
        [pltpu.VMEM(qg.shape, bf16), pltpu.SemaphoreType.DMA((blocks,))],
    )(kv, qg, edge, far)


def land_kernel(
    blocks, lanes, slots, main_ref, third_ref, sum_ref, edge_ref, home_ref, *refs
):
    thirds, out = refs[:lanes], refs[lanes]
    total, low, sems = refs[lanes + 1 :]
    f32 = jnp.float32
    total[pl.ds(0, blocks)] = sum_ref[...]
    total[blocks - 1] += edge_ref[...].astype(f32)
    for step in range(lanes):
        for side in range(2):
            index = third_ref[2 * step + side]

            @pl.when(index >= 0)
            def _():
                total[index] += thirds[step][side].astype(f32)

    for slot in range(slots):
        total[main_ref[slot]] += home_ref[slot].astype(f32)
    writes = [pltpu.make_async_copy(low.at[n], out.at[n], sems.at[n]) for n in range(blocks)]
    for n in range(blocks):
        low[n] = total[n].astype(low.dtype)
        writes[n].start()
    wait_all(writes)


def land(main_index, third_index, sums, edge, home, thirds):
    blocks, lanes, slots = sums.shape[0], len(thirds), home.shape[0]
    return call(
        functools.partial(land_kernel, blocks, lanes, slots),
        pltpu.HBM(sums.shape, home.dtype),
        [SMEM] * 2 + [VMEM] * (3 + lanes),
        ANY,
        "land",
        sums.size * 2,
        10 * sums.size,
        [
            pltpu.VMEM((blocks + 1,) + sums.shape[1:], jnp.float32),
            pltpu.VMEM(sums.shape, home.dtype),
            pltpu.SemaphoreType.DMA((blocks,)),
        ],
    )(main_index, third_index, sums, edge, home, *thirds)


def plan(key_lists, blocks, ctx_count, lanes):
    i32 = jnp.int32
    me = lax.axis_index("ctx")
    half, lane = me // lanes, me % lanes
    requests = 2 * blocks
    slabs = jnp.arange(ctx_count, dtype=i32)
    numbers = jnp.arange(requests, dtype=i32)
    far_all = key_lists[:, 2:].reshape(ctx_count, requests)
    source, inside = far_all // blocks, far_all % blocks
    earlier = (numbers[None, :] < numbers[:, None])[None]
    rank = jnp.sum(((source[:, None, :] == source[:, :, None]) & earlier).astype(i32), axis=2)
    is_third = rank == 2
    order = jnp.sum((is_third[:, None, :] & earlier).astype(i32), axis=2)
    pair = jnp.arange(2, dtype=i32)[None, :, None]

    wanted = (source[:, None, :] == me) & (rank[:, None, :] == pair)
    send_main = jnp.sum(jnp.where(wanted, inside[:, None, :], 0), axis=2)
    main_index = jnp.where(slabs[:, None] == me, blocks, send_main).reshape(-1)
    from_me = is_third & (source == me)
    third_of = jnp.sum(jnp.where(from_me, inside + 1, 0), axis=1) - 1

    step = jnp.arange(lanes, dtype=i32)[:, None]
    side = jnp.arange(2, dtype=i32)[None, :]
    third_asker = jnp.where(side == 0, half, 1 - half) * lanes + (lane + step) % lanes
    hit = third_asker[:, :, None] == slabs[None, None, :]
    third_index = jnp.sum(jnp.where(hit, third_of[None, None, :], 0), axis=2).reshape(-1)

    def row(of, array):
        return jnp.sum(jnp.where(slabs[:, None] == of, array, 0), axis=0)

    my_source, my_rank = row(me, source), row(me, rank)
    serves = (slabs[:, None, None] == my_source[None, None, :]) & (pair == my_rank[None, None, :])
    request = jnp.sum(jnp.where(serves, numbers[None, None, :], 0), axis=2)
    request = jnp.where(slabs[:, None] == me, requests, request).reshape(-1)

    is_jth = (is_third[:, None, :] & (order[:, None, :] == pair)).astype(i32)
    third_source = jnp.sum(is_jth * source[:, None, :], axis=2)
    third_request = jnp.sum(is_jth * numbers, axis=2)

    def steps(of):
        slab = row(of, third_source)
        return jnp.where(slab // lanes == half, (lane - slab % lanes + lanes) % lanes, -1)

    partner = (me + lanes) % ctx_count
    return main_index, third_index, request, row(me, third_request), steps(me), steps(partner)


def body(queries, keys, values, out_grad, key_lists):
    ctx_count = lax.axis_size("ctx")
    blocks = lax.axis_size("head")
    lanes = ctx_count // 2
    main_index, third_index, request, my_third, near_steps, cross_steps = plan(
        key_lists, blocks, ctx_count, lanes
    )

    def head_exchange(array):
        return lax.all_to_all(array, "head", split_axis=0, concat_axis=0, tiled=True)

    def ctx_exchange(array):
        return lax.all_to_all(array, "ctx", split_axis=0, concat_axis=0, tiled=True)

    def move(array, target):
        return lax.ppermute(array, "ctx", [(i, target(i)) for i in range(ctx_count)])

    def across(array):
        return move(array, lambda i: (i + lanes) % ctx_count)

    def along(arrays, sign):
        def target(step):
            return lambda i: i // lanes * lanes + (i + sign * step) % lanes

        return [arrays[0]] + [move(arrays[s], target(s)) for s in range(1, lanes)]

    kv = head_exchange(split_heads(keys, values))
    qg = head_exchange(split_heads(queries, out_grad))
    thirds, edge = pick_third(third_index, kv)
    edge = move(edge, lambda i: (i + 1) % ctx_count)
    thirds = along(thirds, 1)
    cross = across(pick_cross(cross_steps, thirds))
    packed, edge, cross = lax.optimization_barrier((pack(main_index, kv), edge, cross))
    main = ctx_exchange(packed)
    far, third_grad = collect(request, my_third, near_steps, kv, qg, edge, cross, main, thirds)
    cross_grad = across(third_grad)
    out, sums, edge_grad, far_grad = attend(kv, qg, edge, far)
    out, cross_grad = lax.optimization_barrier((out, cross_grad))
    out = head_exchange(out)
    edge_grad = move(edge_grad, lambda i: (i - 1) % ctx_count)
    late = along(pick_back(near_steps, cross_steps, third_grad, cross_grad, lanes), -1)
    packed, out, edge_grad, late = lax.optimization_barrier(
        (pack(request, far_grad), out, edge_grad, late)
    )
    home = ctx_exchange(packed)
    attended, query_grad = join_heads(out)
    total = land(main_index, third_index, sums, edge_grad, home, late)
    key_grad, value_grad = join_heads(head_exchange(total))
    return attended, query_grad, key_grad, value_grad


def solution(mesh):
    tokens = P(("ctx", "head"), None)
    return jax.shard_map(
        body,
        mesh=mesh,
        in_specs=(tokens, tokens, tokens, tokens, P()),
        out_specs=(tokens, tokens, tokens, tokens),
        check_vma=False,
    )
```

profile of v0, /device:TPU:56, one launch (start us, length us, event | category | flops | bytes accessed | tf_op | source)
XLA Modules:
  0.0 287.9 jit_solution(18020800818424778700)
XLA Ops:
  0.6 2.4 split_heads.2
  3.0 8.5 %all-to-all-start = ((bf16[16,2,128,128]{3,2,1,0:T(8,128)(2,1)}), bf16[16,2,128,128]{3,2,1,0:T(8,128)(2,1)S(1)}, u32[]{:S(2)}, u32[]{:S(2)}) async-start(bf16[16,2,128,128]{3,2,1,0:T(8,128)(2,1)} %split_heads.2), calls=%async_computation | async-start | bytes 2097152 | tf_op jit(solution)/shard_map/all_to_all | solution.py:424
  12.8 2.4 split_heads.3
  15.3 21.9 %all-to-all-done.in_ref.kv_ref = bf16[16,2,128,128]{3,2,1,0:T(8,128)(2,1)S(1)} async-done(((bf16[16,2,128,128]{3,2,1,0:T(8,128)(2,1)}), bf16[16,2,128,128]{3,2,1,0:T(8,128)(2,1)S(1)}, u32[]{:S(2)}, u32[]{:S(2)}) %all-to-all-start) | async-done | bytes 1048608 | tf_op jit(solution)/shard_map/all_to_all | solution.py:424
  37.2 5.2 %all-to-all-start.1 = ((bf16[16,2,128,128]{3,2,1,0:T(8,128)(2,1)}), bf16[16,2,128,128]{3,2,1,0:T(8,128)(2,1)S(1)}, u32[]{:S(2)}, u32[]{:S(2)}) async-start(bf16[16,2,128,128]{3,2,1,0:T(8,128)(2,1)} %split_heads.3), calls=%async_computation.1 | async-start | bytes 2097152 | tf_op jit(solution)/shard_map/all_to_all | solution.py:424
  45.4 2.6 collective-permute-start.3
  53.6 2.3 collective-permute-done.4.refs_4_
  55.9 2.5 collective-permute-done.5.refs_5_
  60.8 4.6 %collective-permute-start.8 = (bf16[2,2,128,128]{3,2,1,0:T(8,128)(2,1)S(1)}, bf16[2,2,128,128]{3,2,1,0:T(8,128)(2,1)S(1)}, u32[]{:S(2)}, u32[]{:S(2)}) collective-permute-start(bf16[2,2,128,128]{3,2,1,0:T(8,128)(2,1)S(1)} %pick_cross.1), channel_id=1, source_target_pairs={{0,128},{16,144},{32,160},{48,176},{64,192},{80,208},{96,224},{112... | collective-permute-start | bytes 393224 | tf_op jit(solution)/shard_map/ppermute | solution.py:430
  72.7 10.0 %all-to-all-start.2 = ((bf16[32,2,128,128]{3,2,1,0:T(8,128)(2,1)}), bf16[32,2,128,128]{3,2,1,0:T(8,128)(2,1)}, u32[]{:S(2)}, u32[]{:S(2)}) async-start(bf16[32,2,128,128]{3,2,1,0:T(8,128)(2,1)} %pack.2), calls=%async_computation.2 | async-start | bytes 4194304 | tf_op jit(solution)/shard_map/all_to_all | solution.py:427
  82.9 51.4 %all-to-all-done.2.main_ref = bf16[32,2,128,128]{3,2,1,0:T(8,128)(2,1)} async-done(((bf16[32,2,128,128]{3,2,1,0:T(8,128)(2,1)}), bf16[32,2,128,128]{3,2,1,0:T(8,128)(2,1)}, u32[]{:S(2)}, u32[]{:S(2)}) %all-to-all-start.2) | async-done | bytes 2097184 | tf_op jit(solution)/shard_map/all_to_all | solution.py:427
  134.3 4.5 %collect.1 = (bf16[33,2,128,128]{3,2,1,0:T(8,128)(2,1)}, bf16[2,2,128,128]{3,2,1,0:T(8,128)(2,1)S(1)}) custom-call(s32[32]{0:T(128)S(1)} %select_n.154.request_ref.index_ref, s32[2]{0:T(128)S(1)} %get-tuple-element.94.third_ref, s32[2]{0:T(128)S(1)} %compare_select_fusion.6.near_ref, bf16[16,2,128,128]{3,2,1,0:T(8,128)(2,1)} %copy-done, ...), custom_call_target="tpu_custom_call" | custom-call | flops 167772160 | bytes 4194304 | tf_op jit(solution)/shard_map/collect/pallas_call | solution.py:255
  141.0 14.7 %attend.1 = (bf16[16,2,128,128]{3,2,1,0:T(8,128)(2,1)}, f32[16,2,128,128]{3,2,1,0:T(8,128)}, bf16[2,128,128]{2,1,0:T(8,128)(2,1)S(1)}, bf16[32,2,128,128]{3,2,1,0:T(8,128)(2,1)}) custom-call(bf16[16,2,128,128]{3,2,1,0:T(8,128)(2,1)S(1)} %copy-done.2, bf16[16,2,128,128]{3,2,1,0:T(8,128)(2,1)} %copy-done.3, ...), custom_call_target="tpu_custom_call" | custom-call | flops 1342177280 | bytes 10616832 | tf_op jit(solution)/shard_map/attend/pallas_call | solution.py:308
  155.7 9.8 %all-to-all-start.3 = ((bf16[16,2,128,128]{3,2,1,0:T(8,128)(2,1)}), bf16[16,2,128,128]{3,2,1,0:T(8,128)(2,1)S(1)}, u32[]{:S(2)}, u32[]{:S(2)}) async-start(bf16[16,2,128,128]{3,2,1,0:T(8,128)(2,1)} %get-tuple-element.63), calls=%async_computation.3 | async-start | bytes 2097152 | tf_op jit(solution)/shard_map/all_to_all | solution.py:424
  166.5 3.5 %collective-permute-start.13 = (bf16[2,2,128,128]{3,2,1,0:T(8,128)(2,1)S(1)}, bf16[2,2,128,128]{3,2,1,0:T(8,128)(2,1)S(1)}, u32[]{:S(2)}, u32[]{:S(2)}) collective-permute-start(bf16[2,2,128,128]{3,2,1,0:T(8,128)(2,1)S(1)} %get-tuple-element.69), channel_id=1, source_target_pairs={{0,80},{16,96},{32,112},{48,0},{64,16},{80,32},{96,48},{112,64},{1... | collective-permute-start | bytes 393224 | tf_op jit(solution)/shard_map/ppermute | solution.py:430
  170.8 2.7 collective-permute-done.10.edge_ref
  173.5 4.0 %collective-permute-start.16 = (bf16[2,2,128,128]{3,2,1,0:T(8,128)(2,1)S(1)}, bf16[2,2,128,128]{3,2,1,0:T(8,128)(2,1)S(1)}, u32[]{:S(2)}, u32[]{:S(2)}) collective-permute-start(bf16[2,2,128,128]{3,2,1,0:T(8,128)(2,1)S(1)} %get-tuple-element.72), channel_id=1, source_target_pairs={{0,32},{16,48},{32,64},{48,80},{64,96},{80,112},{96,0},{112,16},{1... | collective-permute-start | bytes 393224 | tf_op jit(solution)/shard_map/ppermute | solution.py:430
  177.7 4.3 %collective-permute-start.17 = (bf16[2,2,128,128]{3,2,1,0:T(8,128)(2,1)S(1)}, bf16[2,2,128,128]{3,2,1,0:T(8,128)(2,1)S(1)}, u32[]{:S(2)}, u32[]{:S(2)}) collective-permute-start(bf16[2,2,128,128]{3,2,1,0:T(8,128)(2,1)S(1)} %get-tuple-element.73), channel_id=1, source_target_pairs={{0,16},{16,32},{32,48},{48,64},{64,80},{80,96},{96,112},{112,0},{1... | collective-permute-start | bytes 393224 | tf_op jit(solution)/shard_map/ppermute | solution.py:430
  182.0 3.2 %pack.3 = bf16[32,2,128,128]{3,2,1,0:T(8,128)(2,1)} custom-call(s32[32]{0:T(128)S(1)} %select_n.154.request_ref.index_ref, bf16[32,2,128,128]{3,2,1,0:T(8,128)(2,1)} %get-tuple-element.60.in_ref), custom_call_target="tpu_custom_call" | custom-call | bytes 4194304 | tf_op jit(solution)/shard_map/pack/pallas_call | solution.py:148
  185.3 4.9 %collective-permute-done.16.refs_6_ = bf16[2,2,128,128]{3,2,1,0:T(8,128)(2,1)S(1)} collective-permute-done((bf16[2,2,128,128]{3,2,1,0:T(8,128)(2,1)S(1)}, bf16[2,2,128,128]{3,2,1,0:T(8,128)(2,1)S(1)}, u32[]{:S(2)}, u32[]{:S(2)}) %collective-permute-start.16) | collective-permute-done | bytes 131104 | tf_op jit(solution)/shard_map/ppermute | solution.py:430
  191.2 58.9 %all_to_all.30.home_ref = bf16[32,2,128,128]{3,2,1,0:T(8,128)(2,1)} all-to-all(bf16[32,2,128,128]{3,2,1,0:T(8,128)(2,1)} %pack.3), channel_id=1, replica_groups=mesh['ctx'=16,'head'=16] {'ctx'}, dimensions={0} | all-to-all | bytes 4194304 | tf_op jit(solution)/shard_map/all_to_all | solution.py:427
  250.1 4.0 %land.1 = bf16[16,2,128,128]{3,2,1,0:T(8,128)(2,1)} custom-call(s32[32]{0:T(128)S(1)} %select_n.158.index_ref.main_ref, s32[16]{0:T(128)S(1)} %reshape.251.third_ref, f32[16,2,128,128]{3,2,1,0:T(8,128)} %get-tuple-element.77.sum_ref, bf16[2,128,128]{2,1,0:T(8,128)(2,1)S(1)} %collective-permute-done.10.edge_ref, ...), custom_call_target="tpu_custom_call" | custom-call | flops 1048576 | bytes 5242880 | tf_op jit(solution)/shard_map/land/pallas_call | solution.py:352
  254.1 6.5 %all-to-all-start.5 = ((bf16[16,2,128,128]{3,2,1,0:T(8,128)(2,1)}), bf16[16,2,128,128]{3,2,1,0:T(8,128)(2,1)S(1)}, u32[]{:S(2)}, u32[]{:S(2)}) async-start(bf16[16,2,128,128]{3,2,1,0:T(8,128)(2,1)} %land.1), calls=%async_computation.5 | async-start | bytes 2097152 | tf_op jit(solution)/shard_map/all_to_all | solution.py:424
  261.7 24.9 %all-to-all-done.5.in_ref = bf16[16,2,128,128]{3,2,1,0:T(8,128)(2,1)S(1)} async-done(((bf16[16,2,128,128]{3,2,1,0:T(8,128)(2,1)}), bf16[16,2,128,128]{3,2,1,0:T(8,128)(2,1)S(1)}, u32[]{:S(2)}, u32[]{:S(2)}) %all-to-all-start.5) | async-done | bytes 1048608 | tf_op jit(solution)/shard_map/all_to_all | solution.py:424
  (78 shorter events, 27.2 us)
Async XLA Ops:
  0.6 10.9 %copy-start.4 = (s32[256,4]{0,1:T(4,128)S(1)}, s32[256,4]{0,1:T(4,128)}, u32[]{:S(2)}) copy-start(s32[256,4]{0,1:T(4,128)} %param.9) | copy-start | bytes 12292
  3.0 34.2 %all-to-all-start = ((bf16[16,2,128,128]{3,2,1,0:T(8,128)(2,1)}), bf16[16,2,128,128]{3,2,1,0:T(8,128)(2,1)S(1)}, u32[]{:S(2)}, u32[]{:S(2)}) async-start(bf16[16,2,128,128]{3,2,1,0:T(8,128)(2,1)} %split_heads.2), calls=%async_computation | async-start | bytes 2097152 | tf_op jit(solution)/shard_map/all_to_all | solution.py:424
  37.2 35.5 %all-to-all-start.1 = ((bf16[16,2,128,128]{3,2,1,0:T(8,128)(2,1)}), bf16[16,2,128,128]{3,2,1,0:T(8,128)(2,1)S(1)}, u32[]{:S(2)}, u32[]{:S(2)}) async-start(bf16[16,2,128,128]{3,2,1,0:T(8,128)(2,1)} %split_heads.3), calls=%async_computation.1 | async-start | bytes 2097152 | tf_op jit(solution)/shard_map/all_to_all | solution.py:424
  45.0 6.1 %collective-permute-start.1 = (bf16[2,2,128,128]{3,2,1,0:T(8,128)(2,1)S(1)}, bf16[2,2,128,128]{3,2,1,0:T(8,128)(2,1)S(1)}, u32[]{:S(2)}, u32[]{:S(2)}) collective-permute-start(bf16[2,2,128,128]{3,2,1,0:T(8,128)(2,1)S(1)} %get-tuple-element.49), channel_id=1, source_target_pairs={{0,16},{16,32},{32,48},{48,64},{64,80},{80,96},{96,112},{112,0},{1... | collective-permute-start | bytes 393224 | tf_op jit(solution)/shard_map/ppermute | solution.py:430
  45.0 6.4 %collective-permute-start.2 = (bf16[2,2,128,128]{3,2,1,0:T(8,128)(2,1)S(1)}, bf16[2,2,128,128]{3,2,1,0:T(8,128)(2,1)S(1)}, u32[]{:S(2)}, u32[]{:S(2)}) collective-permute-start(bf16[2,2,128,128]{3,2,1,0:T(8,128)(2,1)S(1)} %get-tuple-element.50), channel_id=1, source_target_pairs={{0,32},{16,48},{32,64},{48,80},{64,96},{80,112},{96,0},{112,16},{1... | collective-permute-start | bytes 393224 | tf_op jit(solution)/shard_map/ppermute | solution.py:430
  45.4 8.1 %collective-permute-start.3 = (bf16[2,2,128,128]{3,2,1,0:T(8,128)(2,1)S(1)}, bf16[2,2,128,128]{3,2,1,0:T(8,128)(2,1)S(1)}, u32[]{:S(2)}, u32[]{:S(2)}) collective-permute-start(bf16[2,2,128,128]{3,2,1,0:T(8,128)(2,1)S(1)} %get-tuple-element.51), channel_id=1, source_target_pairs={{0,48},{16,64},{32,80},{48,96},{64,112},{80,0},{96,16},{112,32},{1... | collective-permute-start | bytes 393224 | tf_op jit(solution)/shard_map/ppermute | solution.py:430
  48.0 7.8 %collective-permute-start.4 = (bf16[2,2,128,128]{3,2,1,0:T(8,128)(2,1)S(1)}, bf16[2,2,128,128]{3,2,1,0:T(8,128)(2,1)S(1)}, u32[]{:S(2)}, u32[]{:S(2)}) collective-permute-start(bf16[2,2,128,128]{3,2,1,0:T(8,128)(2,1)S(1)} %get-tuple-element.52), channel_id=1, source_target_pairs={{0,64},{16,80},{32,96},{48,112},{64,0},{80,16},{96,32},{112,48},{1... | collective-permute-start | bytes 393224 | tf_op jit(solution)/shard_map/ppermute | solution.py:430
  49.0 9.4 %collective-permute-start.5 = (bf16[2,2,128,128]{3,2,1,0:T(8,128)(2,1)S(1)}, bf16[2,2,128,128]{3,2,1,0:T(8,128)(2,1)S(1)}, u32[]{:S(2)}, u32[]{:S(2)}) collective-permute-start(bf16[2,2,128,128]{3,2,1,0:T(8,128)(2,1)S(1)} %get-tuple-element.53), channel_id=1, source_target_pairs={{0,80},{16,96},{32,112},{48,0},{64,16},{80,32},{96,48},{112,64},{1... | collective-permute-start | bytes 393224 | tf_op jit(solution)/shard_map/ppermute | solution.py:430
  51.1 9.1 %collective-permute-start.6 = (bf16[2,2,128,128]{3,2,1,0:T(8,128)(2,1)S(1)}, bf16[2,2,128,128]{3,2,1,0:T(8,128)(2,1)S(1)}, u32[]{:S(2)}, u32[]{:S(2)}) collective-permute-start(bf16[2,2,128,128]{3,2,1,0:T(8,128)(2,1)S(1)} %get-tuple-element.54), channel_id=1, source_target_pairs={{0,96},{16,112},{32,0},{48,16},{64,32},{80,48},{96,64},{112,80},{1... | collective-permute-start | bytes 393224 | tf_op jit(solution)/shard_map/ppermute | solution.py:430
  51.4 8.7 %collective-permute-start.7 = (bf16[2,2,128,128]{3,2,1,0:T(8,128)(2,1)S(1)}, bf16[2,2,128,128]{3,2,1,0:T(8,128)(2,1)S(1)}, u32[]{:S(2)}, u32[]{:S(2)}) collective-permute-start(bf16[2,2,128,128]{3,2,1,0:T(8,128)(2,1)S(1)} %get-tuple-element.55), channel_id=1, source_target_pairs={{0,112},{16,0},{32,16},{48,32},{64,48},{80,64},{96,80},{112,96},{1... | collective-permute-start | bytes 393224 | tf_op jit(solution)/shard_map/ppermute | solution.py:430
  60.8 11.9 %collective-permute-start.8 = (bf16[2,2,128,128]{3,2,1,0:T(8,128)(2,1)S(1)}, bf16[2,2,128,128]{3,2,1,0:T(8,128)(2,1)S(1)}, u32[]{:S(2)}, u32[]{:S(2)}) collective-permute-start(bf16[2,2,128,128]{3,2,1,0:T(8,128)(2,1)S(1)} %pick_cross.1), channel_id=1, source_target_pairs={{0,128},{16,144},{32,160},{48,176},{64,192},{80,208},{96,224},{112... | collective-permute-start | bytes 393224 | tf_op jit(solution)/shard_map/ppermute | solution.py:430
  65.4 5.1 %collective-permute-start = (bf16[2,128,128]{2,1,0:T(8,128)(2,1)S(1)}, bf16[2,128,128]{2,1,0:T(8,128)(2,1)S(1)}, u32[]{:S(2)}, u32[]{:S(2)}) collective-permute-start(bf16[2,128,128]{2,1,0:T(8,128)(2,1)S(1)} %get-tuple-element.47), channel_id=1, source_target_pairs={{0,16},{16,32},{32,48},{48,64},{64,80},{80,96},{96,112},{112,128},... | collective-permute-start | bytes 196616 | tf_op jit(solution)/shard_map/ppermute | solution.py:430
  72.7 61.6 %all-to-all-start.2 = ((bf16[32,2,128,128]{3,2,1,0:T(8,128)(2,1)}), bf16[32,2,128,128]{3,2,1,0:T(8,128)(2,1)}, u32[]{:S(2)}, u32[]{:S(2)}) async-start(bf16[32,2,128,128]{3,2,1,0:T(8,128)(2,1)} %pack.2), calls=%async_computation.2 | async-start | bytes 4194304 | tf_op jit(solution)/shard_map/all_to_all | solution.py:427
  138.9 16.8 %collective-permute-start.9 = (bf16[2,2,128,128]{3,2,1,0:T(8,128)(2,1)S(1)}, bf16[2,2,128,128]{3,2,1,0:T(8,128)(2,1)S(1)}, u32[]{:S(2)}, u32[]{:S(2)}) collective-permute-start(bf16[2,2,128,128]{3,2,1,0:T(8,128)(2,1)S(1)} %get-tuple-element.62.own), channel_id=1, source_target_pairs={{0,128},{16,144},{32,160},{48,176},{64,192},{80,208},{96,224},{112... | collective-permute-start | bytes 393224 | tf_op jit(solution)/shard_map/ppermute | solution.py:430
  155.7 35.5 %all-to-all-start.3 = ((bf16[16,2,128,128]{3,2,1,0:T(8,128)(2,1)}), bf16[16,2,128,128]{3,2,1,0:T(8,128)(2,1)S(1)}, u32[]{:S(2)}, u32[]{:S(2)}) async-start(bf16[16,2,128,128]{3,2,1,0:T(8,128)(2,1)} %get-tuple-element.63), calls=%async_computation.3 | async-start | bytes 2097152 | tf_op jit(solution)/shard_map/all_to_all | solution.py:424
  166.3 7.2 %collective-permute-start.11 = (bf16[2,2,128,128]{3,2,1,0:T(8,128)(2,1)S(1)}, bf16[2,2,128,128]{3,2,1,0:T(8,128)(2,1)S(1)}, u32[]{:S(2)}, u32[]{:S(2)}) collective-permute-start(bf16[2,2,128,128]{3,2,1,0:T(8,128)(2,1)S(1)} %get-tuple-element.67), channel_id=1, source_target_pairs={{0,112},{16,0},{32,16},{48,32},{64,48},{80,64},{96,80},{112,96},{1... | collective-permute-start | bytes 393224 | tf_op jit(solution)/shard_map/ppermute | solution.py:430
  166.3 11.4 %collective-permute-start.12 = (bf16[2,2,128,128]{3,2,1,0:T(8,128)(2,1)S(1)}, bf16[2,2,128,128]{3,2,1,0:T(8,128)(2,1)S(1)}, u32[]{:S(2)}, u32[]{:S(2)}) collective-permute-start(bf16[2,2,128,128]{3,2,1,0:T(8,128)(2,1)S(1)} %get-tuple-element.68), channel_id=1, source_target_pairs={{0,96},{16,112},{32,0},{48,16},{64,32},{80,48},{96,64},{112,80},{1... | collective-permute-start | bytes 393224 | tf_op jit(solution)/shard_map/ppermute | solution.py:430
  166.4 7.1 %collective-permute-start.10 = (bf16[2,128,128]{2,1,0:T(8,128)(2,1)S(1)}, bf16[2,128,128]{2,1,0:T(8,128)(2,1)S(1)}, u32[]{:S(2)}, u32[]{:S(2)}) collective-permute-start(bf16[2,128,128]{2,1,0:T(8,128)(2,1)S(1)} %get-tuple-element.64), channel_id=1, source_target_pairs={{0,240},{16,0},{32,16},{48,32},{64,48},{80,64},{96,80},{112,96},{1... | collective-permute-start | bytes 196616 | tf_op jit(solution)/shard_map/ppermute | solution.py:430
  166.5 18.8 %collective-permute-start.13 = (bf16[2,2,128,128]{3,2,1,0:T(8,128)(2,1)S(1)}, bf16[2,2,128,128]{3,2,1,0:T(8,128)(2,1)S(1)}, u32[]{:S(2)}, u32[]{:S(2)}) collective-permute-start(bf16[2,2,128,128]{3,2,1,0:T(8,128)(2,1)S(1)} %get-tuple-element.69), channel_id=1, source_target_pairs={{0,80},{16,96},{32,112},{48,0},{64,16},{80,32},{96,48},{112,64},{1... | collective-permute-start | bytes 393224 | tf_op jit(solution)/shard_map/ppermute | solution.py:430
  170.0 15.3 %collective-permute-start.14 = (bf16[2,2,128,128]{3,2,1,0:T(8,128)(2,1)S(1)}, bf16[2,2,128,128]{3,2,1,0:T(8,128)(2,1)S(1)}, u32[]{:S(2)}, u32[]{:S(2)}) collective-permute-start(bf16[2,2,128,128]{3,2,1,0:T(8,128)(2,1)S(1)} %get-tuple-element.70), channel_id=1, source_target_pairs={{0,64},{16,80},{32,96},{48,112},{64,0},{80,16},{96,32},{112,48},{1... | collective-permute-start | bytes 393224 | tf_op jit(solution)/shard_map/ppermute | solution.py:430
  173.5 11.8 %collective-permute-start.15 = (bf16[2,2,128,128]{3,2,1,0:T(8,128)(2,1)S(1)}, bf16[2,2,128,128]{3,2,1,0:T(8,128)(2,1)S(1)}, u32[]{:S(2)}, u32[]{:S(2)}) collective-permute-start(bf16[2,2,128,128]{3,2,1,0:T(8,128)(2,1)S(1)} %get-tuple-element.71), channel_id=1, source_target_pairs={{0,48},{16,64},{32,80},{48,96},{64,112},{80,0},{96,16},{112,32},{1... | collective-permute-start | bytes 393224 | tf_op jit(solution)/shard_map/ppermute | solution.py:430
  173.5 16.7 %collective-permute-start.16 = (bf16[2,2,128,128]{3,2,1,0:T(8,128)(2,1)S(1)}, bf16[2,2,128,128]{3,2,1,0:T(8,128)(2,1)S(1)}, u32[]{:S(2)}, u32[]{:S(2)}) collective-permute-start(bf16[2,2,128,128]{3,2,1,0:T(8,128)(2,1)S(1)} %get-tuple-element.72), channel_id=1, source_target_pairs={{0,32},{16,48},{32,64},{48,80},{64,96},{80,112},{96,0},{112,16},{1... | collective-permute-start | bytes 393224 | tf_op jit(solution)/shard_map/ppermute | solution.py:430
  177.7 12.5 %collective-permute-start.17 = (bf16[2,2,128,128]{3,2,1,0:T(8,128)(2,1)S(1)}, bf16[2,2,128,128]{3,2,1,0:T(8,128)(2,1)S(1)}, u32[]{:S(2)}, u32[]{:S(2)}) collective-permute-start(bf16[2,2,128,128]{3,2,1,0:T(8,128)(2,1)S(1)} %get-tuple-element.73), channel_id=1, source_target_pairs={{0,16},{16,32},{32,48},{48,64},{64,80},{80,96},{96,112},{112,0},{1... | collective-permute-start | bytes 393224 | tf_op jit(solution)/shard_map/ppermute | solution.py:430
  254.1 32.6 %all-to-all-start.5 = ((bf16[16,2,128,128]{3,2,1,0:T(8,128)(2,1)}), bf16[16,2,128,128]{3,2,1,0:T(8,128)(2,1)S(1)}, u32[]{:S(2)}, u32[]{:S(2)}) async-start(bf16[16,2,128,128]{3,2,1,0:T(8,128)(2,1)} %land.1), calls=%async_computation.5 | async-start | bytes 2097152 | tf_op jit(solution)/shard_map/all_to_all | solution.py:424
  (4 other events, 24.2 us)
where the time goes:
time: 290 us; the launch traced here: 288 us
  waiting for transfers between devices  116 us (40%)
  starting transfers between devices  69.2 us (24%)
  blocking collectives  58.9 us (20%)
  Pallas kernels  38.4 us (13%)
    all_to_all x1, blocking collectives, ctx_exchange(): return lax.all_to_all(array, 'ctx', split_axis=0, concat_axis=0, tiled=True)  58.9 us
    all_to_all x1, waiting for transfers between devices, ctx_exchange(): return lax.all_to_all(array, 'ctx', split_axis=0, concat_axis=0, tiled=True)  51.4 us
    all_to_all x4, waiting for transfers between devices, head_exchange(): lax.all_to_all(array, 'head', split_axis=0, concat_axis=0, tiled=True)  47.8 us
    all_to_all x4, starting transfers between devices, head_exchange(): lax.all_to_all(array, 'head', split_axis=0, concat_axis=0, tiled=True)  29.9 us
    ppermute x18, starting transfers between devices, move(): lax.ppermute(array, 'ctx', [(i, target(i)) for i in range(ctx_count)])  29.3 us
    ppermute x18, waiting for transfers between devices, move(): lax.ppermute(array, 'ctx', [(i, target(i)) for i in range(ctx_count)])  16.9 us
    pallas_call x1, Pallas kernels, attend(): call(functools.partial(attend_kernel, blocks), (pltpu.HBM(qg.shape, bf16)...  14.7 us
    all_to_all x1, starting transfers between devices, ctx_exchange(): return lax.all_to_all(array, 'ctx', split_axis=0, concat_axis=0, tiled=True)  9.97 us
  transfers between devices with their start and end apart: 23, of which 12 were waited for; matrix products, arithmetic and copies ran while one was open for 1% of the time, Pallas kernels for 9%

commit v1 on v0

--- a/solution.py
+++ b/solution.py
@@ -15,7 +15,7 @@
 FULL = 60 * 1024 * 1024
 
 
-def call(kernel, out_shape, ins, outs, name, flops, nbytes, scratch=(), limit=52 * 1024 * 1024):
+def call(kernel, out_shape, ins, outs, name, flops, nbytes, scratch=(), limit=50 * 1024 * 1024):
     return pl.pallas_call(
         kernel,
         out_shape=out_shape,
@@ -180,31 +180,6 @@
     )(steps, *thirds)
 
 
-def pick_back_kernel(lanes, near_ref, cross_ref, own, crossed, *outs):
-    for j in range(2):
-        for step in range(lanes):
-
-            @pl.when(near_ref[j] == step)
-            def _():
-                outs[step][0] = own[j]
-
-            @pl.when(cross_ref[j] == step)
-            def _():
-                outs[step][1] = crossed[j]
-
-
-def pick_back(near_steps, cross_steps, own, crossed, lanes):
-    return call(
-        functools.partial(pick_back_kernel, lanes),
-        (jax.ShapeDtypeStruct(own.shape, own.dtype),) * lanes,
-        [SMEM, SMEM, VMEM, VMEM],
-        (VMEM,) * lanes,
-        "pick_back",
-        0,
-        8 * own.size,
-    )(near_steps, cross_steps, own, crossed)
-
-
 def attention(q, g, k, v):
     scale = HEAD_DIM ** (-0.5)
     s = dot(k, q, ((1,), (1,))) * scale
@@ -216,61 +191,118 @@
     return p_low, (p * (dp - delta) * scale).astype(jnp.bfloat16)
 
 
-def collect_kernel(lanes, slots, request_ref, third_ref, near_ref, kv_ref, qg_ref, edge_ref, cross_ref, main_ref, *refs):
-    thirds = refs[:lanes]
-    far_ref, grad_ref = refs[lanes:]
-    for slot in range(slots):
-        far_ref[request_ref[slot]] = main_ref[slot]
+def collect_kernel(
+    lanes, slot_ref, third_ref, near_ref, kv, qg, edge, cross, main, *refs
+):
+    thirds, extra, grad_ref = refs[:lanes], refs[lanes], refs[lanes + 1]
+    held, asked, sems, far_sems = refs[lanes + 2 :]
     for j in range(2):
         for step in range(1, lanes):
 
             @pl.when(near_ref[j] == step)
             def _():
-                far_ref[third_ref[j]] = thirds[step][0]
+                pltpu.make_async_copy(thirds[step].at[0], extra.at[j], far_sems.at[j]).start()
 
         @pl.when(near_ref[j] < 0)
         def _():
-            far_ref[third_ref[j]] = cross_ref[j]
+            pltpu.make_async_copy(cross.at[j], extra.at[j], far_sems.at[j]).start()
 
     for j in range(2):
-        r = third_ref[j]
-        n = r // 2
-        other = n * 4 + 1 - r
-        listed = []
-        for which in range(2):
-            before = jnp.where(n == 0, edge_ref[which], kv_ref[jnp.maximum(n - 1, 0), which])
-            listed.append(
-                jnp.concatenate(
-                    [far_ref[r, which], kv_ref[n, which], before, far_ref[other, which]], axis=0
-                )
-            )
-        q, g = qg_ref[n, 0], qg_ref[n, 1]
-        p_low, ds = attention(q, g, *listed)
+        n = third_ref[j] // 2
+        slot = slot_ref[n * 4 + 1 - third_ref[j]]
+        pltpu.make_async_copy(kv.at[n], held.at[j, 0], sems.at[j, 0]).start()
+        pltpu.make_async_copy(qg.at[n], asked.at[j], sems.at[j, 3]).start()
+
+        @pl.when(n == 0)
+        def _():
+            pltpu.make_async_copy(edge, held.at[j, 1], sems.at[j, 1]).start()
+
+        @pl.when(n > 0)
+        def _():
+            pltpu.make_async_copy(kv.at[n - 1], held.at[j, 1], sems.at[j, 1]).start()
+
+        @pl.when(slot >= 0)
+        def _():
+            pltpu.make_async_copy(main.at[slot], held.at[j, 2], sems.at[j, 2]).start()
+
+    for j in range(2):
+        pltpu.make_async_copy(cross.at[j], extra.at[j], far_sems.at[j]).wait()
+    for j in range(2):
+        slot = slot_ref[third_ref[j] // 2 * 4 + 1 - third_ref[j]]
+
+        @pl.when(slot < 0)
+        def _():
+            held[j, 2] = extra[1 - j]
+
+        @pl.when(slot >= 0)
+        def _():
+            pltpu.make_async_copy(main.at[0], held.at[j, 2], sems.at[j, 2]).wait()
+
+        for at in range(2):
+            pltpu.make_async_copy(edge, held.at[j, at], sems.at[j, at]).wait()
+        pltpu.make_async_copy(qg.at[0], asked.at[j], sems.at[j, 3]).wait()
+        k, v = (
+            jnp.concatenate([extra[j, w], held[j, 0, w], held[j, 1, w], held[j, 2, w]], axis=0)
+            for w in range(2)
+        )
+        q, g = asked[j, 0], asked[j, 1]
+        p_low, ds = attention(q, g, k, v)
         grad_ref[j, 0] = dot(ds[:BLOCK], q, ((1,), (0,))).astype(grad_ref.dtype)
         grad_ref[j, 1] = dot(p_low[:BLOCK], g, ((1,), (0,))).astype(grad_ref.dtype)
 
 
-def collect(request, third, near, kv, qg, edge, cross, main, thirds):
-    lanes, slots = len(thirds), main.shape[0]
-    return call(
-        functools.partial(collect_kernel, lanes, slots),
-        (
-            jax.ShapeDtypeStruct((slots + 1,) + kv.shape[1:], kv.dtype),
-            jax.ShapeDtypeStruct(cross.shape, cross.dtype),
-        ),
-        [SMEM] * 3 + [VMEM] * (5 + lanes),
+def collect(slot, third, near, kv, qg, edge, cross, main, thirds):
+    lanes = len(thirds)
+    pair = jax.ShapeDtypeStruct(cross.shape, cross.dtype)
+    return call(
+        functools.partial(collect_kernel, lanes),
+        (pair, pair),
+        [SMEM] * 3 + [ANY] * (5 + lanes),
         (VMEM, VMEM),
         "collect",
         5 * 2 * 2 * 4 * BLOCK * BLOCK * HEAD_DIM,
-        4 * main.size,
-    )(request, third, near, kv, qg, edge, cross, main, *thirds)
-
-
-def attend_kernel(blocks, kv_ref, qg_ref, edge_ref, far_ref, out, sum_ref, edge_out, far_out, out_ref, sems):
+        20 * edge.size,
+        [
+            pltpu.VMEM((2, 3) + edge.shape, edge.dtype),
+            pltpu.VMEM((2,) + edge.shape, edge.dtype),
+            pltpu.SemaphoreType.DMA((2, 4)),
+            pltpu.SemaphoreType.DMA((2,)),
+        ],
+    )(slot, third, near, kv, qg, edge, cross, main, *thirds)
+
+
+def attend_kernel(blocks, slot_ref, third_ref, kv_ref, qg_ref, edge_ref, extra_ref, main, *refs):
+    out, sums, edge_out, main_out = refs[:4]
+    far_ref, out_ref, sum_ref, far_out, far_sems, done_sems, leave_sems = refs[4:]
     bf16 = jnp.bfloat16
 
+    def arrive(r, slot):
+        return pltpu.make_async_copy(main.at[slot], far_ref.at[r], far_sems.at[r])
+
     def finished(n):
-        return pltpu.make_async_copy(out_ref.at[n], out.at[n], sems.at[n])
+        return pltpu.make_async_copy(out_ref.at[n], out.at[n], done_sems.at[0, n])
+
+    def summed(n):
+        return pltpu.make_async_copy(sum_ref.at[n], sums.at[n], done_sems.at[1, n])
+
+    def leave(r, slot):
+        return pltpu.make_async_copy(far_out.at[r], main_out.at[slot], leave_sems.at[r])
+
+    def when_main(r, do):
+        @pl.when(slot_ref[r] >= 0)
+        def _():
+            do(r, slot_ref[r])
+
+    def load(r, _):
+        when_main(r, lambda r, slot: arrive(r, slot).start())
+
+    lax.fori_loop(0, 2 * blocks, load, None)
+    for j in range(2):
+        far_ref[third_ref[j]] = extra_ref[j]
+
+    def ready(n):
+        for r in (2 * n, 2 * n + 1):
+            when_main(r, lambda r, slot: arrive(r, slot).wait())
 
     def one(n, first):
         q, g = qg_ref[n, 0], qg_ref[n, 1]
@@ -285,7 +317,6 @@
         p_low, ds = attention(q, g, k, v)
         out_ref[n, 0] = dot(p_low, v, ((0,), (0,))).astype(bf16)
         out_ref[n, 1] = dot(ds, k, ((0,), (0,))).astype(bf16)
-        finished(n).start()
         dk = dot(ds, q, ((1,), (0,)))
         dv = dot(p_low, g, ((1,), (0,)))
         for which, d in enumerate((dk, dv)):
@@ -297,49 +328,97 @@
             far_out[r2, which] = d[2 * BLOCK : 3 * BLOCK].astype(bf16)
             far_out[r3, which] = d[3 * BLOCK :].astype(bf16)
 
+    def sent(n, first):
+        finished(n).start()
+        if not first:
+            summed(n - 1).start()
+        for r in (2 * n, 2 * n + 1):
+            when_main(r, lambda r, slot: leave(r, slot).start())
+
+    group = 3
+    ready(0)
     one(0, True)
-    lax.fori_loop(1, blocks, lambda n, _: one(n, False), None, unroll=3)
-    wait_all([finished(n) for n in range(blocks)])
-
-
-def attend(kv, qg, edge, far):
+    sent(0, True)
+
+    def several(at, _):
+        first = 1 + at * group
+        for i in range(group):
+            ready(first + i)
+        for i in range(group):
+            one(first + i, False)
+        for i in range(group):
+            sent(first + i, False)
+
+    lax.fori_loop(0, (blocks - 1) // group, several, None)
+    for n in range(1 + (blocks - 1) // group * group, blocks):
+        ready(n)
+        one(n, False)
+        sent(n, False)
+    summed(blocks - 1).start()
+
+    def finish(n, _):
+        finished(n).wait()
+        summed(n).wait()
+        for r in (2 * n, 2 * n + 1):
+            when_main(r, lambda r, slot: leave(r, slot).wait())
+
+    lax.fori_loop(0, blocks, finish, None)
+
+
+def attend(slot, third, kv, qg, edge, extra, main):
     blocks = kv.shape[0]
-    bf16 = kv.dtype
+    bf16, f32 = kv.dtype, jnp.float32
+    far = (2 * blocks,) + kv.shape[1:]
     return call(
         functools.partial(attend_kernel, blocks),
         (
             pltpu.HBM(qg.shape, bf16),
-            jax.ShapeDtypeStruct(kv.shape, jnp.float32),
+            pltpu.HBM(kv.shape, f32),
             jax.ShapeDtypeStruct(edge.shape, bf16),
-            jax.ShapeDtypeStruct((2 * blocks,) + kv.shape[1:], bf16),
+            pltpu.HBM(main.shape, bf16),
         ),
-        [VMEM] * 4,
-        (ANY, VMEM, VMEM, VMEM),
+        [SMEM, SMEM, VMEM, VMEM, VMEM, VMEM, ANY],
+        (ANY, ANY, VMEM, ANY),
         "attend",
         5 * 2 * blocks * 4 * BLOCK * BLOCK * HEAD_DIM,
-        2 * (6 * kv.size + 2 * far.size),
-        [pltpu.VMEM(qg.shape, bf16), pltpu.SemaphoreType.DMA((blocks,))],
-    )(kv, qg, edge, far)
-
-
-def land_kernel(
-    blocks, lanes, slots, main_ref, third_ref, sum_ref, edge_ref, home_ref, *refs
-):
-    thirds, out = refs[:lanes], refs[lanes]
-    total, low, sems = refs[lanes + 1 :]
+        2 * (6 * kv.size + 2 * main.size),
+        [
+            pltpu.VMEM(far, bf16),
+            pltpu.VMEM(qg.shape, bf16),
+            pltpu.VMEM(kv.shape, f32),
+            pltpu.VMEM(far, bf16),
+            pltpu.SemaphoreType.DMA((2 * blocks,)),
+            pltpu.SemaphoreType.DMA((2, blocks)),
+            pltpu.SemaphoreType.DMA((2 * blocks,)),
+        ],
+    )(slot, third, kv, qg, edge, extra, main)
+
+
+def land_kernel(blocks, slots, thirds, main_ref, late_ref, sum_ref, edge_ref, home_ref, late, out, *refs):
+    total, held, low, sems, late_sems = refs
     f32 = jnp.float32
+
+    def arrive(at):
+        return pltpu.make_async_copy(late.at[at], held.at[at], late_sems.at[at])
+
+    def load(at, _):
+        @pl.when(late_ref[at] >= 0)
+        def _():
+            arrive(at).start()
+
+    lax.fori_loop(0, thirds, load, None)
     total[pl.ds(0, blocks)] = sum_ref[...]
     total[blocks - 1] += edge_ref[...].astype(f32)
-    for step in range(lanes):
-        for side in range(2):
-            index = third_ref[2 * step + side]
-
-            @pl.when(index >= 0)
-            def _():
-                total[index] += thirds[step][side].astype(f32)
-
     for slot in range(slots):
         total[main_ref[slot]] += home_ref[slot].astype(f32)
+
+    def add(at, _):
+        @pl.when(late_ref[at] >= 0)
+        def _():
+            arrive(at).wait()
+            total[late_ref[at]] += held[at].astype(f32)
+
+    lax.fori_loop(0, thirds, add, None)
     writes = [pltpu.make_async_copy(low.at[n], out.at[n], sems.at[n]) for n in range(blocks)]
     for n in range(blocks):
         low[n] = total[n].astype(low.dtype)
@@ -347,22 +426,24 @@
     wait_all(writes)
 
 
-def land(main_index, third_index, sums, edge, home, thirds):
-    blocks, lanes, slots = sums.shape[0], len(thirds), home.shape[0]
-    return call(
-        functools.partial(land_kernel, blocks, lanes, slots),
+def land(main_index, late_index, sums, edge, home, late):
+    blocks, slots, thirds = sums.shape[0], home.shape[0], late.shape[0]
+    return call(
+        functools.partial(land_kernel, blocks, slots, thirds),
         pltpu.HBM(sums.shape, home.dtype),
-        [SMEM] * 2 + [VMEM] * (3 + lanes),
+        [SMEM] * 2 + [VMEM] * 3 + [ANY],
         ANY,
         "land",
         sums.size * 2,
         10 * sums.size,
         [
             pltpu.VMEM((blocks + 1,) + sums.shape[1:], jnp.float32),
+            pltpu.VMEM(late.shape, home.dtype),
             pltpu.VMEM(sums.shape, home.dtype),
             pltpu.SemaphoreType.DMA((blocks,)),
+            pltpu.SemaphoreType.DMA((thirds,)),
         ],
-    )(main_index, third_index, sums, edge, home, *thirds)
+    )(main_index, late_index, sums, edge, home, late)
 
 
 def plan(key_lists, blocks, ctx_count, lanes):
@@ -395,28 +476,30 @@
     def row(of, array):
         return jnp.sum(jnp.where(slabs[:, None] == of, array, 0), axis=0)
 
-    my_source, my_rank = row(me, source), row(me, rank)
-    serves = (slabs[:, None, None] == my_source[None, None, :]) & (pair == my_rank[None, None, :])
-    request = jnp.sum(jnp.where(serves, numbers[None, None, :], 0), axis=2)
-    request = jnp.where(slabs[:, None] == me, requests, request).reshape(-1)
-
+    my_slot = row(me, jnp.where(is_third, -1, source * 2 + rank))
     is_jth = (is_third[:, None, :] & (order[:, None, :] == pair)).astype(i32)
     third_source = jnp.sum(is_jth * source[:, None, :], axis=2)
     third_request = jnp.sum(is_jth * numbers, axis=2)
+    third_inside = jnp.sum(is_jth * inside[:, None, :], axis=2)
+    mine = jnp.where(third_source == me, third_inside, -1).reshape(2, lanes, 2)
+    near, far = jnp.where(half == 0, mine[0], mine[1]), jnp.where(half == 0, mine[1], mine[0])
+    late_index = jnp.concatenate([near, far], axis=1).reshape(-1)
 
     def steps(of):
         slab = row(of, third_source)
         return jnp.where(slab // lanes == half, (lane - slab % lanes + lanes) % lanes, -1)
 
     partner = (me + lanes) % ctx_count
-    return main_index, third_index, request, row(me, third_request), steps(me), steps(partner)
+    return (
+        main_index, third_index, late_index, my_slot, row(me, third_request), steps(me), steps(partner)
+    )
 
 
 def body(queries, keys, values, out_grad, key_lists):
     ctx_count = lax.axis_size("ctx")
     blocks = lax.axis_size("head")
     lanes = ctx_count // 2
-    main_index, third_index, request, my_third, near_steps, cross_steps = plan(
+    main_index, third_index, late_index, my_slot, my_third, near_steps, cross_steps = plan(
         key_lists, blocks, ctx_count, lanes
     )
 
@@ -443,22 +526,26 @@
     thirds, edge = pick_third(third_index, kv)
     edge = move(edge, lambda i: (i + 1) % ctx_count)
     thirds = along(thirds, 1)
+    thirds[1], edge = lax.optimization_barrier((thirds[1], edge))
     cross = across(pick_cross(cross_steps, thirds))
-    packed, edge, cross = lax.optimization_barrier((pack(main_index, kv), edge, cross))
+    packed, cross = lax.optimization_barrier((pack(main_index, kv), cross))
     main = ctx_exchange(packed)
-    far, third_grad = collect(request, my_third, near_steps, kv, qg, edge, cross, main, thirds)
+    extra, third_grad = collect(my_slot, my_third, near_steps, kv, qg, edge, cross, main, thirds)
     cross_grad = across(third_grad)
-    out, sums, edge_grad, far_grad = attend(kv, qg, edge, far)
+    out, sums, edge_grad, main_grad = attend(my_slot, my_third, kv, qg, edge, extra, main)
     out, cross_grad = lax.optimization_barrier((out, cross_grad))
+    late = lax.all_gather(
+        jnp.concatenate([third_grad, cross_grad], axis=0),
+        "ctx",
+        axis_index_groups=[list(range(lanes)), list(range(lanes, ctx_count))],
+        tiled=True,
+    )
     out = head_exchange(out)
     edge_grad = move(edge_grad, lambda i: (i - 1) % ctx_count)
-    late = along(pick_back(near_steps, cross_steps, third_grad, cross_grad, lanes), -1)
-    packed, out, edge_grad, late = lax.optimization_barrier(
-        (pack(request, far_grad), out, edge_grad, late)
-    )
-    home = ctx_exchange(packed)
+    main_grad, out, edge_grad, late = lax.optimization_barrier((main_grad, out, edge_grad, late))
+    home = ctx_exchange(main_grad)
     attended, query_grad = join_heads(out)
-    total = land(main_index, third_index, sums, edge_grad, home, late)
+    total = land(main_index, late_index, sums, edge_grad, home, late)
     key_grad, value_grad = join_heads(head_exchange(total))
     return attended, query_grad, key_grad, value_grad
 

time: 290 us -> 306 us (1.055)
  waiting for transfers between devices: 116 us -> 176 us
  blocking collectives: 58.9 us -> 0 us
  between operations: 1.12 us -> 14.3 us
  starting transfers between devices: 69.2 us -> 79.9 us
  Pallas kernels: 38.4 us -> 31.3 us
    all_to_all x1 -> x0, blocking collectives: 58.9 us -> none  [ctx_exchange(): return lax.all_to_all(array, 'ctx', split_axis=0, concat_axis=0, tiled=True)]
    all_to_all x1 -> x2, waiting for transfers between devices: 51.4 us -> 90.1 us  [ctx_exchange(): return lax.all_to_all(array, 'ctx', split_axis=0, concat_axis=0, tiled=True)]
    all_to_all x4, waiting for transfers between devices: 47.8 us -> 71.4 us  [head_exchange(): lax.all_to_all(array, 'head', split_axis=0, concat_axis=0, tiled=True)]
    all_to_all x4, starting transfers between devices: 29.9 us -> 44.9 us  [head_exchange(): lax.all_to_all(array, 'head', split_axis=0, concat_axis=0, tiled=True)]
    ppermute x18 -> x11, starting transfers between devices: 29.3 us -> 20.5 us  [move(): lax.ppermute(array, 'ctx', [(i, target(i)) for i in range(ctx_count)])]
    all_to_all x1 -> x2, starting transfers between devices: 9.97 us -> 14.5 us  [ctx_exchange(): return lax.all_to_all(array, 'ctx', split_axis=0, concat_axis=0, tiled=True)]
    pallas_call x2 -> x1, Pallas kernels: 5.4 us -> 2.13 us  [pack(): call(functools.partial(pack_kernel, rows, array.shape[0] - 1), pltpu.HBM(...]
    ppermute x18 -> x11, waiting for transfers between devices: 16.9 us -> 14.1 us  [move(): lax.ppermute(array, 'ctx', [(i, target(i)) for i in range(ctx_count)])]
  transfers between devices with their start and end apart: 23 -> 18, of which waited for: 12 -> 10; matrix products, arithmetic and copies ran while one was open for 1% -> 1% of each run, Pallas kernels for 9% -> 7%
where the time goes in v1:
time: 306 us; the launch traced here: 305 us
  waiting for transfers between devices  176 us (58%)
  starting transfers between devices  79.9 us (26%)
  Pallas kernels  31.3 us (10%)
  between operations  14.3 us (5%)
    all_to_all x2, waiting for transfers between devices, ctx_exchange(): return lax.all_to_all(array, 'ctx', split_axis=0, concat_axis=0, tiled=True)  90.1 us
    all_to_all x4, waiting for transfers between devices, head_exchange(): lax.all_to_all(array, 'head', split_axis=0, concat_axis=0, tiled=True)  71.4 us
    all_to_all x4, starting transfers between devices, head_exchange(): lax.all_to_all(array, 'head', split_axis=0, concat_axis=0, tiled=True)  44.9 us
    ppermute x11, starting transfers between devices, move(): lax.ppermute(array, 'ctx', [(i, target(i)) for i in range(ctx_count)])  20.5 us
    all_to_all x2, starting transfers between devices, ctx_exchange(): return lax.all_to_all(array, 'ctx', split_axis=0, concat_axis=0, tiled=True)  14.5 us
    ppermute x11, waiting for transfers between devices, move(): lax.ppermute(array, 'ctx', [(i, target(i)) for i in range(ctx_count)])  14.1 us
    pallas_call x1, Pallas kernels, attend(): call(functools.partial(attend_kernel, blocks), (pltpu.HBM(qg.shape, bf16)...  13.4 us
  transfers between devices with their start and end apart: 18, of which 10 were waited for; matrix products, arithmetic and copies ran while one was open for 1% of the time, Pallas kernels for 7%

profile of v1, /device:TPU:56, one launch (start us, length us, event | category | flops | bytes accessed | tf_op | source)
XLA Modules:
  0.0 305.0 jit_solution(37209360635758674)
XLA Ops:
  7.2 2.4 split_heads.2
  9.6 8.5 %all-to-all-start = ((bf16[16,2,128,128]{3,2,1,0:T(8,128)(2,1)}), bf16[16,2,128,128]{3,2,1,0:T(8,128)(2,1)S(1)}, u32[]{:S(2)}, u32[]{:S(2)}) async-start(bf16[16,2,128,128]{3,2,1,0:T(8,128)(2,1)} %split_heads.2), calls=%async_computation | async-start | bytes 2097152 | tf_op jit(solution)/shard_map/all_to_all | solution.py:507
  19.0 2.4 split_heads.3
  21.6 22.2 %all-to-all-done.kv_ref.in_ref.kv = bf16[16,2,128,128]{3,2,1,0:T(8,128)(2,1)S(1)} async-done(((bf16[16,2,128,128]{3,2,1,0:T(8,128)(2,1)}), bf16[16,2,128,128]{3,2,1,0:T(8,128)(2,1)S(1)}, u32[]{:S(2)}, u32[]{:S(2)}) %all-to-all-start) | async-done | bytes 1048608 | tf_op jit(solution)/shard_map/all_to_all | solution.py:507
  43.8 5.2 %all-to-all-start.1 = ((bf16[16,2,128,128]{3,2,1,0:T(8,128)(2,1)}), bf16[16,2,128,128]{3,2,1,0:T(8,128)(2,1)S(1)}, u32[]{:S(2)}, u32[]{:S(2)}) async-start(bf16[16,2,128,128]{3,2,1,0:T(8,128)(2,1)} %split_heads.3), calls=%async_computation.1 | async-start | bytes 2097152 | tf_op jit(solution)/shard_map/all_to_all | solution.py:507
  54.1 4.9 %collective-permute-start.4 = (bf16[2,2,128,128]{3,2,1,0:T(8,128)(2,1)S(1)}, bf16[2,2,128,128]{3,2,1,0:T(8,128)(2,1)S(1)}, u32[]{:S(2)}, u32[]{:S(2)}) collective-permute-start(bf16[2,2,128,128]{3,2,1,0:T(8,128)(2,1)S(1)} %get-tuple-element.40), channel_id=1, source_target_pairs={{0,64},{16,80},{32,96},{48,112},{64,0},{80,16},{96,32},{112,48},{1... | collective-permute-start | bytes 393224 | tf_op jit(solution)/shard_map/ppermute | solution.py:513
  60.3 9.4 %collective-permute-start.7 = (bf16[2,2,128,128]{3,2,1,0:T(8,128)(2,1)S(1)}, bf16[2,2,128,128]{3,2,1,0:T(8,128)(2,1)S(1)}, u32[]{:S(2)}, u32[]{:S(2)}) collective-permute-start(bf16[2,2,128,128]{3,2,1,0:T(8,128)(2,1)S(1)} %get-tuple-element.43), channel_id=1, source_target_pairs={{0,112},{16,0},{32,16},{48,32},{64,48},{80,64},{96,80},{112,96},{1... | collective-permute-start | bytes 393224 | tf_op jit(solution)/shard_map/ppermute | solution.py:513
  69.7 2.0 collective-permute-done.6.refs_6_
  72.9 1.7 collective-permute-start.8
  74.7 2.1 pack.1
  76.9 6.4 %collective-permute-done.8.cross = bf16[2,2,128,128]{3,2,1,0:T(8,128)(2,1)S(1)} collective-permute-done((bf16[2,2,128,128]{3,2,1,0:T(8,128)(2,1)S(1)}, bf16[2,2,128,128]{3,2,1,0:T(8,128)(2,1)S(1)}, u32[]{:S(2)}, u32[]{:S(2)}) %collective-permute-start.8) | collective-permute-done | bytes 131104 | tf_op jit(solution)/shard_map/ppermute | solution.py:513
  83.3 6.0 %all-to-all-start.2 = ((bf16[32,2,128,128]{3,2,1,0:T(8,128)(2,1)}), bf16[32,2,128,128]{3,2,1,0:T(8,128)(2,1)}, u32[]{:S(2)}, u32[]{:S(2)}) async-start(bf16[32,2,128,128]{3,2,1,0:T(8,128)(2,1)} %pack.1), calls=%async_computation.2 | async-start | bytes 4194304 | tf_op jit(solution)/shard_map/all_to_all | solution.py:510
  89.4 35.1 %all-to-all-done.2.main = bf16[32,2,128,128]{3,2,1,0:T(8,128)(2,1)} async-done(((bf16[32,2,128,128]{3,2,1,0:T(8,128)(2,1)}), bf16[32,2,128,128]{3,2,1,0:T(8,128)(2,1)}, u32[]{:S(2)}, u32[]{:S(2)}) %all-to-all-start.2) | async-done | bytes 2097184 | tf_op jit(solution)/shard_map/all_to_all | solution.py:510
  124.5 3.2 %collect.1 = (bf16[2,2,128,128]{3,2,1,0:T(8,128)(2,1)S(1)}, bf16[2,2,128,128]{3,2,1,0:T(8,128)(2,1)S(1)}) custom-call(s32[32]{0:T(128)S(1)} %select_reduce_fusion.5.slot_ref, s32[2]{0:T(128)S(1)} %get-tuple-element.68.third_ref, s32[2]{0:T(128)S(1)} %compare_select_fusion.8.near_ref, bf16[16,2,128,128]{3,2,1,0:T(8,128)(2,1)S(1)} %all-to-all-done.kv_ref.in_ref.kv, ...), custom_call_target="tpu_custom_call" | custom-call | flops 167772160 | bytes 655360 | tf_op jit(solution)/shard_map/collect/pallas_call | solution.py:257
  128.0 13.4 %attend.1 = (bf16[16,2,128,128]{3,2,1,0:T(8,128)(2,1)}, f32[16,2,128,128]{3,2,1,0:T(8,128)}, bf16[2,128,128]{2,1,0:T(8,128)(2,1)S(1)}, bf16[32,2,128,128]{3,2,1,0:T(8,128)(2,1)}) custom-call(s32[32]{0:T(128)S(1)} %select_reduce_fusion.5.slot_ref, s32[2]{0:T(128)S(1)} %get-tuple-element.68.third_ref, ...), custom_call_target="tpu_custom_call" | custom-call | flops 1342177280 | bytes 10485760 | tf_op jit(solution)/shard_map/attend/pallas_call | solution.py:372
  141.3 3.3 %collective-permute-done.9 = bf16[2,2,128,128]{3,2,1,0:T(8,128)(2,1)S(1)} collective-permute-done((bf16[2,2,128,128]{3,2,1,0:T(8,128)(2,1)S(1)}, bf16[2,2,128,128]{3,2,1,0:T(8,128)(2,1)S(1)}, u32[]{:S(2)}, u32[]{:S(2)}) %collective-permute-start.9) | collective-permute-done | bytes 131104 | tf_op jit(solution)/shard_map/ppermute | solution.py:513
  145.4 26.7 %all-to-all-start.3 = ((bf16[16,2,128,128]{3,2,1,0:T(8,128)(2,1)}), bf16[16,2,128,128]{3,2,1,0:T(8,128)(2,1)S(1)}, u32[]{:S(2)}, u32[]{:S(2)}) async-start(bf16[16,2,128,128]{3,2,1,0:T(8,128)(2,1)} %get-tuple-element.50), calls=%async_computation.3 | async-start | bytes 2097152 | tf_op jit(solution)/shard_map/all_to_all | solution.py:507
  172.1 1.9 collective-permute-done.10.edge_ref
  174.0 24.3 %all-to-all-done.3.in_ref = bf16[16,2,128,128]{3,2,1,0:T(8,128)(2,1)S(1)} async-done(((bf16[16,2,128,128]{3,2,1,0:T(8,128)(2,1)}), bf16[16,2,128,128]{3,2,1,0:T(8,128)(2,1)S(1)}, u32[]{:S(2)}, u32[]{:S(2)}) %all-to-all-start.3) | async-done | bytes 1048608 | tf_op jit(solution)/shard_map/all_to_all | solution.py:507
  198.3 8.5 %all-to-all-start.4 = ((bf16[32,2,128,128]{3,2,1,0:T(8,128)(2,1)}), bf16[32,2,128,128]{3,2,1,0:T(8,128)(2,1)}, u32[]{:S(2)}, u32[]{:S(2)}) async-start(bf16[32,2,128,128]{3,2,1,0:T(8,128)(2,1)} %get-tuple-element.58), calls=%async_computation.4 | async-start | bytes 4194304 | tf_op jit(solution)/shard_map/all_to_all | solution.py:510
  207.0 55.0 %all-to-all-done.4.home_ref = bf16[32,2,128,128]{3,2,1,0:T(8,128)(2,1)} async-done(((bf16[32,2,128,128]{3,2,1,0:T(8,128)(2,1)}), bf16[32,2,128,128]{3,2,1,0:T(8,128)(2,1)}, u32[]{:S(2)}, u32[]{:S(2)}) %all-to-all-start.4) | async-done | bytes 2097184 | tf_op jit(solution)/shard_map/all_to_all | solution.py:510
  262.1 4.3 %land.1 = bf16[16,2,128,128]{3,2,1,0:T(8,128)(2,1)} custom-call(s32[32]{0:T(128)S(1)} %select_n.175.index_ref.main_ref, s32[32]{0:T(128)S(1)} %reshape.209.late_ref, f32[16,2,128,128]{3,2,1,0:T(8,128)S(1)} %copy-done, bf16[2,128,128]{2,1,0:T(8,128)(2,1)S(1)} %collective-permute-done.10.edge_ref, bf16[32,2,128,128]{3,2,1,0:T(8,128)(2,1)} %all-to-all-done.4.home_ref, ...), custom_call_target="tpu_custom_call" | custom-call | flops 1048576 | bytes 5242880 | tf_op jit(solution)/shard_map/land/pallas_call | solution.py:431
  266.4 4.6 %all-to-all-start.5 = ((bf16[16,2,128,128]{3,2,1,0:T(8,128)(2,1)}), bf16[16,2,128,128]{3,2,1,0:T(8,128)(2,1)S(1)}, u32[]{:S(2)}, u32[]{:S(2)}) async-start(bf16[16,2,128,128]{3,2,1,0:T(8,128)(2,1)} %land.1), calls=%async_computation.5 | async-start | bytes 2097152 | tf_op jit(solution)/shard_map/all_to_all | solution.py:507
  272.1 24.9 %all-to-all-done.5.in_ref = bf16[16,2,128,128]{3,2,1,0:T(8,128)(2,1)S(1)} async-done(((bf16[16,2,128,128]{3,2,1,0:T(8,128)(2,1)}), bf16[16,2,128,128]{3,2,1,0:T(8,128)(2,1)S(1)}, u32[]{:S(2)}, u32[]{:S(2)}) %all-to-all-start.5) | async-done | bytes 1048608 | tf_op jit(solution)/shard_map/all_to_all | solution.py:507
  (61 shorter events, 12.4 us)
Async XLA Ops:
  7.2 10.9 %copy-start.1 = (s32[256,4]{0,1:T(4,128)S(1)}, s32[256,4]{0,1:T(4,128)}, u32[]{:S(2)}) copy-start(s32[256,4]{0,1:T(4,128)} %param.9) | copy-start | bytes 12292
  9.6 34.2 %all-to-all-start = ((bf16[16,2,128,128]{3,2,1,0:T(8,128)(2,1)}), bf16[16,2,128,128]{3,2,1,0:T(8,128)(2,1)S(1)}, u32[]{:S(2)}, u32[]{:S(2)}) async-start(bf16[16,2,128,128]{3,2,1,0:T(8,128)(2,1)} %split_heads.2), calls=%async_computation | async-start | bytes 2097152 | tf_op jit(solution)/shard_map/all_to_all | solution.py:507
  43.8 39.5 %all-to-all-start.1 = ((bf16[16,2,128,128]{3,2,1,0:T(8,128)(2,1)}), bf16[16,2,128,128]{3,2,1,0:T(8,128)(2,1)S(1)}, u32[]{:S(2)}, u32[]{:S(2)}) async-start(bf16[16,2,128,128]{3,2,1,0:T(8,128)(2,1)} %split_heads.3), calls=%async_computation.1 | async-start | bytes 2097152 | tf_op jit(solution)/shard_map/all_to_all | solution.py:507
  51.0 8.0 %collective-permute-start = (bf16[2,2,128,128]{3,2,1,0:T(8,128)(2,1)S(1)}, bf16[2,2,128,128]{3,2,1,0:T(8,128)(2,1)S(1)}, u32[]{:S(2)}, u32[]{:S(2)}) collective-permute-start(bf16[2,2,128,128]{3,2,1,0:T(8,128)(2,1)S(1)} %get-tuple-element.33), channel_id=1, source_target_pairs={{0,16},{16,32},{32,48},{48,64},{64,80},{80,96},{96,112},{112,0},{1... | collective-permute-start | bytes 393224 | tf_op jit(solution)/shard_map/ppermute | solution.py:513
  51.0 8.0 %collective-permute-start.1 = (bf16[2,128,128]{2,1,0:T(8,128)(2,1)S(1)}, bf16[2,128,128]{2,1,0:T(8,128)(2,1)S(1)}, u32[]{:S(2)}, u32[]{:S(2)}) collective-permute-start(bf16[2,128,128]{2,1,0:T(8,128)(2,1)S(1)} %get-tuple-element.34), channel_id=1, source_target_pairs={{0,16},{16,32},{32,48},{48,64},{64,80},{80,96},{96,112},{112,128},... | collective-permute-start | bytes 196616 | tf_op jit(solution)/shard_map/ppermute | solution.py:513
  51.3 9.0 %collective-permute-start.2 = (bf16[2,2,128,128]{3,2,1,0:T(8,128)(2,1)S(1)}, bf16[2,2,128,128]{3,2,1,0:T(8,128)(2,1)S(1)}, u32[]{:S(2)}, u32[]{:S(2)}) collective-permute-start(bf16[2,2,128,128]{3,2,1,0:T(8,128)(2,1)S(1)} %get-tuple-element.38), channel_id=1, source_target_pairs={{0,32},{16,48},{32,64},{48,80},{64,96},{80,112},{96,0},{112,16},{1... | collective-permute-start | bytes 393224 | tf_op jit(solution)/shard_map/ppermute | solution.py:513
  53.1 16.6 %collective-permute-start.3 = (bf16[2,2,128,128]{3,2,1,0:T(8,128)(2,1)S(1)}, bf16[2,2,128,128]{3,2,1,0:T(8,128)(2,1)S(1)}, u32[]{:S(2)}, u32[]{:S(2)}) collective-permute-start(bf16[2,2,128,128]{3,2,1,0:T(8,128)(2,1)S(1)} %get-tuple-element.39), channel_id=1, source_target_pairs={{0,48},{16,64},{32,80},{48,96},{64,112},{80,0},{96,16},{112,32},{1... | collective-permute-start | bytes 393224 | tf_op jit(solution)/shard_map/ppermute | solution.py:513
  54.1 15.6 %collective-permute-start.4 = (bf16[2,2,128,128]{3,2,1,0:T(8,128)(2,1)S(1)}, bf16[2,2,128,128]{3,2,1,0:T(8,128)(2,1)S(1)}, u32[]{:S(2)}, u32[]{:S(2)}) collective-permute-start(bf16[2,2,128,128]{3,2,1,0:T(8,128)(2,1)S(1)} %get-tuple-element.40), channel_id=1, source_target_pairs={{0,64},{16,80},{32,96},{48,112},{64,0},{80,16},{96,32},{112,48},{1... | collective-permute-start | bytes 393224 | tf_op jit(solution)/shard_map/ppermute | solution.py:513
  59.0 10.7 %collective-permute-start.5 = (bf16[2,2,128,128]{3,2,1,0:T(8,128)(2,1)S(1)}, bf16[2,2,128,128]{3,2,1,0:T(8,128)(2,1)S(1)}, u32[]{:S(2)}, u32[]{:S(2)}) collective-permute-start(bf16[2,2,128,128]{3,2,1,0:T(8,128)(2,1)S(1)} %get-tuple-element.41), channel_id=1, source_target_pairs={{0,80},{16,96},{32,112},{48,0},{64,16},{80,32},{96,48},{112,64},{1... | collective-permute-start | bytes 393224 | tf_op jit(solution)/shard_map/ppermute | solution.py:513
  59.0 12.7 %collective-permute-start.6 = (bf16[2,2,128,128]{3,2,1,0:T(8,128)(2,1)S(1)}, bf16[2,2,128,128]{3,2,1,0:T(8,128)(2,1)S(1)}, u32[]{:S(2)}, u32[]{:S(2)}) collective-permute-start(bf16[2,2,128,128]{3,2,1,0:T(8,128)(2,1)S(1)} %get-tuple-element.42), channel_id=1, source_target_pairs={{0,96},{16,112},{32,0},{48,16},{64,32},{80,48},{96,64},{112,80},{1... | collective-permute-start | bytes 393224 | tf_op jit(solution)/shard_map/ppermute | solution.py:513
  60.3 11.9 %collective-permute-start.7 = (bf16[2,2,128,128]{3,2,1,0:T(8,128)(2,1)S(1)}, bf16[2,2,128,128]{3,2,1,0:T(8,128)(2,1)S(1)}, u32[]{:S(2)}, u32[]{:S(2)}) collective-permute-start(bf16[2,2,128,128]{3,2,1,0:T(8,128)(2,1)S(1)} %get-tuple-element.43), channel_id=1, source_target_pairs={{0,112},{16,0},{32,16},{48,32},{64,48},{80,64},{96,80},{112,96},{1... | collective-permute-start | bytes 393224 | tf_op jit(solution)/shard_map/ppermute | solution.py:513
  72.9 10.4 %collective-permute-start.8 = (bf16[2,2,128,128]{3,2,1,0:T(8,128)(2,1)S(1)}, bf16[2,2,128,128]{3,2,1,0:T(8,128)(2,1)S(1)}, u32[]{:S(2)}, u32[]{:S(2)}) collective-permute-start(bf16[2,2,128,128]{3,2,1,0:T(8,128)(2,1)S(1)} %pick_cross.1), channel_id=1, source_target_pairs={{0,128},{16,144},{32,160},{48,176},{64,192},{80,208},{96,224},{112... | collective-permute-start | bytes 393224 | tf_op jit(solution)/shard_map/ppermute | solution.py:513
  83.3 41.2 %all-to-all-start.2 = ((bf16[32,2,128,128]{3,2,1,0:T(8,128)(2,1)}), bf16[32,2,128,128]{3,2,1,0:T(8,128)(2,1)}, u32[]{:S(2)}, u32[]{:S(2)}) async-start(bf16[32,2,128,128]{3,2,1,0:T(8,128)(2,1)} %pack.1), calls=%async_computation.2 | async-start | bytes 4194304 | tf_op jit(solution)/shard_map/all_to_all | solution.py:510
  89.3 109.0 %all-gather.2.cloned.1.call-start = ((), (), s32[]{:S(2)}) async-start(), calls=%async_computation.6 | async-start | bytes 2359296 | tf_op jit(solution)/shard_map/all_gather | solution.py:537
  127.7 17.0 %collective-permute-start.9 = (bf16[2,2,128,128]{3,2,1,0:T(8,128)(2,1)S(1)}, bf16[2,2,128,128]{3,2,1,0:T(8,128)(2,1)S(1)}, u32[]{:S(2)}, u32[]{:S(2)}) collective-permute-start(bf16[2,2,128,128]{3,2,1,0:T(8,128)(2,1)S(1)} %get-tuple-element.49), channel_id=1, source_target_pairs={{0,128},{16,144},{32,160},{48,176},{64,192},{80,208},{96,224},{112... | collective-permute-start | bytes 393224 | tf_op jit(solution)/shard_map/ppermute | solution.py:513
  145.4 52.9 %all-to-all-start.3 = ((bf16[16,2,128,128]{3,2,1,0:T(8,128)(2,1)}), bf16[16,2,128,128]{3,2,1,0:T(8,128)(2,1)S(1)}, u32[]{:S(2)}, u32[]{:S(2)}) async-start(bf16[16,2,128,128]{3,2,1,0:T(8,128)(2,1)} %get-tuple-element.50), calls=%async_computation.3 | async-start | bytes 2097152 | tf_op jit(solution)/shard_map/all_to_all | solution.py:507
  172.1 1.9 collective-permute-start.10
  198.3 63.8 %copy-start = (f32[16,2,128,128]{3,2,1,0:T(8,128)S(1)}, f32[16,2,128,128]{3,2,1,0:T(8,128)}, u32[]{:S(2)}) copy-start(f32[16,2,128,128]{3,2,1,0:T(8,128)} %get-tuple-element.56.sum_ref) | copy-start | bytes 6291460
  198.3 63.8 %all-to-all-start.4 = ((bf16[32,2,128,128]{3,2,1,0:T(8,128)(2,1)}), bf16[32,2,128,128]{3,2,1,0:T(8,128)(2,1)}, u32[]{:S(2)}, u32[]{:S(2)}) async-start(bf16[32,2,128,128]{3,2,1,0:T(8,128)(2,1)} %get-tuple-element.58), calls=%async_computation.4 | async-start | bytes 4194304 | tf_op jit(solution)/shard_map/all_to_all | solution.py:510
  266.4 30.6 %all-to-all-start.5 = ((bf16[16,2,128,128]{3,2,1,0:T(8,128)(2,1)}), bf16[16,2,128,128]{3,2,1,0:T(8,128)(2,1)S(1)}, u32[]{:S(2)}, u32[]{:S(2)}) async-start(bf16[16,2,128,128]{3,2,1,0:T(8,128)(2,1)} %land.1), calls=%async_computation.5 | async-start | bytes 2097152 | tf_op jit(solution)/shard_map/all_to_all | solution.py:507
Sparse Core Ops, SparseCore 0:
  145.5 46.1 all-gather.1

commit v2 on v0

--- a/solution.py
+++ b/solution.py
@@ -15,7 +15,7 @@
 FULL = 60 * 1024 * 1024
 
 
-def call(kernel, out_shape, ins, outs, name, flops, nbytes, scratch=(), limit=52 * 1024 * 1024):
+def call(kernel, out_shape, ins, outs, name, flops, nbytes, scratch=(), limit=51 * 1024 * 1024):
     return pl.pallas_call(
         kernel,
         out_shape=out_shape,
@@ -216,61 +216,50 @@
     return p_low, (p * (dp - delta) * scale).astype(jnp.bfloat16)
 
 
-def collect_kernel(lanes, slots, request_ref, third_ref, near_ref, kv_ref, qg_ref, edge_ref, cross_ref, main_ref, *refs):
+def attend_kernel(
+    blocks, lanes, slot_ref, third_ref, near_ref, kv_ref, qg_ref, edge_ref, cross, main, *refs
+):
     thirds = refs[:lanes]
-    far_ref, grad_ref = refs[lanes:]
-    for slot in range(slots):
-        far_ref[request_ref[slot]] = main_ref[slot]
+    out, sums, edge_out, main_out, third_out = refs[lanes : lanes + 5]
+    far_ref, out_ref, sum_ref, far_out, far_sems, done_sems, leave_sems = refs[lanes + 5 :]
+    bf16 = jnp.bfloat16
+
+    def arrive(r, slot):
+        return pltpu.make_async_copy(main.at[slot], far_ref.at[r], far_sems.at[r])
+
+    def finished(n):
+        return pltpu.make_async_copy(out_ref.at[n], out.at[n], done_sems.at[0, n])
+
+    def summed(n):
+        return pltpu.make_async_copy(sum_ref.at[n], sums.at[n], done_sems.at[1, n])
+
+    def leave(r, slot):
+        return pltpu.make_async_copy(far_out.at[r], main_out.at[slot], leave_sems.at[r])
+
+    def when_main(r, do):
+        @pl.when(slot_ref[r] >= 0)
+        def _():
+            do(r, slot_ref[r])
+
+    def load(r, _):
+        when_main(r, lambda r, slot: arrive(r, slot).start())
+
+    lax.fori_loop(0, 2 * blocks, load, None)
     for j in range(2):
+        r = third_ref[j]
         for step in range(1, lanes):
 
             @pl.when(near_ref[j] == step)
             def _():
-                far_ref[third_ref[j]] = thirds[step][0]
+                pltpu.make_async_copy(thirds[step].at[0], far_ref.at[r], far_sems.at[r]).start()
 
         @pl.when(near_ref[j] < 0)
         def _():
-            far_ref[third_ref[j]] = cross_ref[j]
-
-    for j in range(2):
-        r = third_ref[j]
-        n = r // 2
-        other = n * 4 + 1 - r
-        listed = []
-        for which in range(2):
-            before = jnp.where(n == 0, edge_ref[which], kv_ref[jnp.maximum(n - 1, 0), which])
-            listed.append(
-                jnp.concatenate(
-                    [far_ref[r, which], kv_ref[n, which], before, far_ref[other, which]], axis=0
-                )
-            )
-        q, g = qg_ref[n, 0], qg_ref[n, 1]
-        p_low, ds = attention(q, g, *listed)
-        grad_ref[j, 0] = dot(ds[:BLOCK], q, ((1,), (0,))).astype(grad_ref.dtype)
-        grad_ref[j, 1] = dot(p_low[:BLOCK], g, ((1,), (0,))).astype(grad_ref.dtype)
-
-
-def collect(request, third, near, kv, qg, edge, cross, main, thirds):
-    lanes, slots = len(thirds), main.shape[0]
-    return call(
-        functools.partial(collect_kernel, lanes, slots),
-        (
-            jax.ShapeDtypeStruct((slots + 1,) + kv.shape[1:], kv.dtype),
-            jax.ShapeDtypeStruct(cross.shape, cross.dtype),
-        ),
-        [SMEM] * 3 + [VMEM] * (5 + lanes),
-        (VMEM, VMEM),
-        "collect",
-        5 * 2 * 2 * 4 * BLOCK * BLOCK * HEAD_DIM,
-        4 * main.size,
-    )(request, third, near, kv, qg, edge, cross, main, *thirds)
-
-
-def attend_kernel(blocks, kv_ref, qg_ref, edge_ref, far_ref, out, sum_ref, edge_out, far_out, out_ref, sems):
-    bf16 = jnp.bfloat16
-
-    def finished(n):
-        return pltpu.make_async_copy(out_ref.at[n], out.at[n], sems.at[n])
+            pltpu.make_async_copy(cross.at[j], far_ref.at[r], far_sems.at[r]).start()
+
+    def ready(n):
+        for r in (2 * n, 2 * n + 1):
+            arrive(r, 0).wait()
 
     def one(n, first):
         q, g = qg_ref[n, 0], qg_ref[n, 1]
@@ -285,7 +274,6 @@
         p_low, ds = attention(q, g, k, v)
         out_ref[n, 0] = dot(p_low, v, ((0,), (0,))).astype(bf16)
         out_ref[n, 1] = dot(ds, k, ((0,), (0,))).astype(bf16)
-        finished(n).start()
         dk = dot(ds, q, ((1,), (0,)))
         dv = dot(p_low, g, ((1,), (0,)))
         for which, d in enumerate((dk, dv)):
@@ -297,29 +285,73 @@
             far_out[r2, which] = d[2 * BLOCK : 3 * BLOCK].astype(bf16)
             far_out[r3, which] = d[3 * BLOCK :].astype(bf16)
 
+    def sent(n, first):
+        finished(n).start()
+        if not first:
+            summed(n - 1).start()
+        for r in (2 * n, 2 * n + 1):
+            when_main(r, lambda r, slot: leave(r, slot).start())
+
+    group = 3
+    ready(0)
     one(0, True)
-    lax.fori_loop(1, blocks, lambda n, _: one(n, False), None, unroll=3)
-    wait_all([finished(n) for n in range(blocks)])
-
-
-def attend(kv, qg, edge, far):
-    blocks = kv.shape[0]
-    bf16 = kv.dtype
-    return call(
-        functools.partial(attend_kernel, blocks),
+    sent(0, True)
+
+    def several(at, _):
+        first = 1 + at * group
+        for i in range(group):
+            ready(first + i)
+        for i in range(group):
+            one(first + i, False)
+        for i in range(group):
+            sent(first + i, False)
+
+    lax.fori_loop(0, (blocks - 1) // group, several, None)
+    for n in range(1 + (blocks - 1) // group * group, blocks):
+        ready(n)
+        one(n, False)
+        sent(n, False)
+    summed(blocks - 1).start()
+    for j in range(2):
+        third_out[j] = far_out[third_ref[j]]
+
+    def finish(n, _):
+        finished(n).wait()
+        summed(n).wait()
+        for r in (2 * n, 2 * n + 1):
+            when_main(r, lambda r, slot: leave(r, slot).wait())
+
+    lax.fori_loop(0, blocks, finish, None)
+
+
+def attend(slot, third, near, kv, qg, edge, cross, main, thirds):
+    blocks, lanes = kv.shape[0], len(thirds)
+    bf16, f32 = kv.dtype, jnp.float32
+    far = (2 * blocks,) + kv.shape[1:]
+    return call(
+        functools.partial(attend_kernel, blocks, lanes),
         (
             pltpu.HBM(qg.shape, bf16),
-            jax.ShapeDtypeStruct(kv.shape, jnp.float32),
+            pltpu.HBM(kv.shape, f32),
             jax.ShapeDtypeStruct(edge.shape, bf16),
-            jax.ShapeDtypeStruct((2 * blocks,) + kv.shape[1:], bf16),
+            pltpu.HBM(main.shape, bf16),
+            jax.ShapeDtypeStruct(cross.shape, bf16),
         ),
-        [VMEM] * 4,
-        (ANY, VMEM, VMEM, VMEM),
+        [SMEM] * 3 + [VMEM] * 3 + [ANY] * (2 + lanes),
+        (ANY, ANY, VMEM, ANY, VMEM),
         "attend",
         5 * 2 * blocks * 4 * BLOCK * BLOCK * HEAD_DIM,
-        2 * (6 * kv.size + 2 * far.size),
-        [pltpu.VMEM(qg.shape, bf16), pltpu.SemaphoreType.DMA((blocks,))],
-    )(kv, qg, edge, far)
+        2 * (6 * kv.size + 2 * main.size),
+        [
+            pltpu.VMEM(far, bf16),
+            pltpu.VMEM(qg.shape, bf16),
+            pltpu.VMEM(kv.shape, f32),
+            pltpu.VMEM(far, bf16),
+            pltpu.SemaphoreType.DMA((2 * blocks,)),
+            pltpu.SemaphoreType.DMA((2, blocks)),
+            pltpu.SemaphoreType.DMA((2 * blocks,)),
+        ],
+    )(slot, third, near, kv, qg, edge, cross, main, *thirds)
 
 
 def land_kernel(
@@ -395,11 +427,7 @@
     def row(of, array):
         return jnp.sum(jnp.where(slabs[:, None] == of, array, 0), axis=0)
 
-    my_source, my_rank = row(me, source), row(me, rank)
-    serves = (slabs[:, None, None] == my_source[None, None, :]) & (pair == my_rank[None, None, :])
-    request = jnp.sum(jnp.where(serves, numbers[None, None, :], 0), axis=2)
-    request = jnp.where(slabs[:, None] == me, requests, request).reshape(-1)
-
+    my_slot = row(me, jnp.where(is_third, -1, source * 2 + rank))
     is_jth = (is_third[:, None, :] & (order[:, None, :] == pair)).astype(i32)
     third_source = jnp.sum(is_jth * source[:, None, :], axis=2)
     third_request = jnp.sum(is_jth * numbers, axis=2)
@@ -409,14 +437,14 @@
         return jnp.where(slab // lanes == half, (lane - slab % lanes + lanes) % lanes, -1)
 
     partner = (me + lanes) % ctx_count
-    return main_index, third_index, request, row(me, third_request), steps(me), steps(partner)
+    return main_index, third_index, my_slot, row(me, third_request), steps(me), steps(partner)
 
 
 def body(queries, keys, values, out_grad, key_lists):
     ctx_count = lax.axis_size("ctx")
     blocks = lax.axis_size("head")
     lanes = ctx_count // 2
-    main_index, third_index, request, my_third, near_steps, cross_steps = plan(
+    main_index, third_index, my_slot, my_third, near_steps, cross_steps = plan(
         key_lists, blocks, ctx_count, lanes
     )
 
@@ -443,20 +471,21 @@
     thirds, edge = pick_third(third_index, kv)
     edge = move(edge, lambda i: (i + 1) % ctx_count)
     thirds = along(thirds, 1)
+    thirds[1], packed = lax.optimization_barrier((thirds[1], pack(main_index, kv)))
     cross = across(pick_cross(cross_steps, thirds))
-    packed, edge, cross = lax.optimization_barrier((pack(main_index, kv), edge, cross))
+    packed, edge, cross = lax.optimization_barrier((packed, edge, cross))
     main = ctx_exchange(packed)
-    far, third_grad = collect(request, my_third, near_steps, kv, qg, edge, cross, main, thirds)
+    out, sums, edge_grad, main_grad, third_grad = attend(
+        my_slot, my_third, near_steps, kv, qg, edge, cross, main, thirds
+    )
+    out = head_exchange(out)
     cross_grad = across(third_grad)
-    out, sums, edge_grad, far_grad = attend(kv, qg, edge, far)
-    out, cross_grad = lax.optimization_barrier((out, cross_grad))
-    out = head_exchange(out)
     edge_grad = move(edge_grad, lambda i: (i - 1) % ctx_count)
+    main_grad, out, cross_grad, edge_grad = lax.optimization_barrier(
+        (main_grad, out, cross_grad, edge_grad)
+    )
+    home = ctx_exchange(main_grad)
     late = along(pick_back(near_steps, cross_steps, third_grad, cross_grad, lanes), -1)
-    packed, out, edge_grad, late = lax.optimization_barrier(
-        (pack(request, far_grad), out, edge_grad, late)
-    )
-    home = ctx_exchange(packed)
     attended, query_grad = join_heads(out)
     total = land(main_index, third_index, sums, edge_grad, home, late)
     key_grad, value_grad = join_heads(head_exchange(total))

time: 290 us -> 286 us (0.986)
  waiting for transfers between devices: 116 us -> 185 us
  blocking collectives: 58.9 us -> 0 us
  Pallas kernels: 38.4 us -> 29.2 us
    all_to_all x1 -> x0, blocking collectives: 58.9 us -> none  [ctx_exchange(): return lax.all_to_all(array, 'ctx', split_axis=0, concat_axis=0, tiled=True)]
    ppermute x18, waiting for transfers between devices: 16.9 us -> 45.9 us  [move(): lax.ppermute(array, 'ctx', [(i, target(i)) for i in range(ctx_count)])]
    all_to_all x1 -> x2, waiting for transfers between devices: 51.4 us -> 78.6 us  [ctx_exchange(): return lax.all_to_all(array, 'ctx', split_axis=0, concat_axis=0, tiled=True)]
    all_to_all x4, waiting for transfers between devices: 47.8 us -> 60.5 us  [head_exchange(): lax.all_to_all(array, 'head', split_axis=0, concat_axis=0, tiled=True)]
    all_to_all x1 -> x2, starting transfers between devices: 9.97 us -> 18.5 us  [ctx_exchange(): return lax.all_to_all(array, 'ctx', split_axis=0, concat_axis=0, tiled=True)]
    ppermute x18, starting transfers between devices: 29.3 us -> 21.6 us  [move(): lax.ppermute(array, 'ctx', [(i, target(i)) for i in range(ctx_count)])]
    pallas_call x2 -> x1, Pallas kernels: 19.2 us -> 14 us  [attend(): call(functools.partial(attend_kernel, blocks, lanes), (pltpu.HBM(qg.shape...]
    pallas_call x2 -> x1, Pallas kernels: 5.4 us -> 2.16 us  [pack(): call(functools.partial(pack_kernel, rows, array.shape[0] - 1), pltpu.HBM(...]
  transfers between devices with their start and end apart: 23 -> 24, of which waited for: 12 -> 17; matrix products, arithmetic and copies ran while one was open for 1% -> 1% of each run, Pallas kernels for 9% -> 3%
where the time goes in v2:
time: 286 us; the launch traced here: 285 us
  waiting for transfers between devices  185 us (65%)
  starting transfers between devices  67 us (23%)
  Pallas kernels  29.2 us (10%)
    all_to_all x2, waiting for transfers between devices, ctx_exchange(): return lax.all_to_all(array, 'ctx', split_axis=0, concat_axis=0, tiled=True)  78.6 us
    all_to_all x4, waiting for transfers between devices, head_exchange(): lax.all_to_all(array, 'head', split_axis=0, concat_axis=0, tiled=True)  60.5 us
    ppermute x18, waiting for transfers between devices, move(): lax.ppermute(array, 'ctx', [(i, target(i)) for i in range(ctx_count)])  45.9 us
    all_to_all x4, starting transfers between devices, head_exchange(): lax.all_to_all(array, 'head', split_axis=0, concat_axis=0, tiled=True)  27 us
    ppermute x18, starting transfers between devices, move(): lax.ppermute(array, 'ctx', [(i, target(i)) for i in range(ctx_count)])  21.6 us
    all_to_all x2, starting transfers between devices, ctx_exchange(): return lax.all_to_all(array, 'ctx', split_axis=0, concat_axis=0, tiled=True)  18.5 us
    pallas_call x1, Pallas kernels, attend(): call(functools.partial(attend_kernel, blocks, lanes), (pltpu.HBM(qg.shape...  14 us
  transfers between devices with their start and end apart: 24, of which 17 were waited for; matrix products, arithmetic and copies ran while one was open for 1% of the time, Pallas kernels for 3%

profile of v2, /device:TPU:56, one launch (start us, length us, event | category | flops | bytes accessed | tf_op | source)
XLA Modules:
  0.0 285.0 jit_solution(9017922582491378591)
XLA Ops:
  0.6 2.3 split_heads.2
  3.0 8.5 %all-to-all-start = ((bf16[16,2,128,128]{3,2,1,0:T(8,128)(2,1)}), bf16[16,2,128,128]{3,2,1,0:T(8,128)(2,1)S(1)}, u32[]{:S(2)}, u32[]{:S(2)}) async-start(bf16[16,2,128,128]{3,2,1,0:T(8,128)(2,1)} %split_heads.2), calls=%async_computation | async-start | bytes 2097152 | tf_op jit(solution)/shard_map/all_to_all | solution.py:452
  12.4 2.4 split_heads.3
  15.0 22.2 %all-to-all-done.kv_ref.in_ref = bf16[16,2,128,128]{3,2,1,0:T(8,128)(2,1)S(1)} async-done(((bf16[16,2,128,128]{3,2,1,0:T(8,128)(2,1)}), bf16[16,2,128,128]{3,2,1,0:T(8,128)(2,1)S(1)}, u32[]{:S(2)}, u32[]{:S(2)}) %all-to-all-start) | async-done | bytes 1048608 | tf_op jit(solution)/shard_map/all_to_all | solution.py:452
  37.2 5.2 %all-to-all-start.1 = ((bf16[16,2,128,128]{3,2,1,0:T(8,128)(2,1)}), bf16[16,2,128,128]{3,2,1,0:T(8,128)(2,1)}, u32[]{:S(2)}, u32[]{:S(2)}) async-start(bf16[16,2,128,128]{3,2,1,0:T(8,128)(2,1)} %split_heads.3), calls=%async_computation.1 | async-start | bytes 2097152 | tf_op jit(solution)/shard_map/all_to_all | solution.py:452
  45.0 2.6 collective-permute-start.3
  55.4 2.5 collective-permute-done.5.refs_5_
  60.4 4.6 %collective-permute-start.8 = (bf16[2,2,128,128]{3,2,1,0:T(8,128)(2,1)S(1)}, bf16[2,2,128,128]{3,2,1,0:T(8,128)(2,1)S(1)}, u32[]{:S(2)}, u32[]{:S(2)}) collective-permute-start(bf16[2,2,128,128]{3,2,1,0:T(8,128)(2,1)S(1)} %pick_cross.1), channel_id=1, source_target_pairs={{0,128},{16,144},{32,160},{48,176},{64,192},{80,208},{96,224},{112... | collective-permute-start | bytes 393224 | tf_op jit(solution)/shard_map/ppermute | solution.py:458
  69.7 12.5 %all-to-all-start.2 = ((bf16[32,2,128,128]{3,2,1,0:T(8,128)(2,1)}), bf16[32,2,128,128]{3,2,1,0:T(8,128)(2,1)}, u32[]{:S(2)}, u32[]{:S(2)}) async-start(bf16[32,2,128,128]{3,2,1,0:T(8,128)(2,1)} %pack.1), calls=%async_computation.2 | async-start | bytes 4194304 | tf_op jit(solution)/shard_map/all_to_all | solution.py:455
  82.4 51.1 %all-to-all-done.2.main = bf16[32,2,128,128]{3,2,1,0:T(8,128)(2,1)} async-done(((bf16[32,2,128,128]{3,2,1,0:T(8,128)(2,1)}), bf16[32,2,128,128]{3,2,1,0:T(8,128)(2,1)}, u32[]{:S(2)}, u32[]{:S(2)}) %all-to-all-start.2) | async-done | bytes 2097184 | tf_op jit(solution)/shard_map/all_to_all | solution.py:455
  133.4 14.0 %attend.1 = (bf16[16,2,128,128]{3,2,1,0:T(8,128)(2,1)}, f32[16,2,128,128]{3,2,1,0:T(8,128)}, bf16[2,128,128]{2,1,0:T(8,128)(2,1)S(1)}, bf16[32,2,128,128]{3,2,1,0:T(8,128)(2,1)}, bf16[2,2,128,128]{3,2,1,0:T(8,128)(2,1)S(1)}) custom-call(s32[32]{0:T(128)S(1)} %select_reduce_fusion.4.slot_ref, s32[2]{0:T(128)S(1)} %get-tuple-element.78.third_ref, ...), custom_call_target="tpu_custom_call" | custom-call | flops 1342177280 | bytes 10485760 | tf_op jit(solution)/shard_map/attend/pallas_call | solution.py:331
  147.4 8.9 %all-to-all-start.3 = ((bf16[16,2,128,128]{3,2,1,0:T(8,128)(2,1)}), bf16[16,2,128,128]{3,2,1,0:T(8,128)(2,1)S(1)}, u32[]{:S(2)}, u32[]{:S(2)}) async-start(bf16[16,2,128,128]{3,2,1,0:T(8,128)(2,1)} %get-tuple-element.54), calls=%async_computation.3 | async-start | bytes 2097152 | tf_op jit(solution)/shard_map/all_to_all | solution.py:452
  158.8 15.7 %collective-permute-done.9.crossed = bf16[2,2,128,128]{3,2,1,0:T(8,128)(2,1)S(1)} collective-permute-done((bf16[2,2,128,128]{3,2,1,0:T(8,128)(2,1)S(1)}, bf16[2,2,128,128]{3,2,1,0:T(8,128)(2,1)S(1)}, u32[]{:S(2)}, u32[]{:S(2)}) %collective-permute-start.9) | collective-permute-done | bytes 131104 | tf_op jit(solution)/shard_map/ppermute | solution.py:458
  174.4 13.4 %all-to-all-done.3.in_ref = bf16[16,2,128,128]{3,2,1,0:T(8,128)(2,1)S(1)} async-done(((bf16[16,2,128,128]{3,2,1,0:T(8,128)(2,1)}), bf16[16,2,128,128]{3,2,1,0:T(8,128)(2,1)S(1)}, u32[]{:S(2)}, u32[]{:S(2)}) %all-to-all-start.3) | async-done | bytes 1048608 | tf_op jit(solution)/shard_map/all_to_all | solution.py:452
  187.8 6.0 %all-to-all-start.4 = ((bf16[32,2,128,128]{3,2,1,0:T(8,128)(2,1)}), bf16[32,2,128,128]{3,2,1,0:T(8,128)(2,1)}, u32[]{:S(2)}, u32[]{:S(2)}) async-start(bf16[32,2,128,128]{3,2,1,0:T(8,128)(2,1)} %get-tuple-element.62), calls=%async_computation.4 | async-start | bytes 4194304 | tf_op jit(solution)/shard_map/all_to_all | solution.py:455
  196.2 2.9 %collective-permute-start.14 = (bf16[2,2,128,128]{3,2,1,0:T(8,128)(2,1)S(1)}, bf16[2,2,128,128]{3,2,1,0:T(8,128)(2,1)S(1)}, u32[]{:S(2)}, u32[]{:S(2)}) collective-permute-start(bf16[2,2,128,128]{3,2,1,0:T(8,128)(2,1)S(1)} %get-tuple-element.68), channel_id=1, source_target_pairs={{0,64},{16,80},{32,96},{48,112},{64,0},{80,16},{96,32},{112,48},{1... | collective-permute-start | bytes 393224 | tf_op jit(solution)/shard_map/ppermute | solution.py:458
  201.2 8.1 %collective-permute-done.11.refs_1_ = bf16[2,2,128,128]{3,2,1,0:T(8,128)(2,1)S(1)} collective-permute-done((bf16[2,2,128,128]{3,2,1,0:T(8,128)(2,1)S(1)}, bf16[2,2,128,128]{3,2,1,0:T(8,128)(2,1)S(1)}, u32[]{:S(2)}, u32[]{:S(2)}) %collective-permute-start.11) | collective-permute-done | bytes 131104 | tf_op jit(solution)/shard_map/ppermute | solution.py:458
  209.3 2.9 %collective-permute-done.12.refs_2_ = bf16[2,2,128,128]{3,2,1,0:T(8,128)(2,1)S(1)} collective-permute-done((bf16[2,2,128,128]{3,2,1,0:T(8,128)(2,1)S(1)}, bf16[2,2,128,128]{3,2,1,0:T(8,128)(2,1)S(1)}, u32[]{:S(2)}, u32[]{:S(2)}) %collective-permute-start.12) | collective-permute-done | bytes 131104 | tf_op jit(solution)/shard_map/ppermute | solution.py:458
  212.2 2.6 collective-permute-done.13.refs_3_
  214.8 6.9 %collective-permute-done.14.refs_4_ = bf16[2,2,128,128]{3,2,1,0:T(8,128)(2,1)S(1)} collective-permute-done((bf16[2,2,128,128]{3,2,1,0:T(8,128)(2,1)S(1)}, bf16[2,2,128,128]{3,2,1,0:T(8,128)(2,1)S(1)}, u32[]{:S(2)}, u32[]{:S(2)}) %collective-permute-start.14) | collective-permute-done | bytes 131104 | tf_op jit(solution)/shard_map/ppermute | solution.py:458
  221.8 27.5 %all-to-all-done.4.home_ref = bf16[32,2,128,128]{3,2,1,0:T(8,128)(2,1)} async-done(((bf16[32,2,128,128]{3,2,1,0:T(8,128)(2,1)}), bf16[32,2,128,128]{3,2,1,0:T(8,128)(2,1)}, u32[]{:S(2)}, u32[]{:S(2)}) %all-to-all-start.4) | async-done | bytes 2097184 | tf_op jit(solution)/shard_map/all_to_all | solution.py:455
  249.2 4.0 %land.1 = bf16[16,2,128,128]{3,2,1,0:T(8,128)(2,1)} custom-call(s32[32]{0:T(128)S(1)} %select_n.159.index_ref.main_ref, s32[16]{0:T(128)S(1)} %reshape.200.third_ref, f32[16,2,128,128]{3,2,1,0:T(8,128)} %get-tuple-element.60.sum_ref, bf16[2,128,128]{2,1,0:T(8,128)(2,1)S(1)} %collective-permute-done.10.edge_ref, ...), custom_call_target="tpu_custom_call" | custom-call | flops 1048576 | bytes 5242880 | tf_op jit(solution)/shard_map/land/pallas_call | solution.py:384
  253.3 4.4 %all-to-all-start.5 = ((bf16[16,2,128,128]{3,2,1,0:T(8,128)(2,1)}), bf16[16,2,128,128]{3,2,1,0:T(8,128)(2,1)S(1)}, u32[]{:S(2)}, u32[]{:S(2)}) async-start(bf16[16,2,128,128]{3,2,1,0:T(8,128)(2,1)} %land.1), calls=%async_computation.5 | async-start | bytes 2097152 | tf_op jit(solution)/shard_map/all_to_all | solution.py:452
  258.8 24.9 %all-to-all-done.5.in_ref = bf16[16,2,128,128]{3,2,1,0:T(8,128)(2,1)S(1)} async-done(((bf16[16,2,128,128]{3,2,1,0:T(8,128)(2,1)}), bf16[16,2,128,128]{3,2,1,0:T(8,128)(2,1)S(1)}, u32[]{:S(2)}, u32[]{:S(2)}) %all-to-all-start.5) | async-done | bytes 1048608 | tf_op jit(solution)/shard_map/all_to_all | solution.py:452
  (65 shorter events, 27.9 us)
Async XLA Ops:
  3.0 34.2 %all-to-all-start = ((bf16[16,2,128,128]{3,2,1,0:T(8,128)(2,1)}), bf16[16,2,128,128]{3,2,1,0:T(8,128)(2,1)S(1)}, u32[]{:S(2)}, u32[]{:S(2)}) async-start(bf16[16,2,128,128]{3,2,1,0:T(8,128)(2,1)} %split_heads.2), calls=%async_computation | async-start | bytes 2097152 | tf_op jit(solution)/shard_map/all_to_all | solution.py:452
  37.2 32.5 %all-to-all-start.1 = ((bf16[16,2,128,128]{3,2,1,0:T(8,128)(2,1)}), bf16[16,2,128,128]{3,2,1,0:T(8,128)(2,1)}, u32[]{:S(2)}, u32[]{:S(2)}) async-start(bf16[16,2,128,128]{3,2,1,0:T(8,128)(2,1)} %split_heads.3), calls=%async_computation.1 | async-start | bytes 2097152 | tf_op jit(solution)/shard_map/all_to_all | solution.py:452
  44.4 6.3 %collective-permute-start = (bf16[2,2,128,128]{3,2,1,0:T(8,128)(2,1)S(1)}, bf16[2,2,128,128]{3,2,1,0:T(8,128)(2,1)S(1)}, u32[]{:S(2)}, u32[]{:S(2)}) collective-permute-start(bf16[2,2,128,128]{3,2,1,0:T(8,128)(2,1)S(1)} %get-tuple-element.39), channel_id=1, source_target_pairs={{0,16},{16,32},{32,48},{48,64},{64,80},{80,96},{96,112},{112,0},{1... | collective-permute-start | bytes 393224 | tf_op jit(solution)/shard_map/ppermute | solution.py:458
  44.4 6.4 %collective-permute-start.2 = (bf16[2,2,128,128]{3,2,1,0:T(8,128)(2,1)S(1)}, bf16[2,2,128,128]{3,2,1,0:T(8,128)(2,1)S(1)}, u32[]{:S(2)}, u32[]{:S(2)}) collective-permute-start(bf16[2,2,128,128]{3,2,1,0:T(8,128)(2,1)S(1)} %get-tuple-element.44), channel_id=1, source_target_pairs={{0,32},{16,48},{32,64},{48,80},{64,96},{80,112},{96,0},{112,16},{1... | collective-permute-start | bytes 393224 | tf_op jit(solution)/shard_map/ppermute | solution.py:458
  45.0 10.1 %collective-permute-start.3 = (bf16[2,2,128,128]{3,2,1,0:T(8,128)(2,1)S(1)}, bf16[2,2,128,128]{3,2,1,0:T(8,128)(2,1)S(1)}, u32[]{:S(2)}, u32[]{:S(2)}) collective-permute-start(bf16[2,2,128,128]{3,2,1,0:T(8,128)(2,1)S(1)} %get-tuple-element.45), channel_id=1, source_target_pairs={{0,48},{16,64},{32,80},{48,96},{64,112},{80,0},{96,16},{112,32},{1... | collective-permute-start | bytes 393224 | tf_op jit(solution)/shard_map/ppermute | solution.py:458
  47.6 7.8 %collective-permute-start.4 = (bf16[2,2,128,128]{3,2,1,0:T(8,128)(2,1)S(1)}, bf16[2,2,128,128]{3,2,1,0:T(8,128)(2,1)S(1)}, u32[]{:S(2)}, u32[]{:S(2)}) collective-permute-start(bf16[2,2,128,128]{3,2,1,0:T(8,128)(2,1)S(1)} %get-tuple-element.46), channel_id=1, source_target_pairs={{0,64},{16,80},{32,96},{48,112},{64,0},{80,16},{96,32},{112,48},{1... | collective-permute-start | bytes 393224 | tf_op jit(solution)/shard_map/ppermute | solution.py:458
  48.6 9.4 %collective-permute-start.5 = (bf16[2,2,128,128]{3,2,1,0:T(8,128)(2,1)S(1)}, bf16[2,2,128,128]{3,2,1,0:T(8,128)(2,1)S(1)}, u32[]{:S(2)}, u32[]{:S(2)}) collective-permute-start(bf16[2,2,128,128]{3,2,1,0:T(8,128)(2,1)S(1)} %get-tuple-element.47), channel_id=1, source_target_pairs={{0,80},{16,96},{32,112},{48,0},{64,16},{80,32},{96,48},{112,64},{1... | collective-permute-start | bytes 393224 | tf_op jit(solution)/shard_map/ppermute | solution.py:458
  50.6 9.1 %collective-permute-start.6 = (bf16[2,2,128,128]{3,2,1,0:T(8,128)(2,1)S(1)}, bf16[2,2,128,128]{3,2,1,0:T(8,128)(2,1)S(1)}, u32[]{:S(2)}, u32[]{:S(2)}) collective-permute-start(bf16[2,2,128,128]{3,2,1,0:T(8,128)(2,1)S(1)} %get-tuple-element.48), channel_id=1, source_target_pairs={{0,96},{16,112},{32,0},{48,16},{64,32},{80,48},{96,64},{112,80},{1... | collective-permute-start | bytes 393224 | tf_op jit(solution)/shard_map/ppermute | solution.py:458
  50.8 8.9 %collective-permute-start.7 = (bf16[2,2,128,128]{3,2,1,0:T(8,128)(2,1)S(1)}, bf16[2,2,128,128]{3,2,1,0:T(8,128)(2,1)S(1)}, u32[]{:S(2)}, u32[]{:S(2)}) collective-permute-start(bf16[2,2,128,128]{3,2,1,0:T(8,128)(2,1)S(1)} %get-tuple-element.49), channel_id=1, source_target_pairs={{0,112},{16,0},{32,16},{48,32},{64,48},{80,64},{96,80},{112,96},{1... | collective-permute-start | bytes 393224 | tf_op jit(solution)/shard_map/ppermute | solution.py:458
  60.4 9.4 %collective-permute-start.8 = (bf16[2,2,128,128]{3,2,1,0:T(8,128)(2,1)S(1)}, bf16[2,2,128,128]{3,2,1,0:T(8,128)(2,1)S(1)}, u32[]{:S(2)}, u32[]{:S(2)}) collective-permute-start(bf16[2,2,128,128]{3,2,1,0:T(8,128)(2,1)S(1)} %pick_cross.1), channel_id=1, source_target_pairs={{0,128},{16,144},{32,160},{48,176},{64,192},{80,208},{96,224},{112... | collective-permute-start | bytes 393224 | tf_op jit(solution)/shard_map/ppermute | solution.py:458
  65.0 3.7 %collective-permute-start.1 = (bf16[2,128,128]{2,1,0:T(8,128)(2,1)S(1)}, bf16[2,128,128]{2,1,0:T(8,128)(2,1)S(1)}, u32[]{:S(2)}, u32[]{:S(2)}) collective-permute-start(bf16[2,128,128]{2,1,0:T(8,128)(2,1)S(1)} %get-tuple-element.41), channel_id=1, source_target_pairs={{0,16},{16,32},{32,48},{48,64},{64,80},{80,96},{96,112},{112,128},... | collective-permute-start | bytes 196616 | tf_op jit(solution)/shard_map/ppermute | solution.py:458
  69.7 63.7 %all-to-all-start.2 = ((bf16[32,2,128,128]{3,2,1,0:T(8,128)(2,1)}), bf16[32,2,128,128]{3,2,1,0:T(8,128)(2,1)}, u32[]{:S(2)}, u32[]{:S(2)}) async-start(bf16[32,2,128,128]{3,2,1,0:T(8,128)(2,1)} %pack.1), calls=%async_computation.2 | async-start | bytes 4194304 | tf_op jit(solution)/shard_map/all_to_all | solution.py:455
  147.4 40.4 %all-to-all-start.3 = ((bf16[16,2,128,128]{3,2,1,0:T(8,128)(2,1)}), bf16[16,2,128,128]{3,2,1,0:T(8,128)(2,1)S(1)}, u32[]{:S(2)}, u32[]{:S(2)}) async-start(bf16[16,2,128,128]{3,2,1,0:T(8,128)(2,1)} %get-tuple-element.54), calls=%async_computation.3 | async-start | bytes 2097152 | tf_op jit(solution)/shard_map/all_to_all | solution.py:452
  156.3 18.1 %collective-permute-start.9 = (bf16[2,2,128,128]{3,2,1,0:T(8,128)(2,1)S(1)}, bf16[2,2,128,128]{3,2,1,0:T(8,128)(2,1)S(1)}, u32[]{:S(2)}, u32[]{:S(2)}) collective-permute-start(bf16[2,2,128,128]{3,2,1,0:T(8,128)(2,1)S(1)} %get-tuple-element.55.own), channel_id=1, source_target_pairs={{0,128},{16,144},{32,160},{48,176},{64,192},{80,208},{96,224},{112... | collective-permute-start | bytes 393224 | tf_op jit(solution)/shard_map/ppermute | solution.py:458
  156.9 1.9 collective-permute-start.10
  187.8 61.4 %all-to-all-start.4 = ((bf16[32,2,128,128]{3,2,1,0:T(8,128)(2,1)}), bf16[32,2,128,128]{3,2,1,0:T(8,128)(2,1)}, u32[]{:S(2)}, u32[]{:S(2)}) async-start(bf16[32,2,128,128]{3,2,1,0:T(8,128)(2,1)} %get-tuple-element.62), calls=%async_computation.4 | async-start | bytes 4194304 | tf_op jit(solution)/shard_map/all_to_all | solution.py:455
  194.6 14.7 %collective-permute-start.11 = (bf16[2,2,128,128]{3,2,1,0:T(8,128)(2,1)S(1)}, bf16[2,2,128,128]{3,2,1,0:T(8,128)(2,1)S(1)}, u32[]{:S(2)}, u32[]{:S(2)}) collective-permute-start(bf16[2,2,128,128]{3,2,1,0:T(8,128)(2,1)S(1)} %get-tuple-element.65), channel_id=1, source_target_pairs={{0,112},{16,0},{32,16},{48,32},{64,48},{80,64},{96,80},{112,96},{1... | collective-permute-start | bytes 393224 | tf_op jit(solution)/shard_map/ppermute | solution.py:458
  195.2 17.0 %collective-permute-start.12 = (bf16[2,2,128,128]{3,2,1,0:T(8,128)(2,1)S(1)}, bf16[2,2,128,128]{3,2,1,0:T(8,128)(2,1)S(1)}, u32[]{:S(2)}, u32[]{:S(2)}) collective-permute-start(bf16[2,2,128,128]{3,2,1,0:T(8,128)(2,1)S(1)} %get-tuple-element.66), channel_id=1, source_target_pairs={{0,96},{16,112},{32,0},{48,16},{64,32},{80,48},{96,64},{112,80},{1... | collective-permute-start | bytes 393224 | tf_op jit(solution)/shard_map/ppermute | solution.py:458
  195.8 19.1 %collective-permute-start.13 = (bf16[2,2,128,128]{3,2,1,0:T(8,128)(2,1)S(1)}, bf16[2,2,128,128]{3,2,1,0:T(8,128)(2,1)S(1)}, u32[]{:S(2)}, u32[]{:S(2)}) collective-permute-start(bf16[2,2,128,128]{3,2,1,0:T(8,128)(2,1)S(1)} %get-tuple-element.67), channel_id=1, source_target_pairs={{0,80},{16,96},{32,112},{48,0},{64,16},{80,32},{96,48},{112,64},{1... | collective-permute-start | bytes 393224 | tf_op jit(solution)/shard_map/ppermute | solution.py:458
  196.2 25.6 %collective-permute-start.14 = (bf16[2,2,128,128]{3,2,1,0:T(8,128)(2,1)S(1)}, bf16[2,2,128,128]{3,2,1,0:T(8,128)(2,1)S(1)}, u32[]{:S(2)}, u32[]{:S(2)}) collective-permute-start(bf16[2,2,128,128]{3,2,1,0:T(8,128)(2,1)S(1)} %get-tuple-element.68), channel_id=1, source_target_pairs={{0,64},{16,80},{32,96},{48,112},{64,0},{80,16},{96,32},{112,48},{1... | collective-permute-start | bytes 393224 | tf_op jit(solution)/shard_map/ppermute | solution.py:458
  199.1 22.7 %collective-permute-start.15 = (bf16[2,2,128,128]{3,2,1,0:T(8,128)(2,1)S(1)}, bf16[2,2,128,128]{3,2,1,0:T(8,128)(2,1)S(1)}, u32[]{:S(2)}, u32[]{:S(2)}) collective-permute-start(bf16[2,2,128,128]{3,2,1,0:T(8,128)(2,1)S(1)} %get-tuple-element.69), channel_id=1, source_target_pairs={{0,48},{16,64},{32,80},{48,96},{64,112},{80,0},{96,16},{112,32},{1... | collective-permute-start | bytes 393224 | tf_op jit(solution)/shard_map/ppermute | solution.py:458
  209.3 12.5 %collective-permute-start.16 = (bf16[2,2,128,128]{3,2,1,0:T(8,128)(2,1)S(1)}, bf16[2,2,128,128]{3,2,1,0:T(8,128)(2,1)S(1)}, u32[]{:S(2)}, u32[]{:S(2)}) collective-permute-start(bf16[2,2,128,128]{3,2,1,0:T(8,128)(2,1)S(1)} %get-tuple-element.70), channel_id=1, source_target_pairs={{0,32},{16,48},{32,64},{48,80},{64,96},{80,112},{96,0},{112,16},{1... | collective-permute-start | bytes 393224 | tf_op jit(solution)/shard_map/ppermute | solution.py:458
  212.2 9.6 %collective-permute-start.17 = (bf16[2,2,128,128]{3,2,1,0:T(8,128)(2,1)S(1)}, bf16[2,2,128,128]{3,2,1,0:T(8,128)(2,1)S(1)}, u32[]{:S(2)}, u32[]{:S(2)}) collective-permute-start(bf16[2,2,128,128]{3,2,1,0:T(8,128)(2,1)S(1)} %get-tuple-element.71), channel_id=1, source_target_pairs={{0,16},{16,32},{32,48},{48,64},{64,80},{80,96},{96,112},{112,0},{1... | collective-permute-start | bytes 393224 | tf_op jit(solution)/shard_map/ppermute | solution.py:458
  253.3 30.5 %all-to-all-start.5 = ((bf16[16,2,128,128]{3,2,1,0:T(8,128)(2,1)}), bf16[16,2,128,128]{3,2,1,0:T(8,128)(2,1)S(1)}, u32[]{:S(2)}, u32[]{:S(2)}) async-start(bf16[16,2,128,128]{3,2,1,0:T(8,128)(2,1)} %land.1), calls=%async_computation.5 | async-start | bytes 2097152 | tf_op jit(solution)/shard_map/all_to_all | solution.py:452
  (1 other events, 10.9 us)

commit v3 on v2

--- a/solution.py
+++ b/solution.py
@@ -354,47 +354,82 @@
     )(slot, third, near, kv, qg, edge, cross, main, *thirds)
 
 
-def land_kernel(
-    blocks, lanes, slots, main_ref, third_ref, sum_ref, edge_ref, home_ref, *refs
-):
+def land_kernel(blocks, slots, main_ref, sum_ref, edge_ref, home_ref, total):
+    f32 = jnp.float32
+    total[...] = sum_ref[...]
+    total[blocks - 1] += edge_ref[...].astype(f32)
+    for slot in range(slots):
+        row = main_ref[slot]
+
+        @pl.when(row < blocks)
+        def _():
+            total[row] += home_ref[slot].astype(f32)
+
+
+def land(main_index, sums, edge, home):
+    blocks, slots = sums.shape[0], home.shape[0]
+    return call(
+        functools.partial(land_kernel, blocks, slots),
+        jax.ShapeDtypeStruct(sums.shape, jnp.float32),
+        [SMEM] + [VMEM] * 3,
+        VMEM,
+        "land",
+        sums.size * 2,
+        12 * sums.size,
+    )(main_index, sums, edge, home)
+
+
+def land_thirds_kernel(blocks, lanes, third_ref, total, *refs):
     thirds, out = refs[:lanes], refs[lanes]
-    total, low, sems = refs[lanes + 1 :]
-    f32 = jnp.float32
-    total[pl.ds(0, blocks)] = sum_ref[...]
-    total[blocks - 1] += edge_ref[...].astype(f32)
-    for step in range(lanes):
-        for side in range(2):
-            index = third_ref[2 * step + side]
-
-            @pl.when(index >= 0)
-            def _():
-                total[index] += thirds[step][side].astype(f32)
-
-    for slot in range(slots):
-        total[main_ref[slot]] += home_ref[slot].astype(f32)
+    held, low, in_sems, sems, late, late_sems = refs[lanes + 1 :]
+    reads = [pltpu.make_async_copy(total.at[n], held.at[n], in_sems.at[n]) for n in range(blocks)]
     writes = [pltpu.make_async_copy(low.at[n], out.at[n], sems.at[n]) for n in range(blocks)]
+    start_all(reads)
+
+    def arrive(at):
+        step, side = divmod(at, 2)
+        return pltpu.make_async_copy(thirds[step].at[side], late.at[at], late_sems.at[at])
+
+    for at in range(2 * lanes):
+
+        @pl.when(third_ref[at] >= 0)
+        def _():
+            arrive(at).start()
+
+    wait_all(reads)
+    for at in range(2 * lanes):
+
+        @pl.when(third_ref[at] >= 0)
+        def _():
+            arrive(at).wait()
+            held[third_ref[at]] += late[at].astype(jnp.float32)
+
     for n in range(blocks):
-        low[n] = total[n].astype(low.dtype)
+        low[n] = held[n].astype(low.dtype)
         writes[n].start()
     wait_all(writes)
 
 
-def land(main_index, third_index, sums, edge, home, thirds):
-    blocks, lanes, slots = sums.shape[0], len(thirds), home.shape[0]
-    return call(
-        functools.partial(land_kernel, blocks, lanes, slots),
-        pltpu.HBM(sums.shape, home.dtype),
-        [SMEM] * 2 + [VMEM] * (3 + lanes),
+def land_thirds(third_index, total, thirds):
+    blocks, lanes = total.shape[0], len(thirds)
+    dtype = thirds[0].dtype
+    return call(
+        functools.partial(land_thirds_kernel, blocks, lanes),
+        pltpu.HBM(total.shape, dtype),
+        [SMEM] + [ANY] * (1 + lanes),
         ANY,
-        "land",
-        sums.size * 2,
-        10 * sums.size,
+        "land_thirds",
+        total.size,
+        6 * total.size,
         [
-            pltpu.VMEM((blocks + 1,) + sums.shape[1:], jnp.float32),
-            pltpu.VMEM(sums.shape, home.dtype),
+            pltpu.VMEM(total.shape, jnp.float32),
+            pltpu.VMEM(total.shape, dtype),
             pltpu.SemaphoreType.DMA((blocks,)),
+            pltpu.SemaphoreType.DMA((blocks,)),
+            pltpu.VMEM((2 * lanes,) + total.shape[1:], dtype),
+            pltpu.SemaphoreType.DMA((2 * lanes,)),
         ],
-    )(main_index, third_index, sums, edge, home, *thirds)
+    )(third_index, total, *thirds)
 
 
 def plan(key_lists, blocks, ctx_count, lanes):
@@ -478,16 +513,16 @@
     out, sums, edge_grad, main_grad, third_grad = attend(
         my_slot, my_third, near_steps, kv, qg, edge, cross, main, thirds
     )
-    out = head_exchange(out)
+    home = ctx_exchange(main_grad)
     cross_grad = across(third_grad)
     edge_grad = move(edge_grad, lambda i: (i - 1) % ctx_count)
-    main_grad, out, cross_grad, edge_grad = lax.optimization_barrier(
-        (main_grad, out, cross_grad, edge_grad)
-    )
-    home = ctx_exchange(main_grad)
+    out, home, cross_grad, edge_grad = lax.optimization_barrier((out, home, cross_grad, edge_grad))
+    out = head_exchange(out)
     late = along(pick_back(near_steps, cross_steps, third_grad, cross_grad, lanes), -1)
+    total = land(main_index, sums, edge_grad, home)
+    total, out = lax.optimization_barrier((total, out))
+    total = land_thirds(third_index, total, late)
     attended, query_grad = join_heads(out)
-    total = land(main_index, third_index, sums, edge_grad, home, late)
     key_grad, value_grad = join_heads(head_exchange(total))
     return attended, query_grad, key_grad, value_grad
 

time: 286 us -> 281 us (0.983)
  waiting for transfers between devices: 185 us -> 172 us
  starting transfers between devices: 67 us -> 71.6 us
    all_to_all x2, waiting for transfers between devices: 78.6 us -> 51.3 us  [ctx_exchange(): return lax.all_to_all(array, 'ctx', split_axis=0, concat_axis=0, tiled=True)]
    ppermute x18, waiting for transfers between devices: 45.9 us -> 67.6 us  [move(): lax.ppermute(array, 'ctx', [(i, target(i)) for i in range(ctx_count)])]
    all_to_all x4, waiting for transfers between devices: 60.5 us -> 52.9 us  [head_exchange(): lax.all_to_all(array, 'head', split_axis=0, concat_axis=0, tiled=True)]
    ppermute x18, starting transfers between devices: 21.6 us -> 27.3 us  [move(): lax.ppermute(array, 'ctx', [(i, target(i)) for i in range(ctx_count)])]
    pallas_call x1 -> x2, Pallas kernels: 4.01 us -> 6.5 us  [the longest x1 3.6 us: land_thirds(): call(functools.partial(land_thirds_kernel, blocks, lanes), pltpu.HBM(tota...]
  transfers between devices with their start and end apart: 24 -> 24, of which waited for: 17 -> 13; matrix products, arithmetic and copies ran while one was open for 1% -> 1% of each run, Pallas kernels for 3% -> 4%
where the time goes in v3:
time: 281 us; the launch traced here: 280 us
  waiting for transfers between devices  172 us (61%)
  starting transfers between devices  71.6 us (25%)
  Pallas kernels  31.7 us (11%)
    ppermute x18, waiting for transfers between devices, move(): lax.ppermute(array, 'ctx', [(i, target(i)) for i in range(ctx_count)])  67.6 us
    all_to_all x4, waiting for transfers between devices, head_exchange(): lax.all_to_all(array, 'head', split_axis=0, concat_axis=0, tiled=True)  52.9 us
    all_to_all x2, waiting for transfers between devices, ctx_exchange(): return lax.all_to_all(array, 'ctx', split_axis=0, concat_axis=0, tiled=True)  51.3 us
    ppermute x18, starting transfers between devices, move(): lax.ppermute(array, 'ctx', [(i, target(i)) for i in range(ctx_count)])  27.3 us
    all_to_all x4, starting transfers between devices, head_exchange(): lax.all_to_all(array, 'head', split_axis=0, concat_axis=0, tiled=True)  25.6 us
    all_to_all x2, starting transfers between devices, ctx_exchange(): return lax.all_to_all(array, 'ctx', split_axis=0, concat_axis=0, tiled=True)  18.6 us
    pallas_call x1, Pallas kernels, attend(): call(functools.partial(attend_kernel, blocks, lanes), (pltpu.HBM(qg.shape...  14 us
  transfers between devices with their start and end apart: 24, of which 13 were waited for; matrix products, arithmetic and copies ran while one was open for 1% of the time, Pallas kernels for 4%

profile of v3, /device:TPU:56, one launch (start us, length us, event | category | flops | bytes accessed | tf_op | source)
XLA Modules:
  0.0 280.3 jit_solution(4646952010537736899)
XLA Ops:
  0.6 2.4 split_heads.2
  3.0 8.5 %all-to-all-start = ((bf16[16,2,128,128]{3,2,1,0:T(8,128)(2,1)}), bf16[16,2,128,128]{3,2,1,0:T(8,128)(2,1)S(1)}, u32[]{:S(2)}, u32[]{:S(2)}) async-start(bf16[16,2,128,128]{3,2,1,0:T(8,128)(2,1)} %split_heads.2), calls=%async_computation | async-start | bytes 2097152 | tf_op jit(solution)/shard_map/all_to_all | solution.py:487
  12.4 2.3 split_heads.3
  15.0 22.2 %all-to-all-done.kv_ref.in_ref = bf16[16,2,128,128]{3,2,1,0:T(8,128)(2,1)S(1)} async-done(((bf16[16,2,128,128]{3,2,1,0:T(8,128)(2,1)}), bf16[16,2,128,128]{3,2,1,0:T(8,128)(2,1)S(1)}, u32[]{:S(2)}, u32[]{:S(2)}) %all-to-all-start) | async-done | bytes 1048608 | tf_op jit(solution)/shard_map/all_to_all | solution.py:487
  37.3 5.2 %all-to-all-start.1 = ((bf16[16,2,128,128]{3,2,1,0:T(8,128)(2,1)}), bf16[16,2,128,128]{3,2,1,0:T(8,128)(2,1)}, u32[]{:S(2)}, u32[]{:S(2)}) async-start(bf16[16,2,128,128]{3,2,1,0:T(8,128)(2,1)} %split_heads.3), calls=%async_computation.1 | async-start | bytes 2097152 | tf_op jit(solution)/shard_map/all_to_all | solution.py:487
  45.0 2.6 collective-permute-start.3
  50.8 2.2 collective-permute-start.7
  55.5 2.5 collective-permute-done.5.refs_5_
  60.4 4.6 %collective-permute-start.8 = (bf16[2,2,128,128]{3,2,1,0:T(8,128)(2,1)S(1)}, bf16[2,2,128,128]{3,2,1,0:T(8,128)(2,1)S(1)}, u32[]{:S(2)}, u32[]{:S(2)}) collective-permute-start(bf16[2,2,128,128]{3,2,1,0:T(8,128)(2,1)S(1)} %pick_cross.1), channel_id=1, source_target_pairs={{0,128},{16,144},{32,160},{48,176},{64,192},{80,208},{96,224},{112... | collective-permute-start | bytes 393224 | tf_op jit(solution)/shard_map/ppermute | solution.py:493
  69.8 12.5 %all-to-all-start.2 = ((bf16[32,2,128,128]{3,2,1,0:T(8,128)(2,1)}), bf16[32,2,128,128]{3,2,1,0:T(8,128)(2,1)}, u32[]{:S(2)}, u32[]{:S(2)}) async-start(bf16[32,2,128,128]{3,2,1,0:T(8,128)(2,1)} %pack.1), calls=%async_computation.2 | async-start | bytes 4194304 | tf_op jit(solution)/shard_map/all_to_all | solution.py:490
  82.4 51.3 %all-to-all-done.2.main = bf16[32,2,128,128]{3,2,1,0:T(8,128)(2,1)} async-done(((bf16[32,2,128,128]{3,2,1,0:T(8,128)(2,1)}), bf16[32,2,128,128]{3,2,1,0:T(8,128)(2,1)}, u32[]{:S(2)}, u32[]{:S(2)}) %all-to-all-start.2) | async-done | bytes 2097184 | tf_op jit(solution)/shard_map/all_to_all | solution.py:490
  133.7 14.0 %attend.1 = (bf16[16,2,128,128]{3,2,1,0:T(8,128)(2,1)}, f32[16,2,128,128]{3,2,1,0:T(8,128)}, bf16[2,128,128]{2,1,0:T(8,128)(2,1)S(1)}, bf16[32,2,128,128]{3,2,1,0:T(8,128)(2,1)}, bf16[2,2,128,128]{3,2,1,0:T(8,128)(2,1)S(1)}) custom-call(s32[32]{0:T(128)S(1)} %select_reduce_fusion.4.slot_ref, s32[2]{0:T(128)S(1)} %get-tuple-element.82.third_ref, ...), custom_call_target="tpu_custom_call" | custom-call | flops 1342177280 | bytes 10485760 | tf_op jit(solution)/shard_map/attend/pallas_call | solution.py:331
  147.7 6.1 %all-to-all-start.3 = ((bf16[32,2,128,128]{3,2,1,0:T(8,128)(2,1)}), bf16[32,2,128,128]{3,2,1,0:T(8,128)(2,1)}, u32[]{:S(2)}, u32[]{:S(2)}) async-start(bf16[32,2,128,128]{3,2,1,0:T(8,128)(2,1)} %get-tuple-element.57), calls=%async_computation.3 | async-start | bytes 4194304 | tf_op jit(solution)/shard_map/all_to_all | solution.py:490
  153.8 5.4 %collective-permute-start.9 = (bf16[2,2,128,128]{3,2,1,0:T(8,128)(2,1)S(1)}, bf16[2,2,128,128]{3,2,1,0:T(8,128)(2,1)S(1)}, u32[]{:S(2)}, u32[]{:S(2)}) collective-permute-start(bf16[2,2,128,128]{3,2,1,0:T(8,128)(2,1)S(1)} %get-tuple-element.58.own), channel_id=1, source_target_pairs={{0,128},{16,144},{32,160},{48,176},{64,192},{80,208},{96,224},{112... | collective-permute-start | bytes 393224 | tf_op jit(solution)/shard_map/ppermute | solution.py:493
  159.5 12.7 %collective-permute-done.10.edge_ref = bf16[2,128,128]{2,1,0:T(8,128)(2,1)S(1)} collective-permute-done((bf16[2,128,128]{2,1,0:T(8,128)(2,1)S(1)}, bf16[2,128,128]{2,1,0:T(8,128)(2,1)S(1)}, u32[]{:S(2)}, u32[]{:S(2)}) %collective-permute-start.10) | collective-permute-done | bytes 65568 | tf_op jit(solution)/shard_map/ppermute | solution.py:493
  172.2 38.8 %collective-permute-done.9.crossed = bf16[2,2,128,128]{3,2,1,0:T(8,128)(2,1)S(1)} collective-permute-done((bf16[2,2,128,128]{3,2,1,0:T(8,128)(2,1)S(1)}, bf16[2,2,128,128]{3,2,1,0:T(8,128)(2,1)S(1)}, u32[]{:S(2)}, u32[]{:S(2)}) %collective-permute-start.9) | collective-permute-done | bytes 131104 | tf_op jit(solution)/shard_map/ppermute | solution.py:493
  211.0 6.4 %all-to-all-start.4 = ((bf16[16,2,128,128]{3,2,1,0:T(8,128)(2,1)}), bf16[16,2,128,128]{3,2,1,0:T(8,128)(2,1)S(1)}, u32[]{:S(2)}, u32[]{:S(2)}) async-start(bf16[16,2,128,128]{3,2,1,0:T(8,128)(2,1)} %get-tuple-element.62), calls=%async_computation.4 | async-start | bytes 2097152 | tf_op jit(solution)/shard_map/all_to_all | solution.py:487
  220.6 2.4 collective-permute-start.14
  225.4 8.4 %collective-permute-done.12.refs_2_ = bf16[2,2,128,128]{3,2,1,0:T(8,128)(2,1)S(1)} collective-permute-done((bf16[2,2,128,128]{3,2,1,0:T(8,128)(2,1)S(1)}, bf16[2,2,128,128]{3,2,1,0:T(8,128)(2,1)S(1)}, u32[]{:S(2)}, u32[]{:S(2)}) %collective-permute-start.12) | collective-permute-done | bytes 131104 | tf_op jit(solution)/shard_map/ppermute | solution.py:493
  233.8 2.9 %land.1.total = f32[16,2,128,128]{3,2,1,0:T(8,128)S(1)} custom-call(s32[32]{0:T(128)S(1)} %select_n.143.index_ref.main_ref, f32[16,2,128,128]{3,2,1,0:T(8,128)} %get-tuple-element.55.sum_ref, bf16[2,128,128]{2,1,0:T(8,128)(2,1)S(1)} %collective-permute-done.10.edge_ref, bf16[32,2,128,128]{3,2,1,0:T(8,128)(2,1)} %all-to-all-done.3.home_ref), custom_call_target="tpu_custom_call" | custom-call | flops 1048576 | bytes 6291456 | tf_op jit(solution)/shard_map/land/pallas_call | solution.py:371
  238.0 5.9 %all-to-all-done.4.in_ref = bf16[16,2,128,128]{3,2,1,0:T(8,128)(2,1)S(1)} async-done(((bf16[16,2,128,128]{3,2,1,0:T(8,128)(2,1)}), bf16[16,2,128,128]{3,2,1,0:T(8,128)(2,1)S(1)}, u32[]{:S(2)}, u32[]{:S(2)}) %all-to-all-start.4) | async-done | bytes 1048608 | tf_op jit(solution)/shard_map/all_to_all | solution.py:487
  244.0 3.6 %land_thirds.1 = bf16[16,2,128,128]{3,2,1,0:T(8,128)(2,1)} custom-call(s32[16]{0:T(128)S(1)} %reshape.200.third_ref, f32[16,2,128,128]{3,2,1,0:T(8,128)} %copy-done, bf16[2,2,128,128]{3,2,1,0:T(8,128)(2,1)S(1)} %get-tuple-element.68.refs_0_, bf16[2,2,128,128]{3,2,1,0:T(8,128)(2,1)S(1)} %collective-permute-done.11.refs_1_, ...), custom_call_target="tpu_custom_call" | custom-call | flops 524288 | bytes 3145728 | tf_op jit(solution)/shard_map/land_thirds/pallas_call | solution.py:416
  247.6 5.6 %all-to-all-start.5 = ((bf16[16,2,128,128]{3,2,1,0:T(8,128)(2,1)}), bf16[16,2,128,128]{3,2,1,0:T(8,128)(2,1)S(1)}, u32[]{:S(2)}, u32[]{:S(2)}) async-start(bf16[16,2,128,128]{3,2,1,0:T(8,128)(2,1)} %land_thirds.1), calls=%async_computation.5 | async-start | bytes 2097152 | tf_op jit(solution)/shard_map/all_to_all | solution.py:487
  254.3 24.7 %all-to-all-done.5.in_ref = bf16[16,2,128,128]{3,2,1,0:T(8,128)(2,1)S(1)} async-done(((bf16[16,2,128,128]{3,2,1,0:T(8,128)(2,1)}), bf16[16,2,128,128]{3,2,1,0:T(8,128)(2,1)S(1)}, u32[]{:S(2)}, u32[]{:S(2)}) %all-to-all-start.5) | async-done | bytes 1048608 | tf_op jit(solution)/shard_map/all_to_all | solution.py:487
  (68 shorter events, 26.1 us)
Async XLA Ops:
  3.0 34.2 %all-to-all-start = ((bf16[16,2,128,128]{3,2,1,0:T(8,128)(2,1)}), bf16[16,2,128,128]{3,2,1,0:T(8,128)(2,1)S(1)}, u32[]{:S(2)}, u32[]{:S(2)}) async-start(bf16[16,2,128,128]{3,2,1,0:T(8,128)(2,1)} %split_heads.2), calls=%async_computation | async-start | bytes 2097152 | tf_op jit(solution)/shard_map/all_to_all | solution.py:487
  37.3 32.5 %all-to-all-start.1 = ((bf16[16,2,128,128]{3,2,1,0:T(8,128)(2,1)}), bf16[16,2,128,128]{3,2,1,0:T(8,128)(2,1)}, u32[]{:S(2)}, u32[]{:S(2)}) async-start(bf16[16,2,128,128]{3,2,1,0:T(8,128)(2,1)} %split_heads.3), calls=%async_computation.1 | async-start | bytes 2097152 | tf_op jit(solution)/shard_map/all_to_all | solution.py:487
  44.4 6.3 %collective-permute-start = (bf16[2,2,128,128]{3,2,1,0:T(8,128)(2,1)S(1)}, bf16[2,2,128,128]{3,2,1,0:T(8,128)(2,1)S(1)}, u32[]{:S(2)}, u32[]{:S(2)}) collective-permute-start(bf16[2,2,128,128]{3,2,1,0:T(8,128)(2,1)S(1)} %get-tuple-element.41), channel_id=1, source_target_pairs={{0,16},{16,32},{32,48},{48,64},{64,80},{80,96},{96,112},{112,0},{1... | collective-permute-start | bytes 393224 | tf_op jit(solution)/shard_map/ppermute | solution.py:493
  44.4 6.4 %collective-permute-start.2 = (bf16[2,2,128,128]{3,2,1,0:T(8,128)(2,1)S(1)}, bf16[2,2,128,128]{3,2,1,0:T(8,128)(2,1)S(1)}, u32[]{:S(2)}, u32[]{:S(2)}) collective-permute-start(bf16[2,2,128,128]{3,2,1,0:T(8,128)(2,1)S(1)} %get-tuple-element.46), channel_id=1, source_target_pairs={{0,32},{16,48},{32,64},{48,80},{64,96},{80,112},{96,0},{112,16},{1... | collective-permute-start | bytes 393224 | tf_op jit(solution)/shard_map/ppermute | solution.py:493
  45.0 10.1 %collective-permute-start.3 = (bf16[2,2,128,128]{3,2,1,0:T(8,128)(2,1)S(1)}, bf16[2,2,128,128]{3,2,1,0:T(8,128)(2,1)S(1)}, u32[]{:S(2)}, u32[]{:S(2)}) collective-permute-start(bf16[2,2,128,128]{3,2,1,0:T(8,128)(2,1)S(1)} %get-tuple-element.47), channel_id=1, source_target_pairs={{0,48},{16,64},{32,80},{48,96},{64,112},{80,0},{96,16},{112,32},{1... | collective-permute-start | bytes 393224 | tf_op jit(solution)/shard_map/ppermute | solution.py:493
  47.6 7.8 %collective-permute-start.4 = (bf16[2,2,128,128]{3,2,1,0:T(8,128)(2,1)S(1)}, bf16[2,2,128,128]{3,2,1,0:T(8,128)(2,1)S(1)}, u32[]{:S(2)}, u32[]{:S(2)}) collective-permute-start(bf16[2,2,128,128]{3,2,1,0:T(8,128)(2,1)S(1)} %get-tuple-element.48), channel_id=1, source_target_pairs={{0,64},{16,80},{32,96},{48,112},{64,0},{80,16},{96,32},{112,48},{1... | collective-permute-start | bytes 393224 | tf_op jit(solution)/shard_map/ppermute | solution.py:493
  48.6 9.4 %collective-permute-start.5 = (bf16[2,2,128,128]{3,2,1,0:T(8,128)(2,1)S(1)}, bf16[2,2,128,128]{3,2,1,0:T(8,128)(2,1)S(1)}, u32[]{:S(2)}, u32[]{:S(2)}) collective-permute-start(bf16[2,2,128,128]{3,2,1,0:T(8,128)(2,1)S(1)} %get-tuple-element.49), channel_id=1, source_target_pairs={{0,80},{16,96},{32,112},{48,0},{64,16},{80,32},{96,48},{112,64},{1... | collective-permute-start | bytes 393224 | tf_op jit(solution)/shard_map/ppermute | solution.py:493
  50.7 9.1 %collective-permute-start.6 = (bf16[2,2,128,128]{3,2,1,0:T(8,128)(2,1)S(1)}, bf16[2,2,128,128]{3,2,1,0:T(8,128)(2,1)S(1)}, u32[]{:S(2)}, u32[]{:S(2)}) collective-permute-start(bf16[2,2,128,128]{3,2,1,0:T(8,128)(2,1)S(1)} %get-tuple-element.50), channel_id=1, source_target_pairs={{0,96},{16,112},{32,0},{48,16},{64,32},{80,48},{96,64},{112,80},{1... | collective-permute-start | bytes 393224 | tf_op jit(solution)/shard_map/ppermute | solution.py:493
  50.8 8.9 %collective-permute-start.7 = (bf16[2,2,128,128]{3,2,1,0:T(8,128)(2,1)S(1)}, bf16[2,2,128,128]{3,2,1,0:T(8,128)(2,1)S(1)}, u32[]{:S(2)}, u32[]{:S(2)}) collective-permute-start(bf16[2,2,128,128]{3,2,1,0:T(8,128)(2,1)S(1)} %get-tuple-element.51), channel_id=1, source_target_pairs={{0,112},{16,0},{32,16},{48,32},{64,48},{80,64},{96,80},{112,96},{1... | collective-permute-start | bytes 393224 | tf_op jit(solution)/shard_map/ppermute | solution.py:493
  60.4 9.4 %collective-permute-start.8 = (bf16[2,2,128,128]{3,2,1,0:T(8,128)(2,1)S(1)}, bf16[2,2,128,128]{3,2,1,0:T(8,128)(2,1)S(1)}, u32[]{:S(2)}, u32[]{:S(2)}) collective-permute-start(bf16[2,2,128,128]{3,2,1,0:T(8,128)(2,1)S(1)} %pick_cross.1), channel_id=1, source_target_pairs={{0,128},{16,144},{32,160},{48,176},{64,192},{80,208},{96,224},{112... | collective-permute-start | bytes 393224 | tf_op jit(solution)/shard_map/ppermute | solution.py:493
  65.0 3.7 %collective-permute-start.1 = (bf16[2,128,128]{2,1,0:T(8,128)(2,1)S(1)}, bf16[2,128,128]{2,1,0:T(8,128)(2,1)S(1)}, u32[]{:S(2)}, u32[]{:S(2)}) collective-permute-start(bf16[2,128,128]{2,1,0:T(8,128)(2,1)S(1)} %get-tuple-element.43), channel_id=1, source_target_pairs={{0,16},{16,32},{32,48},{48,64},{64,80},{80,96},{96,112},{112,128},... | collective-permute-start | bytes 196616 | tf_op jit(solution)/shard_map/ppermute | solution.py:493
  69.8 64.0 %all-to-all-start.2 = ((bf16[32,2,128,128]{3,2,1,0:T(8,128)(2,1)}), bf16[32,2,128,128]{3,2,1,0:T(8,128)(2,1)}, u32[]{:S(2)}, u32[]{:S(2)}) async-start(bf16[32,2,128,128]{3,2,1,0:T(8,128)(2,1)} %pack.1), calls=%async_computation.2 | async-start | bytes 4194304 | tf_op jit(solution)/shard_map/all_to_all | solution.py:490
  147.7 63.2 %all-to-all-start.3 = ((bf16[32,2,128,128]{3,2,1,0:T(8,128)(2,1)}), bf16[32,2,128,128]{3,2,1,0:T(8,128)(2,1)}, u32[]{:S(2)}, u32[]{:S(2)}) async-start(bf16[32,2,128,128]{3,2,1,0:T(8,128)(2,1)} %get-tuple-element.57), calls=%async_computation.3 | async-start | bytes 4194304 | tf_op jit(solution)/shard_map/all_to_all | solution.py:490
  153.8 57.1 %collective-permute-start.9 = (bf16[2,2,128,128]{3,2,1,0:T(8,128)(2,1)S(1)}, bf16[2,2,128,128]{3,2,1,0:T(8,128)(2,1)S(1)}, u32[]{:S(2)}, u32[]{:S(2)}) collective-permute-start(bf16[2,2,128,128]{3,2,1,0:T(8,128)(2,1)S(1)} %get-tuple-element.58.own), channel_id=1, source_target_pairs={{0,128},{16,144},{32,160},{48,176},{64,192},{80,208},{96,224},{112... | collective-permute-start | bytes 393224 | tf_op jit(solution)/shard_map/ppermute | solution.py:493
  159.2 13.0 %collective-permute-start.10 = (bf16[2,128,128]{2,1,0:T(8,128)(2,1)S(1)}, bf16[2,128,128]{2,1,0:T(8,128)(2,1)S(1)}, u32[]{:S(2)}, u32[]{:S(2)}) collective-permute-start(bf16[2,128,128]{2,1,0:T(8,128)(2,1)S(1)} %get-tuple-element.59), channel_id=1, source_target_pairs={{0,240},{16,0},{32,16},{48,32},{64,48},{80,64},{96,80},{112,96},{1... | collective-permute-start | bytes 196616 | tf_op jit(solution)/shard_map/ppermute | solution.py:493
  211.0 33.0 %all-to-all-start.4 = ((bf16[16,2,128,128]{3,2,1,0:T(8,128)(2,1)}), bf16[16,2,128,128]{3,2,1,0:T(8,128)(2,1)S(1)}, u32[]{:S(2)}, u32[]{:S(2)}) async-start(bf16[16,2,128,128]{3,2,1,0:T(8,128)(2,1)} %get-tuple-element.62), calls=%async_computation.4 | async-start | bytes 2097152 | tf_op jit(solution)/shard_map/all_to_all | solution.py:487
  218.2 6.9 %collective-permute-start.11 = (bf16[2,2,128,128]{3,2,1,0:T(8,128)(2,1)S(1)}, bf16[2,2,128,128]{3,2,1,0:T(8,128)(2,1)S(1)}, u32[]{:S(2)}, u32[]{:S(2)}) collective-permute-start(bf16[2,2,128,128]{3,2,1,0:T(8,128)(2,1)S(1)} %get-tuple-element.69), channel_id=1, source_target_pairs={{0,112},{16,0},{32,16},{48,32},{64,48},{80,64},{96,80},{112,96},{1... | collective-permute-start | bytes 393224 | tf_op jit(solution)/shard_map/ppermute | solution.py:493
  218.2 15.6 %collective-permute-start.12 = (bf16[2,2,128,128]{3,2,1,0:T(8,128)(2,1)S(1)}, bf16[2,2,128,128]{3,2,1,0:T(8,128)(2,1)S(1)}, u32[]{:S(2)}, u32[]{:S(2)}) collective-permute-start(bf16[2,2,128,128]{3,2,1,0:T(8,128)(2,1)S(1)} %get-tuple-element.70), channel_id=1, source_target_pairs={{0,96},{16,112},{32,0},{48,16},{64,32},{80,48},{96,64},{112,80},{1... | collective-permute-start | bytes 393224 | tf_op jit(solution)/shard_map/ppermute | solution.py:493
  219.6 24.4 %collective-permute-start.13 = (bf16[2,2,128,128]{3,2,1,0:T(8,128)(2,1)S(1)}, bf16[2,2,128,128]{3,2,1,0:T(8,128)(2,1)S(1)}, u32[]{:S(2)}, u32[]{:S(2)}) collective-permute-start(bf16[2,2,128,128]{3,2,1,0:T(8,128)(2,1)S(1)} %get-tuple-element.71), channel_id=1, source_target_pairs={{0,80},{16,96},{32,112},{48,0},{64,16},{80,32},{96,48},{112,64},{1... | collective-permute-start | bytes 393224 | tf_op jit(solution)/shard_map/ppermute | solution.py:493
  220.6 23.3 %collective-permute-start.14 = (bf16[2,2,128,128]{3,2,1,0:T(8,128)(2,1)S(1)}, bf16[2,2,128,128]{3,2,1,0:T(8,128)(2,1)S(1)}, u32[]{:S(2)}, u32[]{:S(2)}) collective-permute-start(bf16[2,2,128,128]{3,2,1,0:T(8,128)(2,1)S(1)} %get-tuple-element.72), channel_id=1, source_target_pairs={{0,64},{16,80},{32,96},{48,112},{64,0},{80,16},{96,32},{112,48},{1... | collective-permute-start | bytes 393224 | tf_op jit(solution)/shard_map/ppermute | solution.py:493
  223.0 20.9 %collective-permute-start.15 = (bf16[2,2,128,128]{3,2,1,0:T(8,128)(2,1)S(1)}, bf16[2,2,128,128]{3,2,1,0:T(8,128)(2,1)S(1)}, u32[]{:S(2)}, u32[]{:S(2)}) collective-permute-start(bf16[2,2,128,128]{3,2,1,0:T(8,128)(2,1)S(1)} %get-tuple-element.73), channel_id=1, source_target_pairs={{0,48},{16,64},{32,80},{48,96},{64,112},{80,0},{96,16},{112,32},{1... | collective-permute-start | bytes 393224 | tf_op jit(solution)/shard_map/ppermute | solution.py:493
  225.1 18.9 %collective-permute-start.16 = (bf16[2,2,128,128]{3,2,1,0:T(8,128)(2,1)S(1)}, bf16[2,2,128,128]{3,2,1,0:T(8,128)(2,1)S(1)}, u32[]{:S(2)}, u32[]{:S(2)}) collective-permute-start(bf16[2,2,128,128]{3,2,1,0:T(8,128)(2,1)S(1)} %get-tuple-element.74), channel_id=1, source_target_pairs={{0,32},{16,48},{32,64},{48,80},{64,96},{80,112},{96,0},{112,16},{1... | collective-permute-start | bytes 393224 | tf_op jit(solution)/shard_map/ppermute | solution.py:493
  233.8 10.2 %collective-permute-start.17 = (bf16[2,2,128,128]{3,2,1,0:T(8,128)(2,1)S(1)}, bf16[2,2,128,128]{3,2,1,0:T(8,128)(2,1)S(1)}, u32[]{:S(2)}, u32[]{:S(2)}) collective-permute-start(bf16[2,2,128,128]{3,2,1,0:T(8,128)(2,1)S(1)} %get-tuple-element.75), channel_id=1, source_target_pairs={{0,16},{16,32},{32,48},{48,64},{64,80},{80,96},{96,112},{112,0},{1... | collective-permute-start | bytes 393224 | tf_op jit(solution)/shard_map/ppermute | solution.py:493
  247.6 31.5 %all-to-all-start.5 = ((bf16[16,2,128,128]{3,2,1,0:T(8,128)(2,1)}), bf16[16,2,128,128]{3,2,1,0:T(8,128)(2,1)S(1)}, u32[]{:S(2)}, u32[]{:S(2)}) async-start(bf16[16,2,128,128]{3,2,1,0:T(8,128)(2,1)} %land_thirds.1), calls=%async_computation.5 | async-start | bytes 2097152 | tf_op jit(solution)/shard_map/all_to_all | solution.py:487
  (2 other events, 12.2 us)

commit v4 on v3

--- a/solution.py
+++ b/solution.py
@@ -15,13 +15,14 @@
 FULL = 60 * 1024 * 1024
 
 
-def call(kernel, out_shape, ins, outs, name, flops, nbytes, scratch=(), limit=51 * 1024 * 1024):
+def call(kernel, out_shape, ins, outs, name, flops, nbytes, scratch=(), limit=51 * 1024 * 1024, aliases=None):
     return pl.pallas_call(
         kernel,
         out_shape=out_shape,
         in_specs=list(ins),
         out_specs=outs,
         scratch_shapes=list(scratch),
+        input_output_aliases=aliases or {},
         compiler_params=pltpu.CompilerParams(vmem_limit_bytes=limit),
         cost_estimate=pl.CostEstimate(flops=flops, bytes_accessed=nbytes, transcendentals=0),
         name=name,
@@ -46,15 +47,15 @@
     arrays, out = refs[:count], refs[count]
     held, packed, sems, out_sems = refs[count + 1 :]
     reads = [pltpu.make_async_copy(arrays[w], held.at[w], sems.at[w]) for w in range(count)]
-    writes = [
-        pltpu.make_async_copy(packed.at[head], out.at[head], out_sems.at[head]) for head in range(heads)
-    ]
+    writes = []
     start_all(reads)
-    wait_all(reads)
-    for head in range(heads):
-        for w in range(count):
+    for w in range(count):
+        reads[w].wait()
+        for head in range(heads):
             packed[head, w] = held[w, :, pl.ds(head * HEAD_DIM, HEAD_DIM)]
-        writes[head].start()
+            sem = out_sems.at[w * heads + head]
+            writes.append(pltpu.make_async_copy(packed.at[head, w], out.at[head, w], sem))
+            writes[-1].start()
     wait_all(writes)
 
 
@@ -75,7 +76,7 @@
             pltpu.VMEM((count, rows, features), dtype),
             pltpu.VMEM(packed, dtype),
             pltpu.SemaphoreType.DMA((count,)),
-            pltpu.SemaphoreType.DMA((heads,)),
+            pltpu.SemaphoreType.DMA((count * heads,)),
         ],
         FULL,
     )(*arrays)
@@ -220,18 +221,15 @@
     blocks, lanes, slot_ref, third_ref, near_ref, kv_ref, qg_ref, edge_ref, cross, main, *refs
 ):
     thirds = refs[:lanes]
-    out, sums, edge_out, main_out, third_out = refs[lanes : lanes + 5]
-    far_ref, out_ref, sum_ref, far_out, far_sems, done_sems, leave_sems = refs[lanes + 5 :]
+    out, sum_ref, edge_out, main_out, third_out = refs[lanes : lanes + 5]
+    far_ref, out_ref, far_out, far_sems, done_sems, leave_sems = refs[lanes + 5 :]
     bf16 = jnp.bfloat16
 
     def arrive(r, slot):
         return pltpu.make_async_copy(main.at[slot], far_ref.at[r], far_sems.at[r])
 
     def finished(n):
-        return pltpu.make_async_copy(out_ref.at[n], out.at[n], done_sems.at[0, n])
-
-    def summed(n):
-        return pltpu.make_async_copy(sum_ref.at[n], sums.at[n], done_sems.at[1, n])
+        return pltpu.make_async_copy(out_ref.at[n], out.at[n], done_sems.at[n])
 
     def leave(r, slot):
         return pltpu.make_async_copy(far_out.at[r], main_out.at[slot], leave_sems.at[r])
@@ -285,17 +283,15 @@
             far_out[r2, which] = d[2 * BLOCK : 3 * BLOCK].astype(bf16)
             far_out[r3, which] = d[3 * BLOCK :].astype(bf16)
 
-    def sent(n, first):
+    def sent(n):
         finished(n).start()
-        if not first:
-            summed(n - 1).start()
         for r in (2 * n, 2 * n + 1):
             when_main(r, lambda r, slot: leave(r, slot).start())
 
     group = 3
     ready(0)
     one(0, True)
-    sent(0, True)
+    sent(0)
 
     def several(at, _):
         first = 1 + at * group
@@ -304,20 +300,18 @@
         for i in range(group):
             one(first + i, False)
         for i in range(group):
-            sent(first + i, False)
+            sent(first + i)
 
     lax.fori_loop(0, (blocks - 1) // group, several, None)
     for n in range(1 + (blocks - 1) // group * group, blocks):
         ready(n)
         one(n, False)
-        sent(n, False)
-    summed(blocks - 1).start()
+        sent(n)
     for j in range(2):
         third_out[j] = far_out[third_ref[j]]
 
     def finish(n, _):
         finished(n).wait()
-        summed(n).wait()
         for r in (2 * n, 2 * n + 1):
             when_main(r, lambda r, slot: leave(r, slot).wait())
 
@@ -332,29 +326,28 @@
         functools.partial(attend_kernel, blocks, lanes),
         (
             pltpu.HBM(qg.shape, bf16),
-            pltpu.HBM(kv.shape, f32),
+            jax.ShapeDtypeStruct(kv.shape, f32),
             jax.ShapeDtypeStruct(edge.shape, bf16),
             pltpu.HBM(main.shape, bf16),
             jax.ShapeDtypeStruct(cross.shape, bf16),
         ),
         [SMEM] * 3 + [VMEM] * 3 + [ANY] * (2 + lanes),
-        (ANY, ANY, VMEM, ANY, VMEM),
+        (ANY, VMEM, VMEM, ANY, VMEM),
         "attend",
         5 * 2 * blocks * 4 * BLOCK * BLOCK * HEAD_DIM,
         2 * (6 * kv.size + 2 * main.size),
         [
             pltpu.VMEM(far, bf16),
             pltpu.VMEM(qg.shape, bf16),
-            pltpu.VMEM(kv.shape, f32),
             pltpu.VMEM(far, bf16),
             pltpu.SemaphoreType.DMA((2 * blocks,)),
-            pltpu.SemaphoreType.DMA((2, blocks)),
+            pltpu.SemaphoreType.DMA((blocks,)),
             pltpu.SemaphoreType.DMA((2 * blocks,)),
         ],
     )(slot, third, near, kv, qg, edge, cross, main, *thirds)
 
 
-def land_kernel(blocks, slots, main_ref, sum_ref, edge_ref, home_ref, total):
+def land_kernel(blocks, slots, main_ref, sum_ref, edge_ref, home_ref, total, low):
     f32 = jnp.float32
     total[...] = sum_ref[...]
     total[blocks - 1] += edge_ref[...].astype(f32)
@@ -365,71 +358,81 @@
         def _():
             total[row] += home_ref[slot].astype(f32)
 
+    low[...] = total[...].astype(low.dtype)
+
 
 def land(main_index, sums, edge, home):
     blocks, slots = sums.shape[0], home.shape[0]
     return call(
         functools.partial(land_kernel, blocks, slots),
-        jax.ShapeDtypeStruct(sums.shape, jnp.float32),
+        (pltpu.HBM(sums.shape, jnp.float32), pltpu.HBM(sums.shape, home.dtype)),
         [SMEM] + [VMEM] * 3,
-        VMEM,
+        (VMEM, VMEM),
         "land",
         sums.size * 2,
         12 * sums.size,
     )(main_index, sums, edge, home)
 
 
-def land_thirds_kernel(blocks, lanes, third_ref, total, *refs):
+def land_thirds_kernel(lanes, third_ref, once_ref, total, _, *refs):
     thirds, out = refs[:lanes], refs[lanes]
-    held, low, in_sems, sems, late, late_sems = refs[lanes + 1 :]
-    reads = [pltpu.make_async_copy(total.at[n], held.at[n], in_sems.at[n]) for n in range(blocks)]
-    writes = [pltpu.make_async_copy(low.at[n], out.at[n], sems.at[n]) for n in range(blocks)]
-    start_all(reads)
+    held, low, late, in_sems, late_sems, sems = refs[lanes + 1 :]
+
+    def read(at):
+        row = once_ref[at]
+        return pltpu.make_async_copy(total.at[row], held.at[row], in_sems.at[at])
 
     def arrive(at):
         step, side = divmod(at, 2)
         return pltpu.make_async_copy(thirds[step].at[side], late.at[at], late_sems.at[at])
 
-    for at in range(2 * lanes):
-
-        @pl.when(third_ref[at] >= 0)
-        def _():
-            arrive(at).start()
-
-    wait_all(reads)
-    for at in range(2 * lanes):
-
-        @pl.when(third_ref[at] >= 0)
-        def _():
-            arrive(at).wait()
-            held[third_ref[at]] += late[at].astype(jnp.float32)
-
-    for n in range(blocks):
-        low[n] = held[n].astype(low.dtype)
-        writes[n].start()
-    wait_all(writes)
-
-
-def land_thirds(third_index, total, thirds):
-    blocks, lanes = total.shape[0], len(thirds)
-    dtype = thirds[0].dtype
-    return call(
-        functools.partial(land_thirds_kernel, blocks, lanes),
-        pltpu.HBM(total.shape, dtype),
-        [SMEM] + [ANY] * (1 + lanes),
+    def write(at):
+        row = once_ref[at]
+        return pltpu.make_async_copy(low.at[row], out.at[row], sems.at[at])
+
+    def add(at):
+        held[third_ref[at]] += late[at].astype(jnp.float32)
+
+    def put(at):
+        row = once_ref[at]
+        low[row] = held[row].astype(low.dtype)
+        write(at).start()
+
+    stages = (
+        (third_ref, lambda at: arrive(at).start()),
+        (once_ref, lambda at: read(at).start()),
+        (third_ref, lambda at: arrive(at).wait()),
+        (once_ref, lambda at: read(at).wait()),
+        (third_ref, add),
+        (once_ref, put),
+        (once_ref, lambda at: write(at).wait()),
+    )
+    for table, do in stages:
+        for at in range(2 * lanes):
+            pl.when(table[at] >= 0)(functools.partial(do, at))
+
+
+def land_thirds(third_index, once, total, low, thirds):
+    lanes = len(thirds)
+    dtype = low.dtype
+    return call(
+        functools.partial(land_thirds_kernel, lanes),
+        pltpu.HBM(low.shape, dtype),
+        [SMEM] * 2 + [ANY] * (2 + lanes),
         ANY,
         "land_thirds",
         total.size,
-        6 * total.size,
+        total.size,
         [
             pltpu.VMEM(total.shape, jnp.float32),
-            pltpu.VMEM(total.shape, dtype),
-            pltpu.SemaphoreType.DMA((blocks,)),
-            pltpu.SemaphoreType.DMA((blocks,)),
-            pltpu.VMEM((2 * lanes,) + total.shape[1:], dtype),
+            pltpu.VMEM(low.shape, dtype),
+            pltpu.VMEM((2 * lanes,) + low.shape[1:], dtype),
+            pltpu.SemaphoreType.DMA((2 * lanes,)),
+            pltpu.SemaphoreType.DMA((2 * lanes,)),
             pltpu.SemaphoreType.DMA((2 * lanes,)),
         ],
-    )(third_index, total, *thirds)
+        aliases={3: 0},
+    )(third_index, once, total, low, *thirds)
 
 
 def plan(key_lists, blocks, ctx_count, lanes):
@@ -472,14 +475,17 @@
         return jnp.where(slab // lanes == half, (lane - slab % lanes + lanes) % lanes, -1)
 
     partner = (me + lanes) % ctx_count
-    return main_index, third_index, my_slot, row(me, third_request), steps(me), steps(partner)
+    places = jnp.arange(2 * lanes, dtype=i32)
+    same = (third_index[:, None] == third_index[None, :]) & (places[None, :] < places[:, None])
+    once = jnp.where(jnp.any(same, axis=1), -1, third_index)
+    return main_index, third_index, once, my_slot, row(me, third_request), steps(me), steps(partner)
 
 
 def body(queries, keys, values, out_grad, key_lists):
     ctx_count = lax.axis_size("ctx")
     blocks = lax.axis_size("head")
     lanes = ctx_count // 2
-    main_index, third_index, my_slot, my_third, near_steps, cross_steps = plan(
+    main_index, third_index, once, my_slot, my_third, near_steps, cross_steps = plan(
         key_lists, blocks, ctx_count, lanes
     )
 
@@ -507,8 +513,8 @@
     edge = move(edge, lambda i: (i + 1) % ctx_count)
     thirds = along(thirds, 1)
     thirds[1], packed = lax.optimization_barrier((thirds[1], pack(main_index, kv)))
-    cross = across(pick_cross(cross_steps, thirds))
-    packed, edge, cross = lax.optimization_barrier((packed, edge, cross))
+    packed, edge, cross = lax.optimization_barrier((packed, edge, pick_cross(cross_steps, thirds)))
+    cross = across(cross)
     main = ctx_exchange(packed)
     out, sums, edge_grad, main_grad, third_grad = attend(
         my_slot, my_third, near_steps, kv, qg, edge, cross, main, thirds
@@ -519,11 +525,11 @@
     out, home, cross_grad, edge_grad = lax.optimization_barrier((out, home, cross_grad, edge_grad))
     out = head_exchange(out)
     late = along(pick_back(near_steps, cross_steps, third_grad, cross_grad, lanes), -1)
-    total = land(main_index, sums, edge_grad, home)
-    total, out = lax.optimization_barrier((total, out))
-    total = land_thirds(third_index, total, late)
+    total, low = land(main_index, sums, edge_grad, home)
+    total, low, out = lax.optimization_barrier((total, low, out))
+    low = land_thirds(third_index, once, total, low, late)
     attended, query_grad = join_heads(out)
-    key_grad, value_grad = join_heads(head_exchange(total))
+    key_grad, value_grad = join_heads(head_exchange(low))
     return attended, query_grad, key_grad, value_grad
 
 

time: 281 us -> 283 us (level); the launches traced: 280 us -> 279 us
    all_to_all x2, waiting for transfers between devices: 51.3 us -> 3.68 us  [ctx_exchange(): return lax.all_to_all(array, 'ctx', split_axis=0, concat_axis=0, tiled=True)]
    ppermute x18, waiting for transfers between devices: 67.6 us -> 106 us  [move(): lax.ppermute(array, 'ctx', [(i, target(i)) for i in range(ctx_count)])]
    all_to_all x4, waiting for transfers between devices: 52.9 us -> 60.2 us  [head_exchange(): lax.all_to_all(array, 'head', split_axis=0, concat_axis=0, tiled=True)]
    ppermute x18, starting transfers between devices: 27.3 us -> 31.7 us  [move(): lax.ppermute(array, 'ctx', [(i, target(i)) for i in range(ctx_count)])]
    all_to_all x2, starting transfers between devices: 18.6 us -> 15 us  [ctx_exchange(): return lax.all_to_all(array, 'ctx', split_axis=0, concat_axis=0, tiled=True)]
  transfers between devices with their start and end apart: 24 -> 24, of which waited for: 13 -> 14; matrix products, arithmetic and copies ran while one was open for 1% -> 1% of each run, Pallas kernels for 4% -> 4%
where the time goes in v4:
time: 283 us; the launch traced here: 279 us
  waiting for transfers between devices  170 us (60%)
  starting transfers between devices  70.9 us (25%)
  Pallas kernels  33.9 us (12%)
    ppermute x18, waiting for transfers between devices, move(): lax.ppermute(array, 'ctx', [(i, target(i)) for i in range(ctx_count)])  106 us
    all_to_all x4, waiting for transfers between devices, head_exchange(): lax.all_to_all(array, 'head', split_axis=0, concat_axis=0, tiled=True)  60.2 us
    ppermute x18, starting transfers between devices, move(): lax.ppermute(array, 'ctx', [(i, target(i)) for i in range(ctx_count)])  31.7 us
    all_to_all x4, starting transfers between devices, head_exchange(): lax.all_to_all(array, 'head', split_axis=0, concat_axis=0, tiled=True)  24.2 us
    all_to_all x2, starting transfers between devices, ctx_exchange(): return lax.all_to_all(array, 'ctx', split_axis=0, concat_axis=0, tiled=True)  15 us
    pallas_call x1, Pallas kernels, attend(): call(functools.partial(attend_kernel, blocks, lanes), (pltpu.HBM(qg.shape...  14.9 us
  transfers between devices with their start and end apart: 24, of which 14 were waited for; matrix products, arithmetic and copies ran while one was open for 1% of the time, Pallas kernels for 4%

profile of v4, /device:TPU:56, one launch (start us, length us, event | category | flops | bytes accessed | tf_op | source)
XLA Modules:
  0.0 279.3 jit_solution(7113044003473473178)
XLA Ops:
  0.6 2.4 split_heads.2
  3.1 8.5 %all-to-all-start = ((bf16[16,2,128,128]{3,2,1,0:T(8,128)(2,1)}), bf16[16,2,128,128]{3,2,1,0:T(8,128)(2,1)S(1)}, u32[]{:S(2)}, u32[]{:S(2)}) async-start(bf16[16,2,128,128]{3,2,1,0:T(8,128)(2,1)} %split_heads.2), calls=%async_computation | async-start | bytes 2097152 | tf_op jit(solution)/shard_map/all_to_all | solution.py:493
  12.5 2.4 split_heads.3
  14.8 22.5 %all-to-all-done.kv_ref.in_ref = bf16[16,2,128,128]{3,2,1,0:T(8,128)(2,1)S(1)} async-done(((bf16[16,2,128,128]{3,2,1,0:T(8,128)(2,1)}), bf16[16,2,128,128]{3,2,1,0:T(8,128)(2,1)S(1)}, u32[]{:S(2)}, u32[]{:S(2)}) %all-to-all-start) | async-done | bytes 1048608 | tf_op jit(solution)/shard_map/all_to_all | solution.py:493
  37.3 5.2 %all-to-all-start.1 = ((bf16[16,2,128,128]{3,2,1,0:T(8,128)(2,1)}), bf16[16,2,128,128]{3,2,1,0:T(8,128)(2,1)}, u32[]{:S(2)}, u32[]{:S(2)}) async-start(bf16[16,2,128,128]{3,2,1,0:T(8,128)(2,1)} %split_heads.3), calls=%async_computation.1 | async-start | bytes 2097152 | tf_op jit(solution)/shard_map/all_to_all | solution.py:493
  45.0 2.5 collective-permute-start.3
  54.2 2.1 pack.1
  60.8 6.5 %all-to-all-done.1.qg_ref = bf16[16,2,128,128]{3,2,1,0:T(8,128)(2,1)} async-done(((bf16[16,2,128,128]{3,2,1,0:T(8,128)(2,1)}), bf16[16,2,128,128]{3,2,1,0:T(8,128)(2,1)}, u32[]{:S(2)}, u32[]{:S(2)}) %all-to-all-start.1) | async-done | bytes 1048608 | tf_op jit(solution)/shard_map/all_to_all | solution.py:493
  67.4 9.8 %all-to-all-start.2 = ((bf16[32,2,128,128]{3,2,1,0:T(8,128)(2,1)}), bf16[32,2,128,128]{3,2,1,0:T(8,128)(2,1)}, u32[]{:S(2)}, u32[]{:S(2)}) async-start(bf16[32,2,128,128]{3,2,1,0:T(8,128)(2,1)} %pack.1), calls=%async_computation.2 | async-start | bytes 4194304 | tf_op jit(solution)/shard_map/all_to_all | solution.py:496
  77.1 5.4 %collective-permute-start.8 = (bf16[2,2,128,128]{3,2,1,0:T(8,128)(2,1)S(1)}, bf16[2,2,128,128]{3,2,1,0:T(8,128)(2,1)S(1)}, u32[]{:S(2)}, u32[]{:S(2)}) collective-permute-start(bf16[2,2,128,128]{3,2,1,0:T(8,128)(2,1)S(1)} %pick_cross.1), channel_id=1, source_target_pairs={{0,128},{16,144},{32,160},{48,176},{64,192},{80,208},{96,224},{112... | collective-permute-start | bytes 393224 | tf_op jit(solution)/shard_map/ppermute | solution.py:499
  82.6 50.6 %collective-permute-done.8.cross = bf16[2,2,128,128]{3,2,1,0:T(8,128)(2,1)S(1)} collective-permute-done((bf16[2,2,128,128]{3,2,1,0:T(8,128)(2,1)S(1)}, bf16[2,2,128,128]{3,2,1,0:T(8,128)(2,1)S(1)}, u32[]{:S(2)}, u32[]{:S(2)}) %collective-permute-start.8) | collective-permute-done | bytes 131104 | tf_op jit(solution)/shard_map/ppermute | solution.py:499
  134.4 14.9 %attend.1 = (bf16[16,2,128,128]{3,2,1,0:T(8,128)(2,1)}, f32[16,2,128,128]{3,2,1,0:T(8,128)}, bf16[2,128,128]{2,1,0:T(8,128)(2,1)S(1)}, bf16[32,2,128,128]{3,2,1,0:T(8,128)(2,1)}, bf16[2,2,128,128]{3,2,1,0:T(8,128)(2,1)S(1)}) custom-call(s32[32]{0:T(128)S(1)} %select_reduce_fusion.4.slot_ref, s32[2]{0:T(128)S(1)} %get-tuple-element.88.third_ref, ...), custom_call_target="tpu_custom_call" | custom-call | flops 1342177280 | bytes 10485760 | tf_op jit(solution)/shard_map/attend/pallas_call | solution.py:325
  149.3 5.2 %all-to-all-start.3 = ((bf16[32,2,128,128]{3,2,1,0:T(8,128)(2,1)}), bf16[32,2,128,128]{3,2,1,0:T(8,128)(2,1)}, u32[]{:S(2)}, u32[]{:S(2)}) async-start(bf16[32,2,128,128]{3,2,1,0:T(8,128)(2,1)} %get-tuple-element.60), calls=%async_computation.3 | async-start | bytes 4194304 | tf_op jit(solution)/shard_map/all_to_all | solution.py:496
  154.5 5.5 %collective-permute-start.9 = (bf16[2,2,128,128]{3,2,1,0:T(8,128)(2,1)S(1)}, bf16[2,2,128,128]{3,2,1,0:T(8,128)(2,1)S(1)}, u32[]{:S(2)}, u32[]{:S(2)}) collective-permute-start(bf16[2,2,128,128]{3,2,1,0:T(8,128)(2,1)S(1)} %get-tuple-element.61.own), channel_id=1, source_target_pairs={{0,128},{16,144},{32,160},{48,176},{64,192},{80,208},{96,224},{112... | collective-permute-start | bytes 393224 | tf_op jit(solution)/shard_map/ppermute | solution.py:499
  160.3 7.1 %collective-permute-done.10.edge_ref = bf16[2,128,128]{2,1,0:T(8,128)(2,1)S(1)} collective-permute-done((bf16[2,128,128]{2,1,0:T(8,128)(2,1)S(1)}, bf16[2,128,128]{2,1,0:T(8,128)(2,1)S(1)}, u32[]{:S(2)}, u32[]{:S(2)}) %collective-permute-start.10) | collective-permute-done | bytes 65568 | tf_op jit(solution)/shard_map/ppermute | solution.py:499
  167.4 42.8 %collective-permute-done.9.crossed = bf16[2,2,128,128]{3,2,1,0:T(8,128)(2,1)S(1)} collective-permute-done((bf16[2,2,128,128]{3,2,1,0:T(8,128)(2,1)S(1)}, bf16[2,2,128,128]{3,2,1,0:T(8,128)(2,1)S(1)}, u32[]{:S(2)}, u32[]{:S(2)}) %collective-permute-start.9) | collective-permute-done | bytes 131104 | tf_op jit(solution)/shard_map/ppermute | solution.py:499
  210.2 2.5 all-to-all-done.3.home_ref
  212.7 4.9 %all-to-all-start.4 = ((bf16[16,2,128,128]{3,2,1,0:T(8,128)(2,1)}), bf16[16,2,128,128]{3,2,1,0:T(8,128)(2,1)S(1)}, u32[]{:S(2)}, u32[]{:S(2)}) async-start(bf16[16,2,128,128]{3,2,1,0:T(8,128)(2,1)} %get-tuple-element.67), calls=%async_computation.4 | async-start | bytes 2097152 | tf_op jit(solution)/shard_map/all_to_all | solution.py:493
  219.2 5.5 %collective-permute-start.12 = (bf16[2,2,128,128]{3,2,1,0:T(8,128)(2,1)S(1)}, bf16[2,2,128,128]{3,2,1,0:T(8,128)(2,1)S(1)}, u32[]{:S(2)}, u32[]{:S(2)}) collective-permute-start(bf16[2,2,128,128]{3,2,1,0:T(8,128)(2,1)S(1)} %get-tuple-element.76), channel_id=1, source_target_pairs={{0,96},{16,112},{32,0},{48,16},{64,32},{80,48},{96,64},{112,80},{1... | collective-permute-start | bytes 393224 | tf_op jit(solution)/shard_map/ppermute | solution.py:499
  233.1 3.9 %land.1 = (f32[16,2,128,128]{3,2,1,0:T(8,128)}, bf16[16,2,128,128]{3,2,1,0:T(8,128)(2,1)}) custom-call(s32[32]{0:T(128)S(1)} %select_n.147.index_ref.main_ref, f32[16,2,128,128]{3,2,1,0:T(8,128)S(1)} %copy-done, bf16[2,128,128]{2,1,0:T(8,128)(2,1)S(1)} %copy-done.2, bf16[32,2,128,128]{3,2,1,0:T(8,128)(2,1)} %all-to-all-done.3.home_ref), custom_call_target="tpu_custom_call" | custom-call | flops 1048576 | bytes 6291456 | tf_op jit(solution)/shard_map/land/pallas_call | solution.py:366
  237.0 6.0 %all-to-all-done.4.in_ref = bf16[16,2,128,128]{3,2,1,0:T(8,128)(2,1)S(1)} async-done(((bf16[16,2,128,128]{3,2,1,0:T(8,128)(2,1)}), bf16[16,2,128,128]{3,2,1,0:T(8,128)(2,1)S(1)}, u32[]{:S(2)}, u32[]{:S(2)}) %all-to-all-start.4) | async-done | bytes 1048608 | tf_op jit(solution)/shard_map/all_to_all | solution.py:493
  243.1 3.0 %land_thirds.1 = bf16[16,2,128,128]{3,2,1,0:T(8,128)(2,1)} custom-call(s32[16]{0:T(128)S(1)} %reshape.202.third_ref, s32[16]{0:T(128)S(1)} %broadcast_select_fusion.1.once_ref, f32[16,2,128,128]{3,2,1,0:T(8,128)} %get-tuple-element.71.total, bf16[16,2,128,128]{3,2,1,0:T(8,128)(2,1)} %get-tuple-element.72._, ...), custom_call_target="tpu_custom_call", output_to_operand_aliasing={{}: (3, {})} | custom-call | flops 524288 | bytes 524288 | tf_op jit(solution)/shard_map/land_thirds/pallas_call | solution.py:418
  246.0 5.6 %all-to-all-start.5 = ((bf16[16,2,128,128]{3,2,1,0:T(8,128)(2,1)}), bf16[16,2,128,128]{3,2,1,0:T(8,128)(2,1)S(1)}, u32[]{:S(2)}, u32[]{:S(2)}) async-start(bf16[16,2,128,128]{3,2,1,0:T(8,128)(2,1)} %land_thirds.1), calls=%async_computation.5 | async-start | bytes 2097152 | tf_op jit(solution)/shard_map/all_to_all | solution.py:493
  252.8 25.3 %all-to-all-done.5.in_ref = bf16[16,2,128,128]{3,2,1,0:T(8,128)(2,1)S(1)} async-done(((bf16[16,2,128,128]{3,2,1,0:T(8,128)(2,1)}), bf16[16,2,128,128]{3,2,1,0:T(8,128)(2,1)S(1)}, u32[]{:S(2)}, u32[]{:S(2)}) %all-to-all-start.5) | async-done | bytes 1048608 | tf_op jit(solution)/shard_map/all_to_all | solution.py:493
  (74 shorter events, 28.3 us)
Async XLA Ops:
  3.1 34.2 %all-to-all-start = ((bf16[16,2,128,128]{3,2,1,0:T(8,128)(2,1)}), bf16[16,2,128,128]{3,2,1,0:T(8,128)(2,1)S(1)}, u32[]{:S(2)}, u32[]{:S(2)}) async-start(bf16[16,2,128,128]{3,2,1,0:T(8,128)(2,1)} %split_heads.2), calls=%async_computation | async-start | bytes 2097152 | tf_op jit(solution)/shard_map/all_to_all | solution.py:493
  37.3 30.1 %all-to-all-start.1 = ((bf16[16,2,128,128]{3,2,1,0:T(8,128)(2,1)}), bf16[16,2,128,128]{3,2,1,0:T(8,128)(2,1)}, u32[]{:S(2)}, u32[]{:S(2)}) async-start(bf16[16,2,128,128]{3,2,1,0:T(8,128)(2,1)} %split_heads.3), calls=%async_computation.1 | async-start | bytes 2097152 | tf_op jit(solution)/shard_map/all_to_all | solution.py:493
  44.7 6.1 %collective-permute-start = (bf16[2,2,128,128]{3,2,1,0:T(8,128)(2,1)S(1)}, bf16[2,2,128,128]{3,2,1,0:T(8,128)(2,1)S(1)}, u32[]{:S(2)}, u32[]{:S(2)}) collective-permute-start(bf16[2,2,128,128]{3,2,1,0:T(8,128)(2,1)S(1)} %get-tuple-element.44), channel_id=1, source_target_pairs={{0,16},{16,32},{32,48},{48,64},{64,80},{80,96},{96,112},{112,0},{1... | collective-permute-start | bytes 393224 | tf_op jit(solution)/shard_map/ppermute | solution.py:499
  44.7 6.4 %collective-permute-start.2 = (bf16[2,2,128,128]{3,2,1,0:T(8,128)(2,1)S(1)}, bf16[2,2,128,128]{3,2,1,0:T(8,128)(2,1)S(1)}, u32[]{:S(2)}, u32[]{:S(2)}) collective-permute-start(bf16[2,2,128,128]{3,2,1,0:T(8,128)(2,1)S(1)} %get-tuple-element.49), channel_id=1, source_target_pairs={{0,32},{16,48},{32,64},{48,80},{64,96},{80,112},{96,0},{112,16},{1... | collective-permute-start | bytes 393224 | tf_op jit(solution)/shard_map/ppermute | solution.py:499
  45.0 8.2 %collective-permute-start.3 = (bf16[2,2,128,128]{3,2,1,0:T(8,128)(2,1)S(1)}, bf16[2,2,128,128]{3,2,1,0:T(8,128)(2,1)S(1)}, u32[]{:S(2)}, u32[]{:S(2)}) collective-permute-start(bf16[2,2,128,128]{3,2,1,0:T(8,128)(2,1)S(1)} %get-tuple-element.50), channel_id=1, source_target_pairs={{0,48},{16,64},{32,80},{48,96},{64,112},{80,0},{96,16},{112,32},{1... | collective-permute-start | bytes 393224 | tf_op jit(solution)/shard_map/ppermute | solution.py:499
  47.6 8.7 %collective-permute-start.4 = (bf16[2,2,128,128]{3,2,1,0:T(8,128)(2,1)S(1)}, bf16[2,2,128,128]{3,2,1,0:T(8,128)(2,1)S(1)}, u32[]{:S(2)}, u32[]{:S(2)}) collective-permute-start(bf16[2,2,128,128]{3,2,1,0:T(8,128)(2,1)S(1)} %get-tuple-element.51), channel_id=1, source_target_pairs={{0,64},{16,80},{32,96},{48,112},{64,0},{80,16},{96,32},{112,48},{1... | collective-permute-start | bytes 393224 | tf_op jit(solution)/shard_map/ppermute | solution.py:499
  48.7 9.3 %collective-permute-start.5 = (bf16[2,2,128,128]{3,2,1,0:T(8,128)(2,1)S(1)}, bf16[2,2,128,128]{3,2,1,0:T(8,128)(2,1)S(1)}, u32[]{:S(2)}, u32[]{:S(2)}) collective-permute-start(bf16[2,2,128,128]{3,2,1,0:T(8,128)(2,1)S(1)} %get-tuple-element.52), channel_id=1, source_target_pairs={{0,80},{16,96},{32,112},{48,0},{64,16},{80,32},{96,48},{112,64},{1... | collective-permute-start | bytes 393224 | tf_op jit(solution)/shard_map/ppermute | solution.py:499
  50.8 9.1 %collective-permute-start.6 = (bf16[2,2,128,128]{3,2,1,0:T(8,128)(2,1)S(1)}, bf16[2,2,128,128]{3,2,1,0:T(8,128)(2,1)S(1)}, u32[]{:S(2)}, u32[]{:S(2)}) collective-permute-start(bf16[2,2,128,128]{3,2,1,0:T(8,128)(2,1)S(1)} %get-tuple-element.53), channel_id=1, source_target_pairs={{0,96},{16,112},{32,0},{48,16},{64,32},{80,48},{96,64},{112,80},{1... | collective-permute-start | bytes 393224 | tf_op jit(solution)/shard_map/ppermute | solution.py:499
  51.1 8.8 %collective-permute-start.7 = (bf16[2,2,128,128]{3,2,1,0:T(8,128)(2,1)S(1)}, bf16[2,2,128,128]{3,2,1,0:T(8,128)(2,1)S(1)}, u32[]{:S(2)}, u32[]{:S(2)}) collective-permute-start(bf16[2,2,128,128]{3,2,1,0:T(8,128)(2,1)S(1)} %get-tuple-element.54), channel_id=1, source_target_pairs={{0,112},{16,0},{32,16},{48,32},{64,48},{80,64},{96,80},{112,96},{1... | collective-permute-start | bytes 393224 | tf_op jit(solution)/shard_map/ppermute | solution.py:499
  53.2 7.6 %collective-permute-start.1 = (bf16[2,128,128]{2,1,0:T(8,128)(2,1)S(1)}, bf16[2,128,128]{2,1,0:T(8,128)(2,1)S(1)}, u32[]{:S(2)}, u32[]{:S(2)}) collective-permute-start(bf16[2,128,128]{2,1,0:T(8,128)(2,1)S(1)} %get-tuple-element.46), channel_id=1, source_target_pairs={{0,16},{16,32},{32,48},{48,64},{64,80},{80,96},{96,112},{112,128},... | collective-permute-start | bytes 196616 | tf_op jit(solution)/shard_map/ppermute | solution.py:499
  67.4 67.0 %all-to-all-start.2 = ((bf16[32,2,128,128]{3,2,1,0:T(8,128)(2,1)}), bf16[32,2,128,128]{3,2,1,0:T(8,128)(2,1)}, u32[]{:S(2)}, u32[]{:S(2)}) async-start(bf16[32,2,128,128]{3,2,1,0:T(8,128)(2,1)} %pack.1), calls=%async_computation.2 | async-start | bytes 4194304 | tf_op jit(solution)/shard_map/all_to_all | solution.py:496
  77.1 56.1 %collective-permute-start.8 = (bf16[2,2,128,128]{3,2,1,0:T(8,128)(2,1)S(1)}, bf16[2,2,128,128]{3,2,1,0:T(8,128)(2,1)S(1)}, u32[]{:S(2)}, u32[]{:S(2)}) collective-permute-start(bf16[2,2,128,128]{3,2,1,0:T(8,128)(2,1)S(1)} %pick_cross.1), channel_id=1, source_target_pairs={{0,128},{16,144},{32,160},{48,176},{64,192},{80,208},{96,224},{112... | collective-permute-start | bytes 393224 | tf_op jit(solution)/shard_map/ppermute | solution.py:499
  149.3 63.4 %all-to-all-start.3 = ((bf16[32,2,128,128]{3,2,1,0:T(8,128)(2,1)}), bf16[32,2,128,128]{3,2,1,0:T(8,128)(2,1)}, u32[]{:S(2)}, u32[]{:S(2)}) async-start(bf16[32,2,128,128]{3,2,1,0:T(8,128)(2,1)} %get-tuple-element.60), calls=%async_computation.3 | async-start | bytes 4194304 | tf_op jit(solution)/shard_map/all_to_all | solution.py:496
  154.5 55.7 %collective-permute-start.9 = (bf16[2,2,128,128]{3,2,1,0:T(8,128)(2,1)S(1)}, bf16[2,2,128,128]{3,2,1,0:T(8,128)(2,1)S(1)}, u32[]{:S(2)}, u32[]{:S(2)}) collective-permute-start(bf16[2,2,128,128]{3,2,1,0:T(8,128)(2,1)S(1)} %get-tuple-element.61.own), channel_id=1, source_target_pairs={{0,128},{16,144},{32,160},{48,176},{64,192},{80,208},{96,224},{112... | collective-permute-start | bytes 393224 | tf_op jit(solution)/shard_map/ppermute | solution.py:499
  160.0 7.4 %collective-permute-start.10 = (bf16[2,128,128]{2,1,0:T(8,128)(2,1)S(1)}, bf16[2,128,128]{2,1,0:T(8,128)(2,1)S(1)}, u32[]{:S(2)}, u32[]{:S(2)}) collective-permute-start(bf16[2,128,128]{2,1,0:T(8,128)(2,1)S(1)} %get-tuple-element.62), channel_id=1, source_target_pairs={{0,240},{16,0},{32,16},{48,32},{64,48},{80,64},{96,80},{112,96},{1... | collective-permute-start | bytes 196616 | tf_op jit(solution)/shard_map/ppermute | solution.py:499
  212.7 30.3 %all-to-all-start.4 = ((bf16[16,2,128,128]{3,2,1,0:T(8,128)(2,1)}), bf16[16,2,128,128]{3,2,1,0:T(8,128)(2,1)S(1)}, u32[]{:S(2)}, u32[]{:S(2)}) async-start(bf16[16,2,128,128]{3,2,1,0:T(8,128)(2,1)} %get-tuple-element.67), calls=%async_computation.4 | async-start | bytes 2097152 | tf_op jit(solution)/shard_map/all_to_all | solution.py:493
  219.2 9.6 %collective-permute-start.11 = (bf16[2,2,128,128]{3,2,1,0:T(8,128)(2,1)S(1)}, bf16[2,2,128,128]{3,2,1,0:T(8,128)(2,1)S(1)}, u32[]{:S(2)}, u32[]{:S(2)}) collective-permute-start(bf16[2,2,128,128]{3,2,1,0:T(8,128)(2,1)S(1)} %get-tuple-element.75), channel_id=1, source_target_pairs={{0,112},{16,0},{32,16},{48,32},{64,48},{80,64},{96,80},{112,96},{1... | collective-permute-start | bytes 393224 | tf_op jit(solution)/shard_map/ppermute | solution.py:499
  219.2 11.8 %collective-permute-start.12 = (bf16[2,2,128,128]{3,2,1,0:T(8,128)(2,1)S(1)}, bf16[2,2,128,128]{3,2,1,0:T(8,128)(2,1)S(1)}, u32[]{:S(2)}, u32[]{:S(2)}) collective-permute-start(bf16[2,2,128,128]{3,2,1,0:T(8,128)(2,1)S(1)} %get-tuple-element.76), channel_id=1, source_target_pairs={{0,96},{16,112},{32,0},{48,16},{64,32},{80,48},{96,64},{112,80},{1... | collective-permute-start | bytes 393224 | tf_op jit(solution)/shard_map/ppermute | solution.py:499
  224.9 18.1 %collective-permute-start.13 = (bf16[2,2,128,128]{3,2,1,0:T(8,128)(2,1)}, bf16[2,2,128,128]{3,2,1,0:T(8,128)(2,1)}, u32[]{:S(2)}, u32[]{:S(2)}) collective-permute-start(bf16[2,2,128,128]{3,2,1,0:T(8,128)(2,1)} %get-tuple-element.77), channel_id=1, source_target_pairs={{0,80},{16,96},{32,112},{48,0},{64,16},{80,32},{96,48},{112,64},{1... | collective-permute-start | bytes 393224 | tf_op jit(solution)/shard_map/ppermute | solution.py:499
  226.5 16.5 %collective-permute-start.14 = (bf16[2,2,128,128]{3,2,1,0:T(8,128)(2,1)}, bf16[2,2,128,128]{3,2,1,0:T(8,128)(2,1)}, u32[]{:S(2)}, u32[]{:S(2)}) collective-permute-start(bf16[2,2,128,128]{3,2,1,0:T(8,128)(2,1)} %get-tuple-element.78), channel_id=1, source_target_pairs={{0,64},{16,80},{32,96},{48,112},{64,0},{80,16},{96,32},{112,48},{1... | collective-permute-start | bytes 393224 | tf_op jit(solution)/shard_map/ppermute | solution.py:499
  226.9 16.1 %collective-permute-start.15 = (bf16[2,2,128,128]{3,2,1,0:T(8,128)(2,1)}, bf16[2,2,128,128]{3,2,1,0:T(8,128)(2,1)}, u32[]{:S(2)}, u32[]{:S(2)}) collective-permute-start(bf16[2,2,128,128]{3,2,1,0:T(8,128)(2,1)} %get-tuple-element.79), channel_id=1, source_target_pairs={{0,48},{16,64},{32,80},{48,96},{64,112},{80,0},{96,16},{112,32},{1... | collective-permute-start | bytes 393224 | tf_op jit(solution)/shard_map/ppermute | solution.py:499
  228.9 14.2 %collective-permute-start.16 = (bf16[2,2,128,128]{3,2,1,0:T(8,128)(2,1)}, bf16[2,2,128,128]{3,2,1,0:T(8,128)(2,1)}, u32[]{:S(2)}, u32[]{:S(2)}) collective-permute-start(bf16[2,2,128,128]{3,2,1,0:T(8,128)(2,1)} %get-tuple-element.80), channel_id=1, source_target_pairs={{0,32},{16,48},{32,64},{48,80},{64,96},{80,112},{96,0},{112,16},{1... | collective-permute-start | bytes 393224 | tf_op jit(solution)/shard_map/ppermute | solution.py:499
  231.1 12.0 %collective-permute-start.17 = (bf16[2,2,128,128]{3,2,1,0:T(8,128)(2,1)}, bf16[2,2,128,128]{3,2,1,0:T(8,128)(2,1)}, u32[]{:S(2)}, u32[]{:S(2)}) collective-permute-start(bf16[2,2,128,128]{3,2,1,0:T(8,128)(2,1)} %get-tuple-element.81), channel_id=1, source_target_pairs={{0,16},{16,32},{32,48},{48,64},{64,80},{80,96},{96,112},{112,0},{1... | collective-permute-start | bytes 393224 | tf_op jit(solution)/shard_map/ppermute | solution.py:499
  246.0 32.0 %all-to-all-start.5 = ((bf16[16,2,128,128]{3,2,1,0:T(8,128)(2,1)}), bf16[16,2,128,128]{3,2,1,0:T(8,128)(2,1)S(1)}, u32[]{:S(2)}, u32[]{:S(2)}) async-start(bf16[16,2,128,128]{3,2,1,0:T(8,128)(2,1)} %land_thirds.1), calls=%async_computation.5 | async-start | bytes 2097152 | tf_op jit(solution)/shard_map/all_to_all | solution.py:493
  (4 other events, 134.8 us)

commit v5 on v4

--- a/solution.py
+++ b/solution.py
@@ -221,15 +221,18 @@
     blocks, lanes, slot_ref, third_ref, near_ref, kv_ref, qg_ref, edge_ref, cross, main, *refs
 ):
     thirds = refs[:lanes]
-    out, sum_ref, edge_out, main_out, third_out = refs[lanes : lanes + 5]
-    far_ref, out_ref, far_out, far_sems, done_sems, leave_sems = refs[lanes + 5 :]
+    out, sums, edge_out, main_out, third_out = refs[lanes : lanes + 5]
+    far_ref, out_ref, sum_ref, far_out, far_sems, done_sems, leave_sems = refs[lanes + 5 :]
     bf16 = jnp.bfloat16
 
     def arrive(r, slot):
         return pltpu.make_async_copy(main.at[slot], far_ref.at[r], far_sems.at[r])
 
     def finished(n):
-        return pltpu.make_async_copy(out_ref.at[n], out.at[n], done_sems.at[n])
+        return pltpu.make_async_copy(out_ref.at[n], out.at[n], done_sems.at[0, n])
+
+    def summed(n):
+        return pltpu.make_async_copy(sum_ref.at[n], sums.at[n], done_sems.at[1, n])
 
     def leave(r, slot):
         return pltpu.make_async_copy(far_out.at[r], main_out.at[slot], leave_sems.at[r])
@@ -283,15 +286,17 @@
             far_out[r2, which] = d[2 * BLOCK : 3 * BLOCK].astype(bf16)
             far_out[r3, which] = d[3 * BLOCK :].astype(bf16)
 
-    def sent(n):
+    def sent(n, first):
         finished(n).start()
+        if not first:
+            summed(n - 1).start()
         for r in (2 * n, 2 * n + 1):
             when_main(r, lambda r, slot: leave(r, slot).start())
 
-    group = 3
+    group = 5
     ready(0)
     one(0, True)
-    sent(0)
+    sent(0, True)
 
     def several(at, _):
         first = 1 + at * group
@@ -300,18 +305,20 @@
         for i in range(group):
             one(first + i, False)
         for i in range(group):
-            sent(first + i)
+            sent(first + i, False)
 
     lax.fori_loop(0, (blocks - 1) // group, several, None)
     for n in range(1 + (blocks - 1) // group * group, blocks):
         ready(n)
         one(n, False)
-        sent(n)
+        sent(n, False)
+    summed(blocks - 1).start()
     for j in range(2):
         third_out[j] = far_out[third_ref[j]]
 
     def finish(n, _):
         finished(n).wait()
+        summed(n).wait()
         for r in (2 * n, 2 * n + 1):
             when_main(r, lambda r, slot: leave(r, slot).wait())
 
@@ -326,22 +333,23 @@
         functools.partial(attend_kernel, blocks, lanes),
         (
             pltpu.HBM(qg.shape, bf16),
-            jax.ShapeDtypeStruct(kv.shape, f32),
+            pltpu.HBM(kv.shape, f32),
             jax.ShapeDtypeStruct(edge.shape, bf16),
             pltpu.HBM(main.shape, bf16),
             jax.ShapeDtypeStruct(cross.shape, bf16),
         ),
         [SMEM] * 3 + [VMEM] * 3 + [ANY] * (2 + lanes),
-        (ANY, VMEM, VMEM, ANY, VMEM),
+        (ANY, ANY, VMEM, ANY, VMEM),
         "attend",
         5 * 2 * blocks * 4 * BLOCK * BLOCK * HEAD_DIM,
         2 * (6 * kv.size + 2 * main.size),
         [
             pltpu.VMEM(far, bf16),
             pltpu.VMEM(qg.shape, bf16),
+            pltpu.VMEM(kv.shape, f32),
             pltpu.VMEM(far, bf16),
             pltpu.SemaphoreType.DMA((2 * blocks,)),
-            pltpu.SemaphoreType.DMA((blocks,)),
+            pltpu.SemaphoreType.DMA((2, blocks)),
             pltpu.SemaphoreType.DMA((2 * blocks,)),
         ],
     )(slot, third, near, kv, qg, edge, cross, main, *thirds)
@@ -513,8 +521,8 @@
     edge = move(edge, lambda i: (i + 1) % ctx_count)
     thirds = along(thirds, 1)
     thirds[1], packed = lax.optimization_barrier((thirds[1], pack(main_index, kv)))
-    packed, edge, cross = lax.optimization_barrier((packed, edge, pick_cross(cross_steps, thirds)))
-    cross = across(cross)
+    cross = across(pick_cross(cross_steps, thirds))
+    packed, edge, cross = lax.optimization_barrier((packed, edge, cross))
     main = ctx_exchange(packed)
     out, sums, edge_grad, main_grad, third_grad = attend(
         my_slot, my_third, near_steps, kv, qg, edge, cross, main, thirds

time: 283 us -> 280 us (0.989); the launches traced: 279 us -> 280 us
    all_to_all x2, waiting for transfers between devices: 3.68 us -> 51.2 us  [ctx_exchange(): return lax.all_to_all(array, 'ctx', split_axis=0, concat_axis=0, tiled=True)]
    ppermute x18, waiting for transfers between devices: 106 us -> 67.3 us  [move(): lax.ppermute(array, 'ctx', [(i, target(i)) for i in range(ctx_count)])]
    all_to_all x4, waiting for transfers between devices: 60.2 us -> 50.6 us  [head_exchange(): lax.all_to_all(array, 'head', split_axis=0, concat_axis=0, tiled=True)]
    all_to_all x2, starting transfers between devices: 15 us -> 18.8 us  [ctx_exchange(): return lax.all_to_all(array, 'ctx', split_axis=0, concat_axis=0, tiled=True)]
    ppermute x18, starting transfers between devices: 31.7 us -> 28.2 us  [move(): lax.ppermute(array, 'ctx', [(i, target(i)) for i in range(ctx_count)])]
  transfers between devices with their start and end apart: 24 -> 24, of which waited for: 14 -> 13; matrix products, arithmetic and copies ran while one was open for 1% -> 1% of each run, Pallas kernels for 4% -> 4%
where the time goes in v5:
time: 280 us
  waiting for transfers between devices  169 us (60%)
  starting transfers between devices  72.9 us (26%)
  Pallas kernels  32.6 us (12%)
    ppermute x18, waiting for transfers between devices, move(): lax.ppermute(array, 'ctx', [(i, target(i)) for i in range(ctx_count)])  67.3 us
    all_to_all x2, waiting for transfers between devices, ctx_exchange(): return lax.all_to_all(array, 'ctx', split_axis=0, concat_axis=0, tiled=True)  51.2 us
    all_to_all x4, waiting for transfers between devices, head_exchange(): lax.all_to_all(array, 'head', split_axis=0, concat_axis=0, tiled=True)  50.6 us
    ppermute x18, starting transfers between devices, move(): lax.ppermute(array, 'ctx', [(i, target(i)) for i in range(ctx_count)])  28.2 us
    all_to_all x4, starting transfers between devices, head_exchange(): lax.all_to_all(array, 'head', split_axis=0, concat_axis=0, tiled=True)  26 us
    all_to_all x2, starting transfers between devices, ctx_exchange(): return lax.all_to_all(array, 'ctx', split_axis=0, concat_axis=0, tiled=True)  18.8 us
    pallas_call x1, Pallas kernels, attend(): call(functools.partial(attend_kernel, blocks, lanes), (pltpu.HBM(qg.shape...  13.8 us
  transfers between devices with their start and end apart: 24, of which 13 were waited for; matrix products, arithmetic and copies ran while one was open for 1% of the time, Pallas kernels for 4%

profile of v5, /device:TPU:56, one launch (start us, length us, event | category | flops | bytes accessed | tf_op | source)
XLA Modules:
  0.0 279.5 jit_solution(8204185417637279933)
XLA Ops:
  0.6 2.4 split_heads.2
  3.1 8.5 %all-to-all-start = ((bf16[16,2,128,128]{3,2,1,0:T(8,128)(2,1)}), bf16[16,2,128,128]{3,2,1,0:T(8,128)(2,1)S(1)}, u32[]{:S(2)}, u32[]{:S(2)}) async-start(bf16[16,2,128,128]{3,2,1,0:T(8,128)(2,1)} %split_heads.2), calls=%async_computation | async-start | bytes 2097152 | tf_op jit(solution)/shard_map/all_to_all | solution.py:501
  12.5 2.4 split_heads.3
  15.1 22.2 %all-to-all-done.kv_ref.in_ref = bf16[16,2,128,128]{3,2,1,0:T(8,128)(2,1)S(1)} async-done(((bf16[16,2,128,128]{3,2,1,0:T(8,128)(2,1)}), bf16[16,2,128,128]{3,2,1,0:T(8,128)(2,1)S(1)}, u32[]{:S(2)}, u32[]{:S(2)}) %all-to-all-start) | async-done | bytes 1048608 | tf_op jit(solution)/shard_map/all_to_all | solution.py:501
  37.3 5.2 %all-to-all-start.1 = ((bf16[16,2,128,128]{3,2,1,0:T(8,128)(2,1)}), bf16[16,2,128,128]{3,2,1,0:T(8,128)(2,1)}, u32[]{:S(2)}, u32[]{:S(2)}) async-start(bf16[16,2,128,128]{3,2,1,0:T(8,128)(2,1)} %split_heads.3), calls=%async_computation.1 | async-start | bytes 2097152 | tf_op jit(solution)/shard_map/all_to_all | solution.py:501
  45.1 2.6 collective-permute-start.3
  50.8 2.2 collective-permute-start.7
  55.5 2.5 collective-permute-done.5.refs_5_
  60.5 4.6 %collective-permute-start.8 = (bf16[2,2,128,128]{3,2,1,0:T(8,128)(2,1)S(1)}, bf16[2,2,128,128]{3,2,1,0:T(8,128)(2,1)S(1)}, u32[]{:S(2)}, u32[]{:S(2)}) collective-permute-start(bf16[2,2,128,128]{3,2,1,0:T(8,128)(2,1)S(1)} %pick_cross.1), channel_id=1, source_target_pairs={{0,128},{16,144},{32,160},{48,176},{64,192},{80,208},{96,224},{112... | collective-permute-start | bytes 393224 | tf_op jit(solution)/shard_map/ppermute | solution.py:507
  69.8 12.5 %all-to-all-start.2 = ((bf16[32,2,128,128]{3,2,1,0:T(8,128)(2,1)}), bf16[32,2,128,128]{3,2,1,0:T(8,128)(2,1)}, u32[]{:S(2)}, u32[]{:S(2)}) async-start(bf16[32,2,128,128]{3,2,1,0:T(8,128)(2,1)} %pack.1), calls=%async_computation.2 | async-start | bytes 4194304 | tf_op jit(solution)/shard_map/all_to_all | solution.py:504
  82.4 51.2 %all-to-all-done.2.main = bf16[32,2,128,128]{3,2,1,0:T(8,128)(2,1)} async-done(((bf16[32,2,128,128]{3,2,1,0:T(8,128)(2,1)}), bf16[32,2,128,128]{3,2,1,0:T(8,128)(2,1)}, u32[]{:S(2)}, u32[]{:S(2)}) %all-to-all-start.2) | async-done | bytes 2097184 | tf_op jit(solution)/shard_map/all_to_all | solution.py:504
  133.6 13.8 %attend.1 = (bf16[16,2,128,128]{3,2,1,0:T(8,128)(2,1)}, f32[16,2,128,128]{3,2,1,0:T(8,128)}, bf16[2,128,128]{2,1,0:T(8,128)(2,1)S(1)}, bf16[32,2,128,128]{3,2,1,0:T(8,128)(2,1)}, bf16[2,2,128,128]{3,2,1,0:T(8,128)(2,1)S(1)}) custom-call(s32[32]{0:T(128)S(1)} %select_reduce_fusion.4.slot_ref, s32[2]{0:T(128)S(1)} %get-tuple-element.88.third_ref, ...), custom_call_target="tpu_custom_call" | custom-call | flops 1342177280 | bytes 10485760 | tf_op jit(solution)/shard_map/attend/pallas_call | solution.py:332
  147.3 6.3 %all-to-all-start.3 = ((bf16[32,2,128,128]{3,2,1,0:T(8,128)(2,1)}), bf16[32,2,128,128]{3,2,1,0:T(8,128)(2,1)}, u32[]{:S(2)}, u32[]{:S(2)}) async-start(bf16[32,2,128,128]{3,2,1,0:T(8,128)(2,1)} %get-tuple-element.60), calls=%async_computation.3 | async-start | bytes 4194304 | tf_op jit(solution)/shard_map/all_to_all | solution.py:504
  153.6 5.6 %collective-permute-start.9 = (bf16[2,2,128,128]{3,2,1,0:T(8,128)(2,1)S(1)}, bf16[2,2,128,128]{3,2,1,0:T(8,128)(2,1)S(1)}, u32[]{:S(2)}, u32[]{:S(2)}) collective-permute-start(bf16[2,2,128,128]{3,2,1,0:T(8,128)(2,1)S(1)} %get-tuple-element.61.own), channel_id=1, source_target_pairs={{0,128},{16,144},{32,160},{48,176},{64,192},{80,208},{96,224},{112... | collective-permute-start | bytes 393224 | tf_op jit(solution)/shard_map/ppermute | solution.py:507
  159.6 12.4 %collective-permute-done.10.edge_ref = bf16[2,128,128]{2,1,0:T(8,128)(2,1)S(1)} collective-permute-done((bf16[2,128,128]{2,1,0:T(8,128)(2,1)S(1)}, bf16[2,128,128]{2,1,0:T(8,128)(2,1)S(1)}, u32[]{:S(2)}, u32[]{:S(2)}) %collective-permute-start.10) | collective-permute-done | bytes 65568 | tf_op jit(solution)/shard_map/ppermute | solution.py:507
  172.0 38.8 %collective-permute-done.9.crossed = bf16[2,2,128,128]{3,2,1,0:T(8,128)(2,1)S(1)} collective-permute-done((bf16[2,2,128,128]{3,2,1,0:T(8,128)(2,1)S(1)}, bf16[2,2,128,128]{3,2,1,0:T(8,128)(2,1)S(1)}, u32[]{:S(2)}, u32[]{:S(2)}) %collective-permute-start.9) | collective-permute-done | bytes 131104 | tf_op jit(solution)/shard_map/ppermute | solution.py:507
  210.8 6.4 %all-to-all-start.4 = ((bf16[16,2,128,128]{3,2,1,0:T(8,128)(2,1)}), bf16[16,2,128,128]{3,2,1,0:T(8,128)(2,1)S(1)}, u32[]{:S(2)}, u32[]{:S(2)}) async-start(bf16[16,2,128,128]{3,2,1,0:T(8,128)(2,1)} %get-tuple-element.67), calls=%async_computation.4 | async-start | bytes 2097152 | tf_op jit(solution)/shard_map/all_to_all | solution.py:501
  221.4 3.3 %collective-permute-start.14 = (bf16[2,2,128,128]{3,2,1,0:T(8,128)(2,1)}, bf16[2,2,128,128]{3,2,1,0:T(8,128)(2,1)}, u32[]{:S(2)}, u32[]{:S(2)}) collective-permute-start(bf16[2,2,128,128]{3,2,1,0:T(8,128)(2,1)} %get-tuple-element.78), channel_id=1, source_target_pairs={{0,64},{16,80},{32,96},{48,112},{64,0},{80,16},{96,32},{112,48},{1... | collective-permute-start | bytes 393224 | tf_op jit(solution)/shard_map/ppermute | solution.py:507
  226.8 8.4 %collective-permute-done.12.refs_2_ = bf16[2,2,128,128]{3,2,1,0:T(8,128)(2,1)S(1)} collective-permute-done((bf16[2,2,128,128]{3,2,1,0:T(8,128)(2,1)S(1)}, bf16[2,2,128,128]{3,2,1,0:T(8,128)(2,1)S(1)}, u32[]{:S(2)}, u32[]{:S(2)}) %collective-permute-start.12) | collective-permute-done | bytes 131104 | tf_op jit(solution)/shard_map/ppermute | solution.py:507
  236.0 3.9 %land.1 = (f32[16,2,128,128]{3,2,1,0:T(8,128)}, bf16[16,2,128,128]{3,2,1,0:T(8,128)(2,1)}) custom-call(s32[32]{0:T(128)S(1)} %select_n.147.index_ref.main_ref, f32[16,2,128,128]{3,2,1,0:T(8,128)S(1)} %copy-done, bf16[2,128,128]{2,1,0:T(8,128)(2,1)S(1)} %copy-done.2, bf16[32,2,128,128]{3,2,1,0:T(8,128)(2,1)} %all-to-all-done.3.home_ref), custom_call_target="tpu_custom_call" | custom-call | flops 1048576 | bytes 6291456 | tf_op jit(solution)/shard_map/land/pallas_call | solution.py:374
  240.0 3.2 %all-to-all-done.4.in_ref = bf16[16,2,128,128]{3,2,1,0:T(8,128)(2,1)S(1)} async-done(((bf16[16,2,128,128]{3,2,1,0:T(8,128)(2,1)}), bf16[16,2,128,128]{3,2,1,0:T(8,128)(2,1)S(1)}, u32[]{:S(2)}, u32[]{:S(2)}) %all-to-all-start.4) | async-done | bytes 1048608 | tf_op jit(solution)/shard_map/all_to_all | solution.py:501
  243.1 2.8 land_thirds.1
  245.9 5.9 %all-to-all-start.5 = ((bf16[16,2,128,128]{3,2,1,0:T(8,128)(2,1)}), bf16[16,2,128,128]{3,2,1,0:T(8,128)(2,1)S(1)}, u32[]{:S(2)}, u32[]{:S(2)}) async-start(bf16[16,2,128,128]{3,2,1,0:T(8,128)(2,1)} %land_thirds.1), calls=%async_computation.5 | async-start | bytes 2097152 | tf_op jit(solution)/shard_map/all_to_all | solution.py:501
  253.0 25.3 %all-to-all-done.5.in_ref = bf16[16,2,128,128]{3,2,1,0:T(8,128)(2,1)S(1)} async-done(((bf16[16,2,128,128]{3,2,1,0:T(8,128)(2,1)}), bf16[16,2,128,128]{3,2,1,0:T(8,128)(2,1)S(1)}, u32[]{:S(2)}, u32[]{:S(2)}) %all-to-all-start.5) | async-done | bytes 1048608 | tf_op jit(solution)/shard_map/all_to_all | solution.py:501
  (74 shorter events, 26.3 us)
Async XLA Ops:
  3.1 34.2 %all-to-all-start = ((bf16[16,2,128,128]{3,2,1,0:T(8,128)(2,1)}), bf16[16,2,128,128]{3,2,1,0:T(8,128)(2,1)S(1)}, u32[]{:S(2)}, u32[]{:S(2)}) async-start(bf16[16,2,128,128]{3,2,1,0:T(8,128)(2,1)} %split_heads.2), calls=%async_computation | async-start | bytes 2097152 | tf_op jit(solution)/shard_map/all_to_all | solution.py:501
  37.3 32.5 %all-to-all-start.1 = ((bf16[16,2,128,128]{3,2,1,0:T(8,128)(2,1)}), bf16[16,2,128,128]{3,2,1,0:T(8,128)(2,1)}, u32[]{:S(2)}, u32[]{:S(2)}) async-start(bf16[16,2,128,128]{3,2,1,0:T(8,128)(2,1)} %split_heads.3), calls=%async_computation.1 | async-start | bytes 2097152 | tf_op jit(solution)/shard_map/all_to_all | solution.py:501
  44.4 6.3 %collective-permute-start = (bf16[2,2,128,128]{3,2,1,0:T(8,128)(2,1)S(1)}, bf16[2,2,128,128]{3,2,1,0:T(8,128)(2,1)S(1)}, u32[]{:S(2)}, u32[]{:S(2)}) collective-permute-start(bf16[2,2,128,128]{3,2,1,0:T(8,128)(2,1)S(1)} %get-tuple-element.44), channel_id=1, source_target_pairs={{0,16},{16,32},{32,48},{48,64},{64,80},{80,96},{96,112},{112,0},{1... | collective-permute-start | bytes 393224 | tf_op jit(solution)/shard_map/ppermute | solution.py:507
  44.4 6.4 %collective-permute-start.2 = (bf16[2,2,128,128]{3,2,1,0:T(8,128)(2,1)S(1)}, bf16[2,2,128,128]{3,2,1,0:T(8,128)(2,1)S(1)}, u32[]{:S(2)}, u32[]{:S(2)}) collective-permute-start(bf16[2,2,128,128]{3,2,1,0:T(8,128)(2,1)S(1)} %get-tuple-element.49), channel_id=1, source_target_pairs={{0,32},{16,48},{32,64},{48,80},{64,96},{80,112},{96,0},{112,16},{1... | collective-permute-start | bytes 393224 | tf_op jit(solution)/shard_map/ppermute | solution.py:507
  45.1 10.1 %collective-permute-start.3 = (bf16[2,2,128,128]{3,2,1,0:T(8,128)(2,1)S(1)}, bf16[2,2,128,128]{3,2,1,0:T(8,128)(2,1)S(1)}, u32[]{:S(2)}, u32[]{:S(2)}) collective-permute-start(bf16[2,2,128,128]{3,2,1,0:T(8,128)(2,1)S(1)} %get-tuple-element.50), channel_id=1, source_target_pairs={{0,48},{16,64},{32,80},{48,96},{64,112},{80,0},{96,16},{112,32},{1... | collective-permute-start | bytes 393224 | tf_op jit(solution)/shard_map/ppermute | solution.py:507
  47.7 7.8 %collective-permute-start.4 = (bf16[2,2,128,128]{3,2,1,0:T(8,128)(2,1)S(1)}, bf16[2,2,128,128]{3,2,1,0:T(8,128)(2,1)S(1)}, u32[]{:S(2)}, u32[]{:S(2)}) collective-permute-start(bf16[2,2,128,128]{3,2,1,0:T(8,128)(2,1)S(1)} %get-tuple-element.51), channel_id=1, source_target_pairs={{0,64},{16,80},{32,96},{48,112},{64,0},{80,16},{96,32},{112,48},{1... | collective-permute-start | bytes 393224 | tf_op jit(solution)/shard_map/ppermute | solution.py:507
  48.7 9.4 %collective-permute-start.5 = (bf16[2,2,128,128]{3,2,1,0:T(8,128)(2,1)S(1)}, bf16[2,2,128,128]{3,2,1,0:T(8,128)(2,1)S(1)}, u32[]{:S(2)}, u32[]{:S(2)}) collective-permute-start(bf16[2,2,128,128]{3,2,1,0:T(8,128)(2,1)S(1)} %get-tuple-element.52), channel_id=1, source_target_pairs={{0,80},{16,96},{32,112},{48,0},{64,16},{80,32},{96,48},{112,64},{1... | collective-permute-start | bytes 393224 | tf_op jit(solution)/shard_map/ppermute | solution.py:507
  50.7 9.1 %collective-permute-start.6 = (bf16[2,2,128,128]{3,2,1,0:T(8,128)(2,1)S(1)}, bf16[2,2,128,128]{3,2,1,0:T(8,128)(2,1)S(1)}, u32[]{:S(2)}, u32[]{:S(2)}) collective-permute-start(bf16[2,2,128,128]{3,2,1,0:T(8,128)(2,1)S(1)} %get-tuple-element.53), channel_id=1, source_target_pairs={{0,96},{16,112},{32,0},{48,16},{64,32},{80,48},{96,64},{112,80},{1... | collective-permute-start | bytes 393224 | tf_op jit(solution)/shard_map/ppermute | solution.py:507
  50.8 8.9 %collective-permute-start.7 = (bf16[2,2,128,128]{3,2,1,0:T(8,128)(2,1)S(1)}, bf16[2,2,128,128]{3,2,1,0:T(8,128)(2,1)S(1)}, u32[]{:S(2)}, u32[]{:S(2)}) collective-permute-start(bf16[2,2,128,128]{3,2,1,0:T(8,128)(2,1)S(1)} %get-tuple-element.54), channel_id=1, source_target_pairs={{0,112},{16,0},{32,16},{48,32},{64,48},{80,64},{96,80},{112,96},{1... | collective-permute-start | bytes 393224 | tf_op jit(solution)/shard_map/ppermute | solution.py:507
  60.5 9.4 %collective-permute-start.8 = (bf16[2,2,128,128]{3,2,1,0:T(8,128)(2,1)S(1)}, bf16[2,2,128,128]{3,2,1,0:T(8,128)(2,1)S(1)}, u32[]{:S(2)}, u32[]{:S(2)}) collective-permute-start(bf16[2,2,128,128]{3,2,1,0:T(8,128)(2,1)S(1)} %pick_cross.1), channel_id=1, source_target_pairs={{0,128},{16,144},{32,160},{48,176},{64,192},{80,208},{96,224},{112... | collective-permute-start | bytes 393224 | tf_op jit(solution)/shard_map/ppermute | solution.py:507
  65.0 3.7 %collective-permute-start.1 = (bf16[2,128,128]{2,1,0:T(8,128)(2,1)S(1)}, bf16[2,128,128]{2,1,0:T(8,128)(2,1)S(1)}, u32[]{:S(2)}, u32[]{:S(2)}) collective-permute-start(bf16[2,128,128]{2,1,0:T(8,128)(2,1)S(1)} %get-tuple-element.46), channel_id=1, source_target_pairs={{0,16},{16,32},{32,48},{48,64},{64,80},{80,96},{96,112},{112,128},... | collective-permute-start | bytes 196616 | tf_op jit(solution)/shard_map/ppermute | solution.py:507
  69.8 63.8 %all-to-all-start.2 = ((bf16[32,2,128,128]{3,2,1,0:T(8,128)(2,1)}), bf16[32,2,128,128]{3,2,1,0:T(8,128)(2,1)}, u32[]{:S(2)}, u32[]{:S(2)}) async-start(bf16[32,2,128,128]{3,2,1,0:T(8,128)(2,1)} %pack.1), calls=%async_computation.2 | async-start | bytes 4194304 | tf_op jit(solution)/shard_map/all_to_all | solution.py:504
  147.3 63.5 %all-to-all-start.3 = ((bf16[32,2,128,128]{3,2,1,0:T(8,128)(2,1)}), bf16[32,2,128,128]{3,2,1,0:T(8,128)(2,1)}, u32[]{:S(2)}, u32[]{:S(2)}) async-start(bf16[32,2,128,128]{3,2,1,0:T(8,128)(2,1)} %get-tuple-element.60), calls=%async_computation.3 | async-start | bytes 4194304 | tf_op jit(solution)/shard_map/all_to_all | solution.py:504
  153.6 57.2 %collective-permute-start.9 = (bf16[2,2,128,128]{3,2,1,0:T(8,128)(2,1)S(1)}, bf16[2,2,128,128]{3,2,1,0:T(8,128)(2,1)S(1)}, u32[]{:S(2)}, u32[]{:S(2)}) collective-permute-start(bf16[2,2,128,128]{3,2,1,0:T(8,128)(2,1)S(1)} %get-tuple-element.61.own), channel_id=1, source_target_pairs={{0,128},{16,144},{32,160},{48,176},{64,192},{80,208},{96,224},{112... | collective-permute-start | bytes 393224 | tf_op jit(solution)/shard_map/ppermute | solution.py:507
  159.3 12.7 %collective-permute-start.10 = (bf16[2,128,128]{2,1,0:T(8,128)(2,1)S(1)}, bf16[2,128,128]{2,1,0:T(8,128)(2,1)S(1)}, u32[]{:S(2)}, u32[]{:S(2)}) collective-permute-start(bf16[2,128,128]{2,1,0:T(8,128)(2,1)S(1)} %get-tuple-element.62), channel_id=1, source_target_pairs={{0,240},{16,0},{32,16},{48,32},{64,48},{80,64},{96,80},{112,96},{1... | collective-permute-start | bytes 196616 | tf_op jit(solution)/shard_map/ppermute | solution.py:507
  210.8 32.3 %all-to-all-start.4 = ((bf16[16,2,128,128]{3,2,1,0:T(8,128)(2,1)}), bf16[16,2,128,128]{3,2,1,0:T(8,128)(2,1)S(1)}, u32[]{:S(2)}, u32[]{:S(2)}) async-start(bf16[16,2,128,128]{3,2,1,0:T(8,128)(2,1)} %get-tuple-element.67), calls=%async_computation.4 | async-start | bytes 2097152 | tf_op jit(solution)/shard_map/all_to_all | solution.py:501
  218.8 7.9 %collective-permute-start.11 = (bf16[2,2,128,128]{3,2,1,0:T(8,128)(2,1)S(1)}, bf16[2,2,128,128]{3,2,1,0:T(8,128)(2,1)S(1)}, u32[]{:S(2)}, u32[]{:S(2)}) collective-permute-start(bf16[2,2,128,128]{3,2,1,0:T(8,128)(2,1)S(1)} %get-tuple-element.75), channel_id=1, source_target_pairs={{0,112},{16,0},{32,16},{48,32},{64,48},{80,64},{96,80},{112,96},{1... | collective-permute-start | bytes 393224 | tf_op jit(solution)/shard_map/ppermute | solution.py:507
  218.8 16.3 %collective-permute-start.12 = (bf16[2,2,128,128]{3,2,1,0:T(8,128)(2,1)S(1)}, bf16[2,2,128,128]{3,2,1,0:T(8,128)(2,1)S(1)}, u32[]{:S(2)}, u32[]{:S(2)}) collective-permute-start(bf16[2,2,128,128]{3,2,1,0:T(8,128)(2,1)S(1)} %get-tuple-element.76), channel_id=1, source_target_pairs={{0,96},{16,112},{32,0},{48,16},{64,32},{80,48},{96,64},{112,80},{1... | collective-permute-start | bytes 393224 | tf_op jit(solution)/shard_map/ppermute | solution.py:507
  219.9 23.2 %collective-permute-start.13 = (bf16[2,2,128,128]{3,2,1,0:T(8,128)(2,1)}, bf16[2,2,128,128]{3,2,1,0:T(8,128)(2,1)}, u32[]{:S(2)}, u32[]{:S(2)}) collective-permute-start(bf16[2,2,128,128]{3,2,1,0:T(8,128)(2,1)} %get-tuple-element.77), channel_id=1, source_target_pairs={{0,80},{16,96},{32,112},{48,0},{64,16},{80,32},{96,48},{112,64},{1... | collective-permute-start | bytes 393224 | tf_op jit(solution)/shard_map/ppermute | solution.py:507
  221.4 21.7 %collective-permute-start.14 = (bf16[2,2,128,128]{3,2,1,0:T(8,128)(2,1)}, bf16[2,2,128,128]{3,2,1,0:T(8,128)(2,1)}, u32[]{:S(2)}, u32[]{:S(2)}) collective-permute-start(bf16[2,2,128,128]{3,2,1,0:T(8,128)(2,1)} %get-tuple-element.78), channel_id=1, source_target_pairs={{0,64},{16,80},{32,96},{48,112},{64,0},{80,16},{96,32},{112,48},{1... | collective-permute-start | bytes 393224 | tf_op jit(solution)/shard_map/ppermute | solution.py:507
  224.8 18.3 %collective-permute-start.15 = (bf16[2,2,128,128]{3,2,1,0:T(8,128)(2,1)}, bf16[2,2,128,128]{3,2,1,0:T(8,128)(2,1)}, u32[]{:S(2)}, u32[]{:S(2)}) collective-permute-start(bf16[2,2,128,128]{3,2,1,0:T(8,128)(2,1)} %get-tuple-element.79), channel_id=1, source_target_pairs={{0,48},{16,64},{32,80},{48,96},{64,112},{80,0},{96,16},{112,32},{1... | collective-permute-start | bytes 393224 | tf_op jit(solution)/shard_map/ppermute | solution.py:507
  226.7 16.4 %collective-permute-start.16 = (bf16[2,2,128,128]{3,2,1,0:T(8,128)(2,1)}, bf16[2,2,128,128]{3,2,1,0:T(8,128)(2,1)}, u32[]{:S(2)}, u32[]{:S(2)}) collective-permute-start(bf16[2,2,128,128]{3,2,1,0:T(8,128)(2,1)} %get-tuple-element.80), channel_id=1, source_target_pairs={{0,32},{16,48},{32,64},{48,80},{64,96},{80,112},{96,0},{112,16},{1... | collective-permute-start | bytes 393224 | tf_op jit(solution)/shard_map/ppermute | solution.py:507
  235.2 8.0 %collective-permute-start.17 = (bf16[2,2,128,128]{3,2,1,0:T(8,128)(2,1)}, bf16[2,2,128,128]{3,2,1,0:T(8,128)(2,1)}, u32[]{:S(2)}, u32[]{:S(2)}) collective-permute-start(bf16[2,2,128,128]{3,2,1,0:T(8,128)(2,1)} %get-tuple-element.81), channel_id=1, source_target_pairs={{0,16},{16,32},{32,48},{48,64},{64,80},{80,96},{96,112},{112,0},{1... | collective-permute-start | bytes 393224 | tf_op jit(solution)/shard_map/ppermute | solution.py:507
  245.9 32.3 %all-to-all-start.5 = ((bf16[16,2,128,128]{3,2,1,0:T(8,128)(2,1)}), bf16[16,2,128,128]{3,2,1,0:T(8,128)(2,1)S(1)}, u32[]{:S(2)}, u32[]{:S(2)}) async-start(bf16[16,2,128,128]{3,2,1,0:T(8,128)(2,1)} %land_thirds.1), calls=%async_computation.5 | async-start | bytes 2097152 | tf_op jit(solution)/shard_map/all_to_all | solution.py:501
  (4 other events, 132.1 us)
